TPU v7x, 1024 devices: a whole 4x4x32 slice. The times are simulated.
1024 devices in a mesh: group: 32 (over x, y, core), local: 32 (over z).
Axes of the slice: x: 4, y: 4, z: 32, core: 2. Of those that a mesh axis runs over, the one named last changes fastest.
Arguments:
- tokens: bfloat16 [8192, 2048], P(('group', 'local')), may hold values from -6 to 6
- grad_mixed: bfloat16 [8192, 2048], P(('group', 'local')), may hold values from -6 to 6
- gates: bfloat16 [8192, 10], P(('group', 'local')), may hold values from 0.029907227 to 0.3984375
- group_ids: int32 [8192, 4], P(('group', 'local')), may hold values from 0 to 15, as said below
- expert_ids: int32 [8192, 10], P(('group', 'local')), may hold values from 0 to 511, as said below
- w_gate: bfloat16 [32, 32, 2048, 256], P('group', 'local'), may hold values from -0.125 to 0.125
- w_up: bfloat16 [32, 32, 2048, 256], P('group', 'local'), may hold values from -0.125 to 0.125
- w_down: bfloat16 [32, 32, 256, 2048], P('group', 'local'), may hold values from -0.25 to 0.25
Outputs:
- mixed: bfloat16 [8192, 2048], P(('group', 'local'))
- grad_tokens: bfloat16 [8192, 2048], P(('group', 'local'))
- grad_gates: float32 [8192, 10], P(('group', 'local'))
Inputs may be any that keep to these rules, and one draw needn't show every extreme that they name: `group_ids`: each row names 4 different groups; the 8 rows of one device name every group exactly 2 times. `expert_ids`: row t names 10 different experts: three of group group_ids[t,0], three of group_ids[t,1], two of group_ids[t,2] and two of group_ids[t,3], in this order; expert G * 32 + j is number j of group G.
All inputs are finite; a program needn't handle non-finite values.
Results may differ from a plain program's by a relative error of at most 0.007.
Values may be sent and summed in bfloat16 or wider, within the bound.
No kernel may reach another device: no remote copies, remote signals or barrier semaphores. Data moves between devices by JAX's collectives and lax.ppermute only.
A program may use at most 32 MiB of HBM per device.

v0:
```python
import jax
import jax.numpy as jnp
from jax import lax
from jax.sharding import PartitionSpec as P


def expert_half(rows_x, rows_dy, rows_gate, w_in, w_lin, w_out):
    pre_gate = jnp.dot(rows_x, w_in, preferred_element_type=jnp.float32)
    pre_up = jnp.dot(rows_x, w_lin, preferred_element_type=jnp.float32)
    sigmoid = jax.nn.sigmoid(pre_gate)
    active = pre_gate * sigmoid
    hidden = (active * pre_up).astype(jnp.bfloat16)
    partial_out = jnp.dot(hidden, w_out, preferred_element_type=jnp.float32)
    scale = rows_gate.astype(jnp.float32)[:, None]
    weighted = (scale * partial_out).astype(jnp.bfloat16)
    gate_term = jnp.sum(rows_dy.astype(jnp.float32) * partial_out, axis=1).astype(jnp.bfloat16)
    scaled_dy = (scale * rows_dy.astype(jnp.float32)).astype(jnp.bfloat16)
    grad_hidden = lax.dot_general(
        scaled_dy, w_out, (((1,), (1,)), ((), ())), preferred_element_type=jnp.float32
    )
    grad_pre = (grad_hidden * pre_up * sigmoid * (1.0 + pre_gate * (1.0 - sigmoid))).astype(
        jnp.bfloat16
    )
    grad_lin = (grad_hidden * active).astype(jnp.bfloat16)
    back_rows = lax.dot_general(
        grad_pre, w_in, (((1,), (1,)), ((), ())), preferred_element_type=jnp.float32
    )
    back_rows = back_rows + lax.dot_general(
        grad_lin, w_lin, (((1,), (1,)), ((), ())), preferred_element_type=jnp.float32
    )
    return (weighted, back_rows.astype(jnp.bfloat16), gate_term)


def body(tokens, grad_mixed, gates, group_ids, expert_ids, w_gate, w_up, w_down):
    highest = lax.Precision.HIGHEST
    n_group = lax.axis_size("group")
    n_local = lax.axis_size("local")
    groups_all = n_group // 2
    tok_rows = tokens.shape[0]
    width = tokens.shape[1]
    topk_all = expert_ids.shape[1]
    per_group = 4 * tok_rows // groups_all
    capacity = (25 * tok_rows + n_local - 1) // n_local
    my_group = lax.axis_index("group") // 2
    member = jnp.any(
        group_ids[:, :, None] == jnp.arange(groups_all, dtype=jnp.int32)[None, None, :], axis=1
    ).astype(jnp.int32)
    placed = jnp.cumsum(member, axis=0) - member
    chooser = (
        (member.T[:, None, :] == 1)
        & (placed.T[:, None, :] == jnp.arange(per_group, dtype=jnp.int32)[None, :, None])
    ).astype(jnp.float32)
    chooser_bf = chooser.astype(jnp.bfloat16)
    send_x = jnp.einsum(
        "gpt,td->gpd", chooser_bf, tokens, preferred_element_type=jnp.float32
    ).astype(jnp.bfloat16)
    send_dy = jnp.einsum(
        "gpt,td->gpd", chooser_bf, grad_mixed, preferred_element_type=jnp.float32
    ).astype(jnp.bfloat16)
    send_gate = jnp.einsum(
        "gpt,tk->gpk", chooser_bf, gates, preferred_element_type=jnp.float32
    ).astype(jnp.bfloat16)
    send_ids = jnp.einsum(
        "gpt,tk->gpk", chooser, expert_ids.astype(jnp.float32), precision=highest
    ).astype(jnp.int32)

    def shape_out(array):
        doubled = jnp.broadcast_to(array[:, None], (groups_all, 2) + array.shape[1:])
        return doubled.reshape((n_group,) + array.shape[1:])

    out_x = shape_out(send_x)
    out_dy = shape_out(send_dy)
    out_gate = shape_out(send_gate)
    out_ids = shape_out(send_ids)
    got_x, got_dy, got_gate, got_ids = (
        lax.all_to_all(out_x, "group", split_axis=0, concat_axis=0, tiled=True),
        lax.all_to_all(out_dy, "group", split_axis=0, concat_axis=0, tiled=True),
        lax.all_to_all(out_gate, "group", split_axis=0, concat_axis=0, tiled=True),
        lax.all_to_all(out_ids, "group", split_axis=0, concat_axis=0, tiled=True),
    )
    row_count = n_group * per_group
    row_x = got_x.reshape(row_count, width)
    row_dy = got_dy.reshape(row_count, width)
    row_gate = got_gate.reshape(row_count, topk_all)
    row_ids = got_ids.reshape(row_count, topk_all)
    in_group = row_ids // n_local == my_group
    position = row_ids % n_local
    picked = (
        in_group[:, :, None]
        & (position[:, :, None] == jnp.arange(n_local, dtype=jnp.int32)[None, None, :])
    ).astype(jnp.float32)
    counted = jnp.sum(picked, axis=1)
    counted_int = counted.astype(jnp.int32)
    ranked = jnp.cumsum(counted_int, axis=0) - counted_int
    kept_rows = counted * (ranked < capacity).astype(jnp.float32)
    dispatch = kept_rows.T[:, None, :] * (
        ranked.T[:, None, :] == jnp.arange(capacity, dtype=jnp.int32)[None, :, None]
    ).astype(jnp.float32)
    dispatch_bf = dispatch.astype(jnp.bfloat16)
    gate_at = jnp.einsum("rkj,rk->rj", picked, row_gate.astype(jnp.float32), precision=highest)
    slot_x = jnp.einsum(
        "jcr,rd->jcd", dispatch_bf, row_x, preferred_element_type=jnp.float32
    ).astype(jnp.bfloat16)
    slot_dy = jnp.einsum(
        "jcr,rd->jcd", dispatch_bf, row_dy, preferred_element_type=jnp.float32
    ).astype(jnp.bfloat16)
    slot_gate = jnp.einsum("jcr,rj->jc", dispatch, gate_at, precision=highest).astype(jnp.bfloat16)
    recv_x, recv_dy, recv_gate = (
        lax.all_to_all(slot_x, "local", split_axis=0, concat_axis=0, tiled=True),
        lax.all_to_all(slot_dy, "local", split_axis=0, concat_axis=0, tiled=True),
        lax.all_to_all(slot_gate, "local", split_axis=0, concat_axis=0, tiled=True),
    )
    slots_all = n_local * capacity
    weighted, back_rows, gate_term = expert_half(
        recv_x.reshape(slots_all, width),
        recv_dy.reshape(slots_all, width),
        recv_gate.reshape(slots_all),
        w_gate[0, 0],
        w_up[0, 0],
        w_down[0, 0],
    )
    ret_out, ret_back, ret_term = (
        lax.all_to_all(
            weighted.reshape(n_local, capacity, width),
            "local",
            split_axis=0,
            concat_axis=0,
            tiled=True,
        ),
        lax.all_to_all(
            back_rows.reshape(n_local, capacity, width),
            "local",
            split_axis=0,
            concat_axis=0,
            tiled=True,
        ),
        lax.all_to_all(
            gate_term.reshape(n_local, capacity), "local", split_axis=0, concat_axis=0, tiled=True
        ),
    )
    sum_out = jnp.einsum("jcr,jcd->rd", dispatch_bf, ret_out, preferred_element_type=jnp.float32)
    sum_back = jnp.einsum("jcr,jcd->rd", dispatch_bf, ret_back, preferred_element_type=jnp.float32)
    term_each = jnp.einsum("jcr,jc->rj", dispatch, ret_term.astype(jnp.float32), precision=highest)
    sum_term = jnp.einsum("rkj,rj->rk", picked, term_each, precision=highest)
    sum_out = sum_out.reshape(n_group, per_group, width)
    sum_back = sum_back.reshape(n_group, per_group, width)
    sum_term = sum_term.reshape(n_group, per_group, topk_all)
    back_out, back_grad, back_term = (
        lax.all_to_all(sum_out, "group", split_axis=0, concat_axis=0, tiled=True),
        lax.all_to_all(sum_back, "group", split_axis=0, concat_axis=0, tiled=True),
        lax.all_to_all(sum_term, "group", split_axis=0, concat_axis=0, tiled=True),
    )
    back_out = jnp.sum(back_out.reshape(groups_all, 2, per_group, width), axis=1)
    back_grad = jnp.sum(back_grad.reshape(groups_all, 2, per_group, width), axis=1)
    back_term = jnp.sum(back_term.reshape(groups_all, 2, per_group, topk_all), axis=1)
    mixed = jnp.einsum("gpt,gpd->td", chooser, back_out, precision=highest).astype(jnp.bfloat16)
    grad_tokens = jnp.einsum("gpt,gpd->td", chooser, back_grad, precision=highest).astype(
        jnp.bfloat16
    )
    grad_gates = jnp.einsum("gpt,gpk->tk", chooser, back_term, precision=highest)
    return (mixed, grad_tokens, grad_gates)


def solution(mesh):
    return jax.shard_map(
        body,
        mesh=mesh,
        in_specs=(
            P(("group", "local"), None),
            P(("group", "local"), None),
            P(("group", "local"), None),
            P(("group", "local"), None),
            P(("group", "local"), None),
            P("group", "local", None, None),
            P("group", "local", None, None),
            P("group", "local", None, None),
        ),
        out_specs=(
            P(("group", "local"), None),
            P(("group", "local"), None),
            P(("group", "local"), None),
        ),
        check_vma=False,
    )
```

profile of v0, /device:TPU:1, one launch (start us, length us, event | category | flops | bytes accessed | tf_op | source)
XLA Modules:
  0.0 634.3 jit_solution(2007572403362808394)
XLA Ops:
  0.7 0.9 fusion.49
  1.5 0.9 convolution_convert_fusion.4
  3.1 17.7 %all-to-all-start = ((s32[32,2,10]{2,1,0:T(2,128)}), s32[32,2,10]{2,1,0:T(2,128)S(1)}, u32[]{:S(2)}, u32[]{:S(2)}) async-start(s32[32,2,10]{2,1,0:T(2,128)} %bitcast.6), calls=%async_computation | async-start | bytes 65536 | tf_op jit(solution)/shard_map/all_to_all | solution.py:79
  20.8 1.0 convolution_convert_fusion.3
  21.7 0.9 convolution_convert_fusion.5
  22.8 5.4 all-to-all-done
  28.8 3.9 all-to-all-start.1
  33.6 6.0 all-to-all-done.1
  39.6 0.8 broadcast_in_dim.10
  40.5 4.2 all-to-all-start.3
  45.8 8.0 %all-to-all-done.3 = bf16[32,2,2048]{2,1,0:T(2,128)(2,1)S(1)} async-done(((bf16[32,2,2048]{2,1,0:T(2,128)(2,1)}), bf16[32,2,2048]{2,1,0:T(2,128)(2,1)S(1)}, u32[]{:S(2)}, u32[]{:S(2)}) %all-to-all-start.3) | async-done | bytes 262176 | tf_op jit(solution)/shard_map/all_to_all | solution.py:76
  53.8 19.3 %all-to-all-start.2 = ((bf16[32,1,7]{2,1,0:T(2,128)(2,1)}), bf16[32,1,7]{2,1,0:T(2,128)(2,1)S(1)}, u32[]{:S(2)}, u32[]{:S(2)}) async-start(bf16[32,1,7]{2,1,0:T(2,128)(2,1)} %copy.137), calls=%async_computation.2 | async-start | bytes 32768 | tf_op jit(solution)/shard_map/all_to_all | solution.py:111
  73.5 20.7 %all-to-all-done.2 = bf16[32,1,7]{2,1,0:T(2,128)(2,1)S(1)} async-done(((bf16[32,1,7]{2,1,0:T(2,128)(2,1)}), bf16[32,1,7]{2,1,0:T(2,128)(2,1)S(1)}, u32[]{:S(2)}, u32[]{:S(2)}) %all-to-all-start.2) | async-done | bytes 480 | tf_op jit(solution)/shard_map/all_to_all | solution.py:111
  94.2 0.8 broadcast_in_dim.11
  95.1 5.2 all-to-all-start.7
  100.6 1.5 copy.139
  102.1 7.2 %all-to-all-done.7 = bf16[32,2,2048]{2,1,0:T(2,128)(2,1)S(1)} async-done(((bf16[32,2,2048]{2,1,0:T(2,128)(2,1)}), bf16[32,2,2048]{2,1,0:T(2,128)(2,1)S(1)}, u32[]{:S(2)}, u32[]{:S(2)}) %all-to-all-start.7) | async-done | bytes 262176 | tf_op jit(solution)/shard_map/all_to_all | solution.py:77
  109.3 3.9 all-to-all-start.4
  113.8 1.5 copy.143
  115.2 103.2 %all-to-all-done.4 = bf16[32,7,2048]{2,1,0:T(8,128)(2,1)S(1)} async-done(((bf16[32,7,2048]{2,1,0:T(8,128)(2,1)}), bf16[32,7,2048]{2,1,0:T(8,128)(2,1)S(1)}, u32[]{:S(2)}, u32[]{:S(2)}) %all-to-all-start.4) | async-done | bytes 917536 | tf_op jit(solution)/shard_map/all_to_all | solution.py:109
  218.4 1.0 copy-done.2
  219.5 7.5 %all-to-all-start.8 = ((bf16[32,7,2048]{2,1,0:T(8,128)(2,1)}), bf16[32,7,2048]{2,1,0:T(8,128)(2,1)S(1)}, u32[]{:S(2)}, u32[]{:S(2)}) async-start(bf16[32,7,2048]{2,1,0:T(8,128)(2,1)} %copy.143), calls=%async_computation.8 | async-start | bytes 2097152 | tf_op jit(solution)/shard_map/all_to_all | solution.py:110
  227.1 1.5 reshape.161
  228.6 1.7 fusion.12
  230.8 101.5 %all-to-all-done.8 = bf16[32,7,2048]{2,1,0:T(8,128)(2,1)S(1)} async-done(((bf16[32,7,2048]{2,1,0:T(8,128)(2,1)}), bf16[32,7,2048]{2,1,0:T(8,128)(2,1)S(1)}, u32[]{:S(2)}, u32[]{:S(2)}) %all-to-all-start.8) | async-done | bytes 917536 | tf_op jit(solution)/shard_map/all_to_all | solution.py:110
  332.3 1.5 reshape.174
  333.8 2.1 multiply_reduce_fusion
  336.6 7.1 %all-to-all-start.11 = ((bf16[32,1,7]{2,1,0:T(2,128)(2,1)}), bf16[32,1,7]{2,1,0:T(2,128)(2,1)S(1)}, u32[]{:S(2)}, u32[]{:S(2)}) async-start(bf16[32,1,7]{2,1,0:T(2,128)(2,1)} %convert_element_type.156), calls=%async_computation.11 | async-start | bytes 32768 | tf_op jit(solution)/shard_map/all_to_all | solution.py:137
  343.7 21.2 %all-to-all-done.11 = bf16[32,1,7]{2,1,0:T(2,128)(2,1)S(1)} async-done(((bf16[32,1,7]{2,1,0:T(2,128)(2,1)}), bf16[32,1,7]{2,1,0:T(2,128)(2,1)S(1)}, u32[]{:S(2)}, u32[]{:S(2)}) %all-to-all-start.11) | async-done | bytes 480 | tf_op jit(solution)/shard_map/all_to_all | solution.py:137
  366.2 5.6 all-to-all-start.12
  371.8 1.3 reshape.162
  373.1 6.1 all-to-all-done.12
  379.2 4.8 all-to-all-start.5
  384.3 1.2 convert_element_type.144
  385.5 1.7 fusion.3
  389.0 1.3 reshape.167
  390.3 98.8 %all-to-all-done.5 = bf16[32,7,2048]{2,1,0:T(8,128)(2,1)} async-done(((bf16[32,7,2048]{2,1,0:T(8,128)(2,1)}), bf16[32,7,2048]{2,1,0:T(8,128)(2,1)}, u32[]{:S(2)}, u32[]{:S(2)}) %all-to-all-start.5) | async-done | bytes 917536 | tf_op jit(solution)/shard_map/all_to_all | solution.py:123
  489.1 7.3 %all-to-all-start.9 = ((bf16[32,7,2048]{2,1,0:T(8,128)(2,1)}), bf16[32,7,2048]{2,1,0:T(8,128)(2,1)S(1)}, u32[]{:S(2)}, u32[]{:S(2)}) async-start(bf16[32,7,2048]{2,1,0:T(8,128)(2,1)} %reshape.167), calls=%async_computation.9 | async-start | bytes 2097152 | tf_op jit(solution)/shard_map/all_to_all | solution.py:130
  496.4 1.9 convolution_bitcast_fusion.1
  498.3 1.1 reshape.163
  499.4 102.5 %all-to-all-done.9 = bf16[32,7,2048]{2,1,0:T(8,128)(2,1)S(1)} async-done(((bf16[32,7,2048]{2,1,0:T(8,128)(2,1)}), bf16[32,7,2048]{2,1,0:T(8,128)(2,1)S(1)}, u32[]{:S(2)}, u32[]{:S(2)}) %all-to-all-start.9) | async-done | bytes 917536 | tf_op jit(solution)/shard_map/all_to_all | solution.py:130
  601.9 4.2 all-to-all-start.6
  606.9 1.1 reshape.168
  608.0 9.9 %all-to-all-done.6 = f32[32,2,2048]{2,1,0:T(2,128)S(1)} async-done(((f32[32,2,2048]{2,1,0:T(2,128)}), f32[32,2,2048]{2,1,0:T(2,128)S(1)}, u32[]{:S(2)}, u32[]{:S(2)}) %all-to-all-start.6) | async-done | bytes 524320 | tf_op jit(solution)/shard_map/all_to_all | solution.py:149
  617.9 3.7 all-to-all-start.10
  622.6 1.0 fusion.1
  623.6 9.5 %all-to-all-done.10 = f32[32,2,2048]{2,1,0:T(2,128)S(1)} async-done(((f32[32,2,2048]{2,1,0:T(2,128)}), f32[32,2,2048]{2,1,0:T(2,128)S(1)}, u32[]{:S(2)}, u32[]{:S(2)}) %all-to-all-start.10) | async-done | bytes 524320 | tf_op jit(solution)/shard_map/all_to_all | solution.py:150
  633.3 1.0 fusion.2
  (65 shorter events, 11.4 us)
Async XLA Ops:
  0.6 333.2 %copy-start = (bf16[1,1,256,2048]{3,2,1,0:T(8,128)(2,1)S(1)}, bf16[1,1,256,2048]{3,2,1,0:T(8,128)(2,1)}, u32[]{:S(2)}) copy-start(bf16[1,1,256,2048]{3,2,1,0:T(8,128)(2,1)} %param.15) | copy-start | bytes 3145732
  0.6 72.4 %copy-start.7 = (bf16[8,2048]{1,0:T(8,128)(2,1)S(1)}, bf16[8,2048]{1,0:T(8,128)(2,1)}, u32[]{:S(2)}) copy-start(bf16[8,2048]{1,0:T(8,128)(2,1)} %param.9) | copy-start | bytes 98308
  3.1 25.1 %all-to-all-start = ((s32[32,2,10]{2,1,0:T(2,128)}), s32[32,2,10]{2,1,0:T(2,128)S(1)}, u32[]{:S(2)}, u32[]{:S(2)}) async-start(s32[32,2,10]{2,1,0:T(2,128)} %bitcast.6), calls=%async_computation | async-start | bytes 65536 | tf_op jit(solution)/shard_map/all_to_all | solution.py:79
  28.8 10.9 %all-to-all-start.1 = ((bf16[32,2,10]{2,1,0:T(2,128)(2,1)}), bf16[32,2,10]{2,1,0:T(2,128)(2,1)S(1)}, u32[]{:S(2)}, u32[]{:S(2)}) async-start(bf16[32,2,10]{2,1,0:T(2,128)(2,1)} %bitcast.11), calls=%async_computation.1 | async-start | bytes 32768 | tf_op jit(solution)/shard_map/all_to_all | solution.py:78
  40.5 13.3 %all-to-all-start.3 = ((bf16[32,2,2048]{2,1,0:T(2,128)(2,1)}), bf16[32,2,2048]{2,1,0:T(2,128)(2,1)S(1)}, u32[]{:S(2)}, u32[]{:S(2)}) async-start(bf16[32,2,2048]{2,1,0:T(2,128)(2,1)} %bitcast.19), calls=%async_computation.3 | async-start | bytes 524288 | tf_op jit(solution)/shard_map/all_to_all | solution.py:76
  53.8 40.5 %all-to-all-start.2 = ((bf16[32,1,7]{2,1,0:T(2,128)(2,1)}), bf16[32,1,7]{2,1,0:T(2,128)(2,1)S(1)}, u32[]{:S(2)}, u32[]{:S(2)}) async-start(bf16[32,1,7]{2,1,0:T(2,128)(2,1)} %copy.137), calls=%async_computation.2 | async-start | bytes 32768 | tf_op jit(solution)/shard_map/all_to_all | solution.py:111
  95.1 14.3 %all-to-all-start.7 = ((bf16[32,2,2048]{2,1,0:T(2,128)(2,1)}), bf16[32,2,2048]{2,1,0:T(2,128)(2,1)S(1)}, u32[]{:S(2)}, u32[]{:S(2)}) async-start(bf16[32,2,2048]{2,1,0:T(2,128)(2,1)} %bitcast.28), calls=%async_computation.7 | async-start | bytes 524288 | tf_op jit(solution)/shard_map/all_to_all | solution.py:77
  109.3 109.1 %all-to-all-start.4 = ((bf16[32,7,2048]{2,1,0:T(8,128)(2,1)}), bf16[32,7,2048]{2,1,0:T(8,128)(2,1)S(1)}, u32[]{:S(2)}, u32[]{:S(2)}) async-start(bf16[32,7,2048]{2,1,0:T(8,128)(2,1)} %copy.139), calls=%async_computation.4 | async-start | bytes 2097152 | tf_op jit(solution)/shard_map/all_to_all | solution.py:109
  218.4 1.0 copy-start.2
  219.5 112.9 %all-to-all-start.8 = ((bf16[32,7,2048]{2,1,0:T(8,128)(2,1)}), bf16[32,7,2048]{2,1,0:T(8,128)(2,1)S(1)}, u32[]{:S(2)}, u32[]{:S(2)}) async-start(bf16[32,7,2048]{2,1,0:T(8,128)(2,1)} %copy.143), calls=%async_computation.8 | async-start | bytes 2097152 | tf_op jit(solution)/shard_map/all_to_all | solution.py:110
  228.6 1.7 copy-start.3
  230.8 105.1 %copy-start.5 = (f32[224,256]{1,0:T(8,128)}, f32[224,256]{1,0:T(8,128)S(1)}, u32[]{:S(2)}) copy-start(f32[224,256]{1,0:T(8,128)S(1)} %fusion.8) | copy-start | bytes 688132
  336.6 28.3 %all-to-all-start.11 = ((bf16[32,1,7]{2,1,0:T(2,128)(2,1)}), bf16[32,1,7]{2,1,0:T(2,128)(2,1)S(1)}, u32[]{:S(2)}, u32[]{:S(2)}) async-start(bf16[32,1,7]{2,1,0:T(2,128)(2,1)} %convert_element_type.156), calls=%async_computation.11 | async-start | bytes 32768 | tf_op jit(solution)/shard_map/all_to_all | solution.py:137
  366.2 13.0 %all-to-all-start.12 = ((f32[32,2,10]{2,1,0:T(2,128)}), f32[32,2,10]{2,1,0:T(2,128)S(1)}, u32[]{:S(2)}, u32[]{:S(2)}) async-start(f32[32,2,10]{2,1,0:T(2,128)} %bitcast.37), calls=%async_computation.12 | async-start | bytes 65536 | tf_op jit(solution)/shard_map/all_to_all | solution.py:151
  379.2 109.9 %all-to-all-start.5 = ((bf16[32,7,2048]{2,1,0:T(8,128)(2,1)}), bf16[32,7,2048]{2,1,0:T(8,128)(2,1)}, u32[]{:S(2)}, u32[]{:S(2)}) async-start(bf16[32,7,2048]{2,1,0:T(8,128)(2,1)} %reshape.162), calls=%async_computation.5 | async-start | bytes 2097152 | tf_op jit(solution)/shard_map/all_to_all | solution.py:123
  384.3 3.0 copy-start.1
  385.5 1.7 copy-start.6
  387.3 1.2 copy-start.4
  489.1 112.8 %all-to-all-start.9 = ((bf16[32,7,2048]{2,1,0:T(8,128)(2,1)}), bf16[32,7,2048]{2,1,0:T(8,128)(2,1)S(1)}, u32[]{:S(2)}, u32[]{:S(2)}) async-start(bf16[32,7,2048]{2,1,0:T(8,128)(2,1)} %reshape.167), calls=%async_computation.9 | async-start | bytes 2097152 | tf_op jit(solution)/shard_map/all_to_all | solution.py:130
  601.9 16.0 %all-to-all-start.6 = ((f32[32,2,2048]{2,1,0:T(2,128)}), f32[32,2,2048]{2,1,0:T(2,128)S(1)}, u32[]{:S(2)}, u32[]{:S(2)}) async-start(f32[32,2,2048]{2,1,0:T(2,128)} %reshape.163), calls=%async_computation.6 | async-start | bytes 1048576 | tf_op jit(solution)/shard_map/all_to_all | solution.py:149
  617.9 15.2 %all-to-all-start.10 = ((f32[32,2,2048]{2,1,0:T(2,128)}), f32[32,2,2048]{2,1,0:T(2,128)S(1)}, u32[]{:S(2)}, u32[]{:S(2)}) async-start(f32[32,2,2048]{2,1,0:T(2,128)} %reshape.168), calls=%async_computation.10 | async-start | bytes 1048576 | tf_op jit(solution)/shard_map/all_to_all | solution.py:150
where the time goes:
time: 636 us; the launch traced here: 634 us
  waiting for transfers between devices  500 us (79%)
  starting transfers between devices  94.3 us (15%)
  local copies, waits for them, and re-layouts  20.4 us (3%)
  matrix products  16.6 us (3%)
    all_to_all x1, waiting for transfers between devices, body(): lax.all_to_all(slot_x, 'local', split_axis=0, concat_axis=0, tiled=True)  103 us
    all_to_all x1, waiting for transfers between devices, body(): lax.all_to_all(back_rows.reshape(n_local, capacity, width), 'local', spli...  102 us
    all_to_all x1, waiting for transfers between devices, body(): lax.all_to_all(slot_dy, 'local', split_axis=0, concat_axis=0, tiled=True)  102 us
    all_to_all x1, waiting for transfers between devices, body(): lax.all_to_all(weighted.reshape(n_local, capacity, width), 'local', split...  98.8 us
    all_to_all x1, waiting for transfers between devices, body(): lax.all_to_all(gate_term.reshape(n_local, capacity), 'local', split_axis=...  21.2 us
    all_to_all x1, waiting for transfers between devices, body(): lax.all_to_all(slot_gate, 'local', split_axis=0, concat_axis=0, tiled=True)  20.7 us
    all_to_all x1, starting transfers between devices, body(): lax.all_to_all(slot_gate, 'local', split_axis=0, concat_axis=0, tiled=True)  19.3 us
    all_to_all x1, starting transfers between devices, body(): lax.all_to_all(out_ids, 'group', split_axis=0, concat_axis=0, tiled=True)  17.7 us
  transfers between devices with their start and end apart: 13, of which 13 were waited for; matrix products, arithmetic and copies ran while one was open for 4% of the time, Pallas kernels for 0%

commit v1 on v0

v1 whole, which is shorter than its diff:
```python
import jax
import jax.numpy as jnp
from jax import lax
from jax.sharding import PartitionSpec as P

BF = jnp.bfloat16
F32 = jnp.float32
META = 128


def dot(a, b, dims):
    return lax.dot_general(a, b, (dims, ((), ())), preferred_element_type=F32)


def body(tokens, grad_mixed, gates, group_ids, expert_ids, w_gate, w_up, w_down):
    n_group = lax.axis_size("group")
    n_local = lax.axis_size("local")
    near = 8 if n_local % 8 == 0 and n_local > 8 else n_local // 2
    far = n_local // near
    groups = n_group // 2
    tok = tokens.shape[0]
    width = tokens.shape[1]
    half = width // 2
    topk = expert_ids.shape[1]
    named = group_ids.shape[1]
    per_group = named * tok // groups
    capacity = (25 * tok + n_local - 1) // n_local
    pad = (capacity // 8 + 1) * 8
    me = lax.axis_index("group")
    my_group = (me // 2).astype(BF)
    core = me % 2
    z = lax.axis_index("local")

    def shift(array, by):
        return lax.ppermute(array, "local", [(i, (i + by) % n_local) for i in range(n_local)])

    def swap(array):
        return lax.ppermute(array, "group", [(i, i ^ 1) for i in range(n_group)])

    meta = jnp.concatenate(
        [(expert_ids // n_local).astype(BF), (expert_ids % n_local).astype(BF), gates, group_ids.astype(BF)], axis=1
    )
    meta = jnp.pad(meta, ((0, 0), (0, META - meta.shape[1])))
    own = jnp.concatenate([tokens, grad_mixed, meta], axis=1)
    rows = jnp.concatenate([own] + [shift(own, near * f) for f in range(1, far)], axis=0)

    names = rows[:, 2 * width + 3 * topk : 2 * width + 3 * topk + named].reshape(far, tok, named)
    member = jnp.any(names[..., None] == jnp.arange(groups, dtype=F32).astype(BF), axis=2).astype(jnp.int32)
    placed = jnp.cumsum(member, axis=1) - member
    chooser = (
        (member.transpose(2, 0, 1)[:, :, None, :] == 1)
        & (placed.transpose(2, 0, 1)[:, :, None, :] == jnp.arange(per_group, dtype=jnp.int32)[None, None, :, None])
    ).astype(BF)
    chooser = chooser[:, :, :, None, :] * jnp.eye(far, dtype=BF)[None, :, None, :, None]
    chooser = chooser.reshape(groups * far * per_group, far * tok)
    parts = []
    for c in range(2):
        piece = jnp.concatenate(
            [rows[:, c * half : (c + 1) * half], rows[:, width + c * half : width + (c + 1) * half], rows[:, 2 * width :]],
            axis=1,
        )
        parts.append(dot(chooser, piece, ((1,), (0,))).astype(BF).reshape(groups, 1, far * per_group, width + META))
    send = jnp.concatenate(parts, axis=1).reshape(n_group, far * per_group, width + META)
    got = lax.all_to_all(send, "group", split_axis=0, concat_axis=0, tiled=True)
    n_rows = n_group * far * per_group
    got = got.reshape(n_rows, width + META)

    shifts = [s - (near // 2 - 1) for s in range(near)]
    info = got[:, width:].T
    row_group, row_pos, row_gate = info[:topk], info[topk : 2 * topk], info[2 * topk : 3 * topk]
    target = ((z + jnp.arange(near, dtype=jnp.int32) - (near // 2 - 1)) % n_local).astype(BF)
    picked = (row_group == my_group)[:, None, :] & (row_pos[:, None, :] == target[None, :, None])
    counted = jnp.any(picked, axis=0)
    gate_at = jnp.sum(jnp.where(picked, row_gate.astype(F32)[:, None, :], 0.0), axis=0)
    index = jnp.arange(n_rows, dtype=jnp.int32)
    plane_of = (index // per_group) % far
    ahead = ((index[:, None] < index[None, :]) & (plane_of[:, None] == plane_of[None, :])).astype(BF)
    ranked = dot(counted.astype(BF), ahead, ((1,), (0,))).astype(jnp.int32)
    kept = counted & (ranked < capacity)
    slot = jnp.where(kept, ranked, -1)
    hit = (slot[:, None, None, :] == jnp.arange(pad, dtype=jnp.int32)[None, None, :, None]) & (
        plane_of[None, None, None, :] == jnp.arange(far, dtype=jnp.int32)[None, :, None, None]
    )
    n_slots = near * far * pad
    plain = hit.astype(BF).reshape(n_slots, n_rows)
    scaled = jnp.where(hit, gate_at[:, None, None, :], 0.0).astype(BF).reshape(n_slots, n_rows)
    slot_x = dot(plain, got[:, :half], ((1,), (0,))).astype(BF)
    slot_dy = dot(scaled, got[:, half:width], ((1,), (0,))).astype(BF)
    slots = jnp.concatenate([slot_x, slot_dy], axis=1).reshape(near, far * pad, width)
    mine = jnp.concatenate(
        [slots[i] if s == 0 else shift(slots[i], s) for i, s in enumerate(shifts)], axis=0
    )

    other = swap(mine)
    first = jnp.where(core == 0, mine, other)
    second = jnp.where(core == 0, other, mine)
    x = jnp.concatenate([first[:, :half], second[:, :half]], axis=1)
    dy = jnp.concatenate([first[:, half:], second[:, half:]], axis=1)

    w_in, w_lin, w_out = w_gate[0, 0], w_up[0, 0], w_down[0, 0]
    pre_gate = dot(x, w_in, ((1,), (0,)))
    pre_up = dot(x, w_lin, ((1,), (0,)))
    sigmoid = jax.nn.sigmoid(pre_gate)
    active = pre_gate * sigmoid
    hidden = (active * pre_up).astype(BF)
    out = dot(hidden, w_out, ((1,), (0,)))
    grad_hidden = dot(dy, w_out, ((1,), (1,)))
    grad_pre = (grad_hidden * pre_up * sigmoid * (1.0 + pre_gate * (1.0 - sigmoid))).astype(BF)
    grad_lin = (grad_hidden * active).astype(BF)
    back = dot(grad_pre, w_in, ((1,), (1,))) + dot(grad_lin, w_lin, ((1,), (1,)))

    keep_out = jnp.where(core == 0, out[:, :half], out[:, half:])
    keep_back = jnp.where(core == 0, back[:, :half], back[:, half:])
    give_out = jnp.where(core == 0, out[:, half:], out[:, :half])
    give_back = jnp.where(core == 0, back[:, half:], back[:, :half])
    gave = swap(jnp.concatenate([give_out.astype(BF), give_back.astype(BF)], axis=1))
    sum_out = keep_out + gave[:, :half].astype(F32)
    sum_back = keep_back + gave[:, half:].astype(F32)
    term = jnp.sum(mine[:, half:].astype(F32) * sum_out, axis=1)
    lane = jnp.arange(half, dtype=jnp.int32)
    place = jnp.arange(pad, dtype=jnp.int32)
    spare = jnp.sum(
        jnp.where(lane[None, None, :] == place[None, :, None], term.reshape(near * far, pad, 1), 0.0), axis=1, keepdims=True
    )
    sum_out = jnp.where(
        (place == pad - 1)[None, :, None], spare, sum_out.reshape(near * far, pad, half)
    ).reshape(n_slots, half)
    ret = jnp.concatenate([sum_out.astype(BF), sum_back.astype(BF)], axis=1).reshape(near, far * pad, width)
    ret = jnp.concatenate(
        [ret[i] if s == 0 else shift(ret[i], -s) for i, s in enumerate(shifts)], axis=0
    )

    row_out = dot(scaled, ret[:, :half], ((0,), (0,)))
    row_back = dot(plain, ret[:, half:], ((0,), (0,)))
    terms = ret.reshape(near, far, pad, width)[:, :, pad - 1, :pad].astype(F32)
    term_at = jnp.sum(jnp.where(hit, terms[:, :, :, None], 0.0), axis=(1, 2))
    term_k = jnp.sum(jnp.where(picked, term_at[None], 0.0), axis=1) / row_gate.astype(F32)
    term_k = jnp.pad(term_k, ((0, META - topk), (0, 0))).T
    send = jnp.concatenate([row_out.astype(BF), row_back.astype(BF), term_k.astype(BF)], axis=1)
    send = send.reshape(n_group, far * per_group, width + META)
    got = lax.all_to_all(send, "group", split_axis=0, concat_axis=0, tiled=True)

    got = got.reshape(groups, 2, far * per_group, width + META)
    sums = [
        dot(chooser, got[:, c].reshape(groups * far * per_group, width + META), ((0,), (0,))) for c in range(2)
    ]
    full = jnp.concatenate(
        [sums[0][:, :half], sums[1][:, :half], sums[0][:, half:width], sums[1][:, half:width], sums[0][:, width:] + sums[1][:, width:]],
        axis=1,
    ).reshape(far, tok, 2 * width + META)
    total = full[0]
    for f in range(1, far):
        total = total + shift(full[f].astype(BF), -near * f).astype(F32)
    return (
        total[:, :width].astype(BF),
        total[:, width : 2 * width].astype(BF),
        total[:, 2 * width : 2 * width + topk],
    )


def solution(mesh):
    rows = P(("group", "local"), None)
    weights = P("group", "local", None, None)
    return jax.shard_map(
        body,
        mesh=mesh,
        in_specs=(rows, rows, rows, rows, rows, weights, weights, weights),
        out_specs=(rows, rows, rows),
        check_vma=False,
    )
```

time: 636 us -> 281 us (0.44)
  waiting for transfers between devices: 500 us -> 86.1 us
  starting transfers between devices: 94.3 us -> 146 us
  blocking collectives: 0 us -> 22.3 us
  local copies, waits for them, and re-layouts: 20.4 us -> 4.3 us
  matrix products: 16.6 us -> 6.19 us
  other arithmetic: 2.08 us -> 12.1 us
    all_to_all x13 -> x1, waiting for transfers between devices: 500 us -> 17.6 us  [body(): got = lax.all_to_all(send, 'group', split_axis=0, concat_axis=0, tiled=True)]
    ppermute x0 -> x22, starting transfers between devices: none -> 139 us  [the longest x20 131 us: shift(): lax.ppermute(array, 'local', [(i, (i + by) % n_local) for i in range(n_lo...]
    all_to_all x13 -> x1, starting transfers between devices: 94.3 us -> 7.63 us  [body(): got = lax.all_to_all(send, 'group', split_axis=0, concat_axis=0, tiled=True)]
    ppermute x0 -> x22, waiting for transfers between devices: none -> 68.5 us  [the longest x20 63.8 us: shift(): lax.ppermute(array, 'local', [(i, (i + by) % n_local) for i in range(n_lo...]
    all_to_all x0 -> x1, blocking collectives: none -> 22.3 us  [body(): got = lax.all_to_all(send, 'group', split_axis=0, concat_axis=0, tiled=True)]
    dot_general x19 -> x15, matrix products: 16.6 us -> 6.19 us  [dot(): return lax.dot_general(a, b, (dims, ((), ())), preferred_element_type=F32)]
    convert_element_type x11 -> x2, local copies, waits for them, and re-layouts: 6.94 us -> 0.12 us  [body(): term_k.astype(BF)]
    reshape x8 -> x0, local copies, waits for them, and re-layouts: 6.58 us -> none  [the longest x1 1.5 us: body(): recv_x.reshape(slots_all, width)]
  transfers between devices with their start and end apart: 13 -> 23, of which waited for: 13 -> 9; matrix products, arithmetic and copies ran while one was open for 4% -> 0% of each run, Pallas kernels for 0% -> 0%
where the time goes in v1:
time: 281 us; the launch traced here: 279 us
  starting transfers between devices  146 us (52%)
  waiting for transfers between devices  86.1 us (31%)
  blocking collectives  22.3 us (8%)
  other arithmetic  12.1 us (4%)
  matrix products  6.19 us (2%)
  local copies, waits for them, and re-layouts  4.3 us (2%)
    ppermute x20, starting transfers between devices, shift(): lax.ppermute(array, 'local', [(i, (i + by) % n_local) for i in range(n_lo...  131 us
    ppermute x20, waiting for transfers between devices, shift(): lax.ppermute(array, 'local', [(i, (i + by) % n_local) for i in range(n_lo...  63.8 us
    all_to_all x1, blocking collectives, body(): got = lax.all_to_all(send, 'group', split_axis=0, concat_axis=0, tiled=True)  22.3 us
    all_to_all x1, waiting for transfers between devices, body(): got = lax.all_to_all(send, 'group', split_axis=0, concat_axis=0, tiled=True)  17.6 us
    ppermute x2, starting transfers between devices, swap(): return lax.ppermute(array, 'group', [(i, i ^ 1) for i in range(n_group)])  7.91 us
    all_to_all x1, starting transfers between devices, body(): got = lax.all_to_all(send, 'group', split_axis=0, concat_axis=0, tiled=True)  7.63 us
    dot_general x15, matrix products, dot(): return lax.dot_general(a, b, (dims, ((), ())), preferred_element_type=F32)  6.19 us
  transfers between devices with their start and end apart: 23, of which 9 were waited for; matrix products, arithmetic and copies ran while one was open for 0% of the time, Pallas kernels for 0%

profile of v1, /device:TPU:1, one launch (start us, length us, event | category | flops | bytes accessed | tf_op | source)
XLA Modules:
  0.0 278.9 jit_solution(9914112673749187276)
XLA Ops:
  0.6 0.8 fusion.125
  1.4 0.8 copy.47
  2.2 0.8 fusion.135
  3.0 0.8 pad_maximum_fusion.10
  3.7 16.3 %collective-permute-start = (bf16[8,4224]{1,0:T(8,128)(2,1)S(1)}, bf16[8,4224]{1,0:T(8,128)(2,1)S(1)}, u32[]{:S(2)}, u32[]{:S(2)}) collective-permute-start(bf16[8,4224]{1,0:T(8,128)(2,1)S(1)} %pad_maximum_fusion.10), channel_id=1, source_target_pairs={{0,8},{1,9},{2,10},{3,11},{4,12},{5,13},{6,14},{7,15},{8,16},{9,17... | collective-permute-start | bytes 202760 | tf_op jit(solution)/shard_map/ppermute | solution.py:35
  20.0 19.1 %collective-permute-start.1 = (bf16[8,4224]{1,0:T(8,128)(2,1)S(1)}, bf16[8,4224]{1,0:T(8,128)(2,1)S(1)}, u32[]{:S(2)}, u32[]{:S(2)}) collective-permute-start(bf16[8,4224]{1,0:T(8,128)(2,1)S(1)} %pad_maximum_fusion.10), channel_id=1, source_target_pairs={{0,16},{1,17},{2,18},{3,19},{4,20},{5,21},{6,22},{7,23},{8,24},{9,... | collective-permute-start | bytes 202760 | tf_op jit(solution)/shard_map/ppermute | solution.py:35
  39.1 8.2 %collective-permute-start.2 = (bf16[8,4224]{1,0:T(8,128)(2,1)S(1)}, bf16[8,4224]{1,0:T(8,128)(2,1)S(1)}, u32[]{:S(2)}, u32[]{:S(2)}) collective-permute-start(bf16[8,4224]{1,0:T(8,128)(2,1)S(1)} %pad_maximum_fusion.10), channel_id=1, source_target_pairs={{0,24},{1,25},{2,26},{3,27},{4,28},{5,29},{6,30},{7,31},{8,0},{9,1... | collective-permute-start | bytes 202760 | tf_op jit(solution)/shard_map/ppermute | solution.py:35
  47.3 5.6 %collective-permute-done.1 = bf16[8,4224]{1,0:T(8,128)(2,1)S(1)} collective-permute-done((bf16[8,4224]{1,0:T(8,128)(2,1)S(1)}, bf16[8,4224]{1,0:T(8,128)(2,1)S(1)}, u32[]{:S(2)}, u32[]{:S(2)}) %collective-permute-start.1) | collective-permute-done | bytes 67616 | tf_op jit(solution)/shard_map/ppermute | solution.py:35
  52.9 11.7 %collective-permute-done.2 = bf16[8,4224]{1,0:T(8,128)(2,1)S(1)} collective-permute-done((bf16[8,4224]{1,0:T(8,128)(2,1)S(1)}, bf16[8,4224]{1,0:T(8,128)(2,1)S(1)}, u32[]{:S(2)}, u32[]{:S(2)}) %collective-permute-start.2) | collective-permute-done | bytes 67616 | tf_op jit(solution)/shard_map/ppermute | solution.py:35
  65.6 0.8 pad_maximum_fusion.5
  66.4 1.1 fusion.2
  67.8 1.2 pad_maximum_fusion
  69.0 7.6 %all-to-all-start = ((bf16[32,8,2176]{2,1,0:T(8,128)(2,1)}), bf16[32,8,2176]{2,1,0:T(8,128)(2,1)S(1)}, u32[]{:S(2)}, u32[]{:S(2)}) async-start(bf16[32,8,2176]{2,1,0:T(8,128)(2,1)} %bitcast.7), calls=%async_computation | async-start | bytes 2228224 | tf_op jit(solution)/shard_map/all_to_all | solution.py:64
  76.7 17.6 %all-to-all-done = bf16[32,8,2176]{2,1,0:T(8,128)(2,1)S(1)} async-done(((bf16[32,8,2176]{2,1,0:T(8,128)(2,1)}), bf16[32,8,2176]{2,1,0:T(8,128)(2,1)S(1)}, u32[]{:S(2)}, u32[]{:S(2)}) %all-to-all-start) | async-done | bytes 1114144 | tf_op jit(solution)/shard_map/all_to_all | solution.py:64
  95.6 1.9 collective-permute-start.3
  97.6 6.7 %collective-permute-start.4 = (bf16[32,2048]{1,0:T(8,128)(2,1)S(1)}, bf16[32,2048]{1,0:T(8,128)(2,1)S(1)}, u32[]{:S(2)}, u32[]{:S(2)}) collective-permute-start(bf16[32,2048]{1,0:T(8,128)(2,1)S(1)} %get-tuple-element.22), channel_id=1, source_target_pairs={{0,30},{1,31},{2,0},{3,1},{4,2},{5,3},{6,4},{7,5},{8,6},{9,7},{10,... | collective-permute-start | bytes 393224 | tf_op jit(solution)/shard_map/ppermute | solution.py:35
  104.3 4.6 %collective-permute-start.5 = (bf16[32,2048]{1,0:T(8,128)(2,1)S(1)}, bf16[32,2048]{1,0:T(8,128)(2,1)S(1)}, u32[]{:S(2)}, u32[]{:S(2)}) collective-permute-start(bf16[32,2048]{1,0:T(8,128)(2,1)S(1)} %get-tuple-element.23), channel_id=1, source_target_pairs={{0,31},{1,0},{2,1},{3,2},{4,3},{5,4},{6,5},{7,6},{8,7},{9,8},{10,9... | collective-permute-start | bytes 393224 | tf_op jit(solution)/shard_map/ppermute | solution.py:35
  108.9 1.9 collective-permute-start.6
  110.8 1.9 collective-permute-start.7
  112.8 2.7 collective-permute-start.8
  115.5 5.2 %collective-permute-start.9 = (bf16[32,2048]{1,0:T(8,128)(2,1)S(1)}, bf16[32,2048]{1,0:T(8,128)(2,1)S(1)}, u32[]{:S(2)}, u32[]{:S(2)}) collective-permute-start(bf16[32,2048]{1,0:T(8,128)(2,1)S(1)} %get-tuple-element.20), channel_id=1, source_target_pairs={{0,4},{1,5},{2,6},{3,7},{4,8},{5,9},{6,10},{7,11},{8,12},{9,13},{1... | collective-permute-start | bytes 393224 | tf_op jit(solution)/shard_map/ppermute | solution.py:35
  120.8 12.5 %collective-permute-done.8 = bf16[32,2048]{1,0:T(8,128)(2,1)S(1)} collective-permute-done((bf16[32,2048]{1,0:T(8,128)(2,1)S(1)}, bf16[32,2048]{1,0:T(8,128)(2,1)S(1)}, u32[]{:S(2)}, u32[]{:S(2)}) %collective-permute-start.8) | collective-permute-done | bytes 131104 | tf_op jit(solution)/shard_map/ppermute | solution.py:35
  133.4 5.6 %collective-permute-start.10 = (bf16[256,2048]{1,0:T(8,128)(2,1)S(1)}, bf16[256,2048]{1,0:T(8,128)(2,1)S(1)}, u32[]{:S(2)}, u32[]{:S(2)}) collective-permute-start(bf16[256,2048]{1,0:T(8,128)(2,1)S(1)} %constant_dynamic-update-slice_fusion), channel_id=1, source_target_pairs={{0,32},{32,0},{64,96},{96,64},{128,160},{160,128},{192,224},{224,1... | collective-permute-start | bytes 3145736 | tf_op jit(solution)/shard_map/ppermute | solution.py:38
  139.0 2.3 collective-permute-done.10
  141.6 1.0 copy-done.5
  144.5 0.5 fusion.21
  145.0 0.5 convolution_add_fusion
  145.8 1.3 pad_maximum_fusion.2
  147.2 2.3 collective-permute-start.11
  149.6 2.5 collective-permute-done.11
  152.1 3.3 %add_convert_fusion = (bf16[256,1024]{1,0:T(8,128)(2,1)}, f32[256]{0:T(256)S(1)}) fusion(f32[256,2048]{1,0:T(8,128)} %copy-done.1, bf16[256,2048]{1,0:T(8,128)(2,1)} %collective-permute-done.11, pred[]{:T(512)S(6)} %eq.187, f32[256,2048]{1,0:T(8,128)S(1)} %fusion.16, bf16[256,2048]{1,0:T(8,128)(2,1)} %copy-done.3), kind=kLoop, calls=%fused_computation.62 | loop fusion | flops 2621184 | bytes 6292481 | tf_op jit(solution)/shard_map/convert_element_type | solution.py:128
  155.4 1.5 fusion.8
  157.0 11.1 %collective-permute-start.12 = (bf16[32,2048]{1,0:T(8,128)(2,1)S(1)}, bf16[32,2048]{1,0:T(8,128)(2,1)S(1)}, u32[]{:S(2)}, u32[]{:S(2)}) collective-permute-start(bf16[32,2048]{1,0:T(8,128)(2,1)S(1)} %get-tuple-element.8), channel_id=1, source_target_pairs={{0,3},{1,4},{2,5},{3,6},{4,7},{5,8},{6,9},{7,10},{8,11},{9,12},{10... | collective-permute-start | bytes 393224 | tf_op jit(solution)/shard_map/ppermute | solution.py:35
  168.1 1.9 collective-permute-start.13
  170.0 2.2 collective-permute-start.14
  172.2 4.3 %collective-permute-start.15 = (bf16[32,2048]{1,0:T(8,128)(2,1)S(1)}, bf16[32,2048]{1,0:T(8,128)(2,1)S(1)}, u32[]{:S(2)}, u32[]{:S(2)}) collective-permute-start(bf16[32,2048]{1,0:T(8,128)(2,1)S(1)} %get-tuple-element.11), channel_id=1, source_target_pairs={{0,31},{1,0},{2,1},{3,2},{4,3},{5,4},{6,5},{7,6},{8,7},{9,8},{10,9... | collective-permute-start | bytes 393224 | tf_op jit(solution)/shard_map/ppermute | solution.py:35
  176.6 4.3 %collective-permute-start.16 = (bf16[32,2048]{1,0:T(8,128)(2,1)S(1)}, bf16[32,2048]{1,0:T(8,128)(2,1)S(1)}, u32[]{:S(2)}, u32[]{:S(2)}) collective-permute-start(bf16[32,2048]{1,0:T(8,128)(2,1)S(1)} %get-tuple-element.12), channel_id=1, source_target_pairs={{0,30},{1,31},{2,0},{3,1},{4,2},{5,3},{6,4},{7,5},{8,6},{9,7},{10,... | collective-permute-start | bytes 393224 | tf_op jit(solution)/shard_map/ppermute | solution.py:35
  180.8 4.3 %collective-permute-start.17 = (bf16[32,2048]{1,0:T(8,128)(2,1)S(1)}, bf16[32,2048]{1,0:T(8,128)(2,1)S(1)}, u32[]{:S(2)}, u32[]{:S(2)}) collective-permute-start(bf16[32,2048]{1,0:T(8,128)(2,1)S(1)} %get-tuple-element.13), channel_id=1, source_target_pairs={{0,29},{1,30},{2,31},{3,0},{4,1},{5,2},{6,3},{7,4},{8,5},{9,6},{10... | collective-permute-start | bytes 393224 | tf_op jit(solution)/shard_map/ppermute | solution.py:35
  185.1 5.2 %collective-permute-start.18 = (bf16[32,2048]{1,0:T(8,128)(2,1)S(1)}, bf16[32,2048]{1,0:T(8,128)(2,1)S(1)}, u32[]{:S(2)}, u32[]{:S(2)}) collective-permute-start(bf16[32,2048]{1,0:T(8,128)(2,1)S(1)} %get-tuple-element.7), channel_id=1, source_target_pairs={{0,28},{1,29},{2,30},{3,31},{4,0},{5,1},{6,2},{7,3},{8,4},{9,5},{1... | collective-permute-start | bytes 393224 | tf_op jit(solution)/shard_map/ppermute | solution.py:35
  190.4 2.4 collective-permute-done.17
  192.8 15.8 %collective-permute-done.18 = bf16[32,2048]{1,0:T(8,128)(2,1)S(1)} collective-permute-done((bf16[32,2048]{1,0:T(8,128)(2,1)S(1)}, bf16[32,2048]{1,0:T(8,128)(2,1)S(1)}, u32[]{:S(2)}, u32[]{:S(2)}) %collective-permute-start.18) | collective-permute-done | bytes 131104 | tf_op jit(solution)/shard_map/ppermute | solution.py:35
  209.9 22.3 %all_to_all.10 = bf16[32,8,2176]{2,1,0:T(8,128)(2,1)S(1)} all-to-all(bf16[32,8,2176]{2,1,0:T(8,128)(2,1)S(1)} %maximum_bitcast_fusion), channel_id=1, replica_groups=mesh['group'=32,'local'=32] {'group'}, dimensions={0} | all-to-all | bytes 2228224 | tf_op jit(solution)/shard_map/all_to_all | solution.py:141
  232.9 8.6 %collective-permute-start.19 = (bf16[8,4224]{1,0:T(8,128)(2,1)S(1)}, bf16[8,4224]{1,0:T(8,128)(2,1)S(1)}, u32[]{:S(2)}, u32[]{:S(2)}) collective-permute-start(bf16[8,4224]{1,0:T(8,128)(2,1)S(1)} %get-tuple-element.27), channel_id=1, source_target_pairs={{0,24},{1,25},{2,26},{3,27},{4,28},{5,29},{6,30},{7,31},{8,0},{9,1... | collective-permute-start | bytes 202760 | tf_op jit(solution)/shard_map/ppermute | solution.py:35
  241.5 9.8 %collective-permute-start.20 = (bf16[8,4224]{1,0:T(8,128)(2,1)S(1)}, bf16[8,4224]{1,0:T(8,128)(2,1)S(1)}, u32[]{:S(2)}, u32[]{:S(2)}) collective-permute-start(bf16[8,4224]{1,0:T(8,128)(2,1)S(1)} %get-tuple-element.29), channel_id=1, source_target_pairs={{0,16},{1,17},{2,18},{3,19},{4,20},{5,21},{6,22},{7,23},{8,24},{9,... | collective-permute-start | bytes 202760 | tf_op jit(solution)/shard_map/ppermute | solution.py:35
  251.4 10.6 %collective-permute-start.21 = (bf16[8,4224]{1,0:T(8,128)(2,1)S(1)}, bf16[8,4224]{1,0:T(8,128)(2,1)S(1)}, u32[]{:S(2)}, u32[]{:S(2)}) collective-permute-start(bf16[8,4224]{1,0:T(8,128)(2,1)S(1)} %get-tuple-element.28), channel_id=1, source_target_pairs={{0,8},{1,9},{2,10},{3,11},{4,12},{5,13},{6,14},{7,15},{8,16},{9,17... | collective-permute-start | bytes 202760 | tf_op jit(solution)/shard_map/ppermute | solution.py:35
  262.0 15.6 %collective-permute-done.20 = bf16[8,4224]{1,0:T(8,128)(2,1)S(1)} collective-permute-done((bf16[8,4224]{1,0:T(8,128)(2,1)S(1)}, bf16[8,4224]{1,0:T(8,128)(2,1)S(1)}, u32[]{:S(2)}, u32[]{:S(2)}) %collective-permute-start.20) | collective-permute-done | bytes 67616 | tf_op jit(solution)/shard_map/ppermute | solution.py:35
  277.6 0.6 fusion.157
  278.3 0.6 slice.323
  (110 shorter events, 7.2 us)
Async XLA Ops:
  0.6 143.0 %copy-start = (bf16[1,1,256,2048]{3,2,1,0:T(8,128)(2,1)S(1)}, bf16[1,1,256,2048]{3,2,1,0:T(8,128)(2,1)}, u32[]{:S(2)}) copy-start(bf16[1,1,256,2048]{3,2,1,0:T(8,128)(2,1)} %param.15) | copy-start | bytes 3145732
  3.7 43.6 %collective-permute-start = (bf16[8,4224]{1,0:T(8,128)(2,1)S(1)}, bf16[8,4224]{1,0:T(8,128)(2,1)S(1)}, u32[]{:S(2)}, u32[]{:S(2)}) collective-permute-start(bf16[8,4224]{1,0:T(8,128)(2,1)S(1)} %pad_maximum_fusion.10), channel_id=1, source_target_pairs={{0,8},{1,9},{2,10},{3,11},{4,12},{5,13},{6,14},{7,15},{8,16},{9,17... | collective-permute-start | bytes 202760 | tf_op jit(solution)/shard_map/ppermute | solution.py:35
  20.0 32.9 %collective-permute-start.1 = (bf16[8,4224]{1,0:T(8,128)(2,1)S(1)}, bf16[8,4224]{1,0:T(8,128)(2,1)S(1)}, u32[]{:S(2)}, u32[]{:S(2)}) collective-permute-start(bf16[8,4224]{1,0:T(8,128)(2,1)S(1)} %pad_maximum_fusion.10), channel_id=1, source_target_pairs={{0,16},{1,17},{2,18},{3,19},{4,20},{5,21},{6,22},{7,23},{8,24},{9,... | collective-permute-start | bytes 202760 | tf_op jit(solution)/shard_map/ppermute | solution.py:35
  39.1 25.6 %collective-permute-start.2 = (bf16[8,4224]{1,0:T(8,128)(2,1)S(1)}, bf16[8,4224]{1,0:T(8,128)(2,1)S(1)}, u32[]{:S(2)}, u32[]{:S(2)}) collective-permute-start(bf16[8,4224]{1,0:T(8,128)(2,1)S(1)} %pad_maximum_fusion.10), channel_id=1, source_target_pairs={{0,24},{1,25},{2,26},{3,27},{4,28},{5,29},{6,30},{7,31},{8,0},{9,1... | collective-permute-start | bytes 202760 | tf_op jit(solution)/shard_map/ppermute | solution.py:35
  65.2 2.3 copy-start.6
  65.2 2.3 copy-start.7
  69.0 25.3 %all-to-all-start = ((bf16[32,8,2176]{2,1,0:T(8,128)(2,1)}), bf16[32,8,2176]{2,1,0:T(8,128)(2,1)S(1)}, u32[]{:S(2)}, u32[]{:S(2)}) async-start(bf16[32,8,2176]{2,1,0:T(8,128)(2,1)} %bitcast.7), calls=%async_computation | async-start | bytes 2228224 | tf_op jit(solution)/shard_map/all_to_all | solution.py:64
  95.6 17.1 %collective-permute-start.3 = (bf16[32,2048]{1,0:T(8,128)(2,1)S(1)}, bf16[32,2048]{1,0:T(8,128)(2,1)S(1)}, u32[]{:S(2)}, u32[]{:S(2)}) collective-permute-start(bf16[32,2048]{1,0:T(8,128)(2,1)S(1)} %get-tuple-element.21), channel_id=1, source_target_pairs={{0,29},{1,30},{2,31},{3,0},{4,1},{5,2},{6,3},{7,4},{8,5},{9,6},{10... | collective-permute-start | bytes 393224 | tf_op jit(solution)/shard_map/ppermute | solution.py:35
  97.6 17.9 %collective-permute-start.4 = (bf16[32,2048]{1,0:T(8,128)(2,1)S(1)}, bf16[32,2048]{1,0:T(8,128)(2,1)S(1)}, u32[]{:S(2)}, u32[]{:S(2)}) collective-permute-start(bf16[32,2048]{1,0:T(8,128)(2,1)S(1)} %get-tuple-element.22), channel_id=1, source_target_pairs={{0,30},{1,31},{2,0},{3,1},{4,2},{5,3},{6,4},{7,5},{8,6},{9,7},{10,... | collective-permute-start | bytes 393224 | tf_op jit(solution)/shard_map/ppermute | solution.py:35
  104.3 16.4 %collective-permute-start.5 = (bf16[32,2048]{1,0:T(8,128)(2,1)S(1)}, bf16[32,2048]{1,0:T(8,128)(2,1)S(1)}, u32[]{:S(2)}, u32[]{:S(2)}) collective-permute-start(bf16[32,2048]{1,0:T(8,128)(2,1)S(1)} %get-tuple-element.23), channel_id=1, source_target_pairs={{0,31},{1,0},{2,1},{3,2},{4,3},{5,4},{6,5},{7,6},{8,7},{9,8},{10,9... | collective-permute-start | bytes 393224 | tf_op jit(solution)/shard_map/ppermute | solution.py:35
  108.9 11.8 %collective-permute-start.6 = (bf16[32,2048]{1,0:T(8,128)(2,1)S(1)}, bf16[32,2048]{1,0:T(8,128)(2,1)S(1)}, u32[]{:S(2)}, u32[]{:S(2)}) collective-permute-start(bf16[32,2048]{1,0:T(8,128)(2,1)S(1)} %get-tuple-element.24), channel_id=1, source_target_pairs={{0,1},{1,2},{2,3},{3,4},{4,5},{5,6},{6,7},{7,8},{8,9},{9,10},{10,1... | collective-permute-start | bytes 393224 | tf_op jit(solution)/shard_map/ppermute | solution.py:35
  110.8 9.9 %collective-permute-start.7 = (bf16[32,2048]{1,0:T(8,128)(2,1)S(1)}, bf16[32,2048]{1,0:T(8,128)(2,1)S(1)}, u32[]{:S(2)}, u32[]{:S(2)}) collective-permute-start(bf16[32,2048]{1,0:T(8,128)(2,1)S(1)} %get-tuple-element.25), channel_id=1, source_target_pairs={{0,2},{1,3},{2,4},{3,5},{4,6},{5,7},{6,8},{7,9},{8,10},{9,11},{10,... | collective-permute-start | bytes 393224 | tf_op jit(solution)/shard_map/ppermute | solution.py:35
  112.8 20.6 %collective-permute-start.8 = (bf16[32,2048]{1,0:T(8,128)(2,1)S(1)}, bf16[32,2048]{1,0:T(8,128)(2,1)S(1)}, u32[]{:S(2)}, u32[]{:S(2)}) collective-permute-start(bf16[32,2048]{1,0:T(8,128)(2,1)S(1)} %get-tuple-element.26), channel_id=1, source_target_pairs={{0,3},{1,4},{2,5},{3,6},{4,7},{5,8},{6,9},{7,10},{8,11},{9,12},{10... | collective-permute-start | bytes 393224 | tf_op jit(solution)/shard_map/ppermute | solution.py:35
  115.5 17.9 %collective-permute-start.9 = (bf16[32,2048]{1,0:T(8,128)(2,1)S(1)}, bf16[32,2048]{1,0:T(8,128)(2,1)S(1)}, u32[]{:S(2)}, u32[]{:S(2)}) collective-permute-start(bf16[32,2048]{1,0:T(8,128)(2,1)S(1)} %get-tuple-element.20), channel_id=1, source_target_pairs={{0,4},{1,5},{2,6},{3,7},{4,8},{5,9},{6,10},{7,11},{8,12},{9,13},{1... | collective-permute-start | bytes 393224 | tf_op jit(solution)/shard_map/ppermute | solution.py:35
  133.4 8.1 %copy-start.3 = (bf16[256,2048]{1,0:T(8,128)(2,1)}, bf16[256,2048]{1,0:T(8,128)(2,1)S(1)}, u32[]{:S(2)}) copy-start(bf16[256,2048]{1,0:T(8,128)(2,1)S(1)} %constant_dynamic-update-slice_fusion) | copy-start | bytes 3145732
  133.4 7.9 %collective-permute-start.10 = (bf16[256,2048]{1,0:T(8,128)(2,1)S(1)}, bf16[256,2048]{1,0:T(8,128)(2,1)S(1)}, u32[]{:S(2)}, u32[]{:S(2)}) collective-permute-start(bf16[256,2048]{1,0:T(8,128)(2,1)S(1)} %constant_dynamic-update-slice_fusion), channel_id=1, source_target_pairs={{0,32},{32,0},{64,96},{96,64},{128,160},{160,128},{192,224},{224,1... | collective-permute-start | bytes 3145736 | tf_op jit(solution)/shard_map/ppermute | solution.py:38
  141.4 1.2 copy-start.5
  141.6 1.5 copy-start.4
  145.5 1.6 copy-start.1
  147.2 4.9 %collective-permute-start.11 = (bf16[256,2048]{1,0:T(8,128)(2,1)}, bf16[256,2048]{1,0:T(8,128)(2,1)}, u32[]{:S(2)}, u32[]{:S(2)}) collective-permute-start(bf16[256,2048]{1,0:T(8,128)(2,1)} %pad_maximum_fusion.2), channel_id=1, source_target_pairs={{0,32},{32,0},{64,96},{96,64},{128,160},{160,128},{192,224},{224,1... | collective-permute-start | bytes 3145736 | tf_op jit(solution)/shard_map/ppermute | solution.py:38
  155.4 1.6 copy-start.2
  157.0 23.8 %collective-permute-start.12 = (bf16[32,2048]{1,0:T(8,128)(2,1)S(1)}, bf16[32,2048]{1,0:T(8,128)(2,1)S(1)}, u32[]{:S(2)}, u32[]{:S(2)}) collective-permute-start(bf16[32,2048]{1,0:T(8,128)(2,1)S(1)} %get-tuple-element.8), channel_id=1, source_target_pairs={{0,3},{1,4},{2,5},{3,6},{4,7},{5,8},{6,9},{7,10},{8,11},{9,12},{10... | collective-permute-start | bytes 393224 | tf_op jit(solution)/shard_map/ppermute | solution.py:35
  168.1 17.0 %collective-permute-start.13 = (bf16[32,2048]{1,0:T(8,128)(2,1)S(1)}, bf16[32,2048]{1,0:T(8,128)(2,1)S(1)}, u32[]{:S(2)}, u32[]{:S(2)}) collective-permute-start(bf16[32,2048]{1,0:T(8,128)(2,1)S(1)} %get-tuple-element.9), channel_id=1, source_target_pairs={{0,2},{1,3},{2,4},{3,5},{4,6},{5,7},{6,8},{7,9},{8,10},{9,11},{10,... | collective-permute-start | bytes 393224 | tf_op jit(solution)/shard_map/ppermute | solution.py:35
  170.0 20.3 %collective-permute-start.14 = (bf16[32,2048]{1,0:T(8,128)(2,1)S(1)}, bf16[32,2048]{1,0:T(8,128)(2,1)S(1)}, u32[]{:S(2)}, u32[]{:S(2)}) collective-permute-start(bf16[32,2048]{1,0:T(8,128)(2,1)S(1)} %get-tuple-element.10), channel_id=1, source_target_pairs={{0,1},{1,2},{2,3},{3,4},{4,5},{5,6},{6,7},{7,8},{8,9},{9,10},{10,1... | collective-permute-start | bytes 393224 | tf_op jit(solution)/shard_map/ppermute | solution.py:35
  172.2 18.1 %collective-permute-start.15 = (bf16[32,2048]{1,0:T(8,128)(2,1)S(1)}, bf16[32,2048]{1,0:T(8,128)(2,1)S(1)}, u32[]{:S(2)}, u32[]{:S(2)}) collective-permute-start(bf16[32,2048]{1,0:T(8,128)(2,1)S(1)} %get-tuple-element.11), channel_id=1, source_target_pairs={{0,31},{1,0},{2,1},{3,2},{4,3},{5,4},{6,5},{7,6},{8,7},{9,8},{10,9... | collective-permute-start | bytes 393224 | tf_op jit(solution)/shard_map/ppermute | solution.py:35
  176.6 13.9 %collective-permute-start.16 = (bf16[32,2048]{1,0:T(8,128)(2,1)S(1)}, bf16[32,2048]{1,0:T(8,128)(2,1)S(1)}, u32[]{:S(2)}, u32[]{:S(2)}) collective-permute-start(bf16[32,2048]{1,0:T(8,128)(2,1)S(1)} %get-tuple-element.12), channel_id=1, source_target_pairs={{0,30},{1,31},{2,0},{3,1},{4,2},{5,3},{6,4},{7,5},{8,6},{9,7},{10,... | collective-permute-start | bytes 393224 | tf_op jit(solution)/shard_map/ppermute | solution.py:35
  180.8 12.0 %collective-permute-start.17 = (bf16[32,2048]{1,0:T(8,128)(2,1)S(1)}, bf16[32,2048]{1,0:T(8,128)(2,1)S(1)}, u32[]{:S(2)}, u32[]{:S(2)}) collective-permute-start(bf16[32,2048]{1,0:T(8,128)(2,1)S(1)} %get-tuple-element.13), channel_id=1, source_target_pairs={{0,29},{1,30},{2,31},{3,0},{4,1},{5,2},{6,3},{7,4},{8,5},{9,6},{10... | collective-permute-start | bytes 393224 | tf_op jit(solution)/shard_map/ppermute | solution.py:35
  185.1 23.5 %collective-permute-start.18 = (bf16[32,2048]{1,0:T(8,128)(2,1)S(1)}, bf16[32,2048]{1,0:T(8,128)(2,1)S(1)}, u32[]{:S(2)}, u32[]{:S(2)}) collective-permute-start(bf16[32,2048]{1,0:T(8,128)(2,1)S(1)} %get-tuple-element.7), channel_id=1, source_target_pairs={{0,28},{1,29},{2,30},{3,31},{4,0},{5,1},{6,2},{7,3},{8,4},{9,5},{1... | collective-permute-start | bytes 393224 | tf_op jit(solution)/shard_map/ppermute | solution.py:35
  232.9 29.1 %collective-permute-start.19 = (bf16[8,4224]{1,0:T(8,128)(2,1)S(1)}, bf16[8,4224]{1,0:T(8,128)(2,1)S(1)}, u32[]{:S(2)}, u32[]{:S(2)}) collective-permute-start(bf16[8,4224]{1,0:T(8,128)(2,1)S(1)} %get-tuple-element.27), channel_id=1, source_target_pairs={{0,24},{1,25},{2,26},{3,27},{4,28},{5,29},{6,30},{7,31},{8,0},{9,1... | collective-permute-start | bytes 202760 | tf_op jit(solution)/shard_map/ppermute | solution.py:35
  241.5 36.1 %collective-permute-start.20 = (bf16[8,4224]{1,0:T(8,128)(2,1)S(1)}, bf16[8,4224]{1,0:T(8,128)(2,1)S(1)}, u32[]{:S(2)}, u32[]{:S(2)}) collective-permute-start(bf16[8,4224]{1,0:T(8,128)(2,1)S(1)} %get-tuple-element.29), channel_id=1, source_target_pairs={{0,16},{1,17},{2,18},{3,19},{4,20},{5,21},{6,22},{7,23},{8,24},{9,... | collective-permute-start | bytes 202760 | tf_op jit(solution)/shard_map/ppermute | solution.py:35
  251.4 26.2 %collective-permute-start.21 = (bf16[8,4224]{1,0:T(8,128)(2,1)S(1)}, bf16[8,4224]{1,0:T(8,128)(2,1)S(1)}, u32[]{:S(2)}, u32[]{:S(2)}) collective-permute-start(bf16[8,4224]{1,0:T(8,128)(2,1)S(1)} %get-tuple-element.28), channel_id=1, source_target_pairs={{0,8},{1,9},{2,10},{3,11},{4,12},{5,13},{6,14},{7,15},{8,16},{9,17... | collective-permute-start | bytes 202760 | tf_op jit(solution)/shard_map/ppermute | solution.py:35

commit v2 on v1

v2 whole, which is shorter than its diff:
```python
import jax
import jax.numpy as jnp
from jax import lax
from jax.sharding import PartitionSpec as P

BF = jnp.bfloat16
F32 = jnp.float32
META = 128


def dot(a, b, dims):
    return lax.dot_general(a, b, (dims, ((), ())), preferred_element_type=F32)


def body(tokens, grad_mixed, gates, group_ids, expert_ids, w_gate, w_up, w_down):
    n_group = lax.axis_size("group")
    n_local = lax.axis_size("local")
    near = 8 if n_local % 8 == 0 and n_local > 8 else n_local // 2
    far = n_local // near
    groups = n_group // 2
    tok = tokens.shape[0]
    width = tokens.shape[1]
    half = width // 2
    topk = expert_ids.shape[1]
    named = group_ids.shape[1]
    per_group = named * tok // groups
    capacity = (25 * tok + n_local - 1) // n_local
    pad = (capacity // 8 + 1) * 8
    me = lax.axis_index("group")
    my_group = (me // 2).astype(BF)
    core = me % 2
    z = lax.axis_index("local")

    def shift(array, by):
        return lax.ppermute(array, "local", [(i, (i + by) % n_local) for i in range(n_local)])

    def hop(array, step, sign):
        if step == 0:
            return array
        if step != near // 2:
            return shift(array, sign * step)
        pairs = [
            (g * n_local + i, g * n_local + (i + sign * (step if g % 2 == 0 else -step)) % n_local)
            for g in range(n_group)
            for i in range(n_local)
        ]
        return lax.ppermute(array, ("group", "local"), pairs)

    def swap(array):
        return lax.ppermute(array, "group", [(i, i ^ 1) for i in range(n_group)])

    group_iota = jnp.arange(groups, dtype=jnp.int32)[None, :]
    member = jnp.zeros((tok, groups), F32)
    for n in range(named):
        member = jnp.maximum(member, (group_ids[:, n : n + 1] == group_iota).astype(F32))
    order = jnp.arange(tok, dtype=jnp.int32)
    placed = dot((order[None, :] < order[:, None]).astype(BF), member.astype(BF), ((1,), (0,)))
    code = jnp.where(member > 0, placed, -1.0)
    meta = jnp.concatenate(
        [(expert_ids // n_local).astype(BF), (expert_ids % n_local).astype(BF), gates, code.astype(BF)], axis=1
    )
    meta = jnp.pad(meta, ((0, 0), (0, META - meta.shape[1])))
    own = jnp.concatenate([tokens, grad_mixed, meta], axis=1)
    rows = lax.all_gather(
        own, "local", axis=0, tiled=True, axis_index_groups=[[b + near * f for f in range(far)] for b in range(near)]
    )

    codes = rows[:, 2 * width + 3 * topk : 2 * width + 3 * topk + groups].T
    codes = codes.astype(F32)[:, None, None, :] == jnp.arange(per_group, dtype=F32)[None, None, :, None]
    row_plane = jnp.arange(far * tok, dtype=jnp.int32) // tok
    planes = jnp.arange(far, dtype=jnp.int32)
    chooser = (codes & (row_plane[None, :] == planes[:, None])[None, :, None, :]).astype(BF)
    chooser = chooser.reshape(groups * far * per_group, far * tok)
    parts = []
    for c in range(2):
        piece = jnp.concatenate(
            [rows[:, c * half : (c + 1) * half], rows[:, width + c * half : width + (c + 1) * half], rows[:, 2 * width :]],
            axis=1,
        )
        parts.append(dot(chooser, piece, ((1,), (0,))).astype(BF).reshape(groups, 1, far * per_group, width + META))
    send = jnp.concatenate(parts, axis=1).reshape(n_group, far * per_group, width + META)
    got = lax.all_to_all(send, "group", split_axis=0, concat_axis=0, tiled=True)
    n_rows = n_group * far * per_group
    got = got.reshape(n_rows, width + META)

    steps = [near // 2] + [s for d in range(near // 2 - 1, 0, -1) for s in (d, -d)] + [0]
    info = got[:, width:].T
    row_group, row_pos, row_gate = info[:topk], info[topk : 2 * topk], info[2 * topk : 3 * topk]
    turned = jnp.where(core == 0, near // 2, n_local - near // 2)
    target = jnp.array([s % n_local for s in steps], jnp.int32).at[0].set(turned)
    target = ((z + target) % n_local).astype(BF)
    picked = (row_group == my_group)[:, None, :] & (row_pos[:, None, :] == target[None, :, None])
    counted = jnp.any(picked, axis=0)
    gate_at = jnp.sum(jnp.where(picked, row_gate.astype(F32)[:, None, :], 0.0), axis=0)
    index = jnp.arange(n_rows, dtype=jnp.int32)
    plane_of = (index // per_group) % far
    ahead = ((index[:, None] < index[None, :]) & (plane_of[:, None] == plane_of[None, :])).astype(BF)
    ranked = dot(counted.astype(BF), ahead, ((1,), (0,))).astype(jnp.int32)
    kept = counted & (ranked < capacity)
    slot = jnp.where(kept, ranked, -1)
    hit = (slot[:, None, None, :] == jnp.arange(pad, dtype=jnp.int32)[None, None, :, None]) & (
        plane_of[None, None, None, :] == jnp.arange(far, dtype=jnp.int32)[None, :, None, None]
    )
    n_slots = near * far * pad
    plain = hit.astype(BF).reshape(n_slots, n_rows)
    scaled = jnp.where(hit, gate_at[:, None, None, :], 0.0).astype(BF).reshape(n_slots, n_rows)
    slot_x = dot(plain, got[:, :half], ((1,), (0,))).astype(BF)
    slot_dy = dot(scaled, got[:, half:width], ((1,), (0,))).astype(BF)
    slots = jnp.concatenate([slot_x, slot_dy], axis=1).reshape(near, far * pad, width)
    mine = jnp.concatenate(
        [hop(slots[i], s, 1) for i, s in enumerate(steps)], axis=0
    )

    def own_first(array, axis):
        low = lax.slice_in_dim(array, 0, half, axis=axis)
        high = lax.slice_in_dim(array, half, width, axis=axis)
        return jnp.where(core == 0, low, high), jnp.where(core == 0, high, low)

    in_own, in_other = own_first(w_gate[0, 0], 0)
    lin_own, lin_other = own_first(w_up[0, 0], 0)
    out_own, out_other = own_first(w_down[0, 0], 1)
    other = swap(mine)
    pre_gate = dot(mine[:, :half], in_own, ((1,), (0,))) + dot(other[:, :half], in_other, ((1,), (0,)))
    pre_up = dot(mine[:, :half], lin_own, ((1,), (0,))) + dot(other[:, :half], lin_other, ((1,), (0,)))
    sigmoid = jax.nn.sigmoid(pre_gate)
    active = pre_gate * sigmoid
    hidden = (active * pre_up).astype(BF)
    grad_hidden = dot(mine[:, half:], out_own, ((1,), (1,))) + dot(other[:, half:], out_other, ((1,), (1,)))
    grad_pre = (grad_hidden * pre_up * sigmoid * (1.0 + pre_gate * (1.0 - sigmoid))).astype(BF)
    grad_lin = (grad_hidden * active).astype(BF)

    give_out = dot(hidden, out_other, ((1,), (0,))).astype(BF)
    give_back = (dot(grad_pre, in_other, ((1,), (1,))) + dot(grad_lin, lin_other, ((1,), (1,)))).astype(BF)
    gave = swap(jnp.concatenate([give_out, give_back], axis=1))
    sum_out = dot(hidden, out_own, ((1,), (0,))) + gave[:, :half].astype(F32)
    sum_back = (
        dot(grad_pre, in_own, ((1,), (1,))) + dot(grad_lin, lin_own, ((1,), (1,))) + gave[:, half:].astype(F32)
    )
    term = jnp.sum(mine[:, half:].astype(F32) * sum_out, axis=1, keepdims=True)
    spots = (jnp.arange(META, dtype=jnp.int32)[None, :] == jnp.arange(n_slots, dtype=jnp.int32)[:, None] % pad)
    spare = jnp.sum(jnp.where(spots, term, 0.0).reshape(near * far, pad, META), axis=1, keepdims=True)
    spare = jnp.where((jnp.arange(pad) == pad - 1)[None, :, None], spare, sum_out[:, :META].reshape(near * far, pad, META))
    ret = jnp.concatenate(
        [spare.reshape(n_slots, META).astype(BF), sum_out[:, META:].astype(BF), sum_back.astype(BF)], axis=1
    ).reshape(near, far * pad, width)
    ret = jnp.concatenate(
        [hop(ret[i], s, -1) for i, s in enumerate(steps)], axis=0
    )

    row_out = dot(scaled, ret[:, :half], ((0,), (0,)))
    row_back = dot(plain, ret[:, half:], ((0,), (0,)))
    terms = ret.reshape(near, far, pad, width)[:, :, pad - 1, :pad].astype(F32)
    term_at = jnp.sum(jnp.where(hit, terms[:, :, :, None], 0.0), axis=(1, 2))
    term_k = jnp.sum(jnp.where(picked, term_at[None], 0.0), axis=1) / row_gate.astype(F32)
    term_k = jnp.pad(term_k, ((0, META - topk), (0, 0))).T
    send = jnp.concatenate([row_out.astype(BF), row_back.astype(BF), term_k.astype(BF)], axis=1)
    send = send.reshape(n_group, far * per_group, width + META)
    got = lax.all_to_all(send, "group", split_axis=0, concat_axis=0, tiled=True)

    wanted = (z // near + planes) % far
    turned = chooser.reshape(groups * far * per_group, far, tok)
    turned = jnp.concatenate([jnp.take(turned, wanted[d], axis=1) for d in range(far)], axis=1)
    got = got.reshape(groups, 2, far * per_group, width + META)
    sums = [
        dot(turned, got[:, c].reshape(groups * far * per_group, width + META), ((0,), (0,))) for c in range(2)
    ]
    full = jnp.concatenate(
        [sums[0][:, :half], sums[1][:, :half], sums[0][:, half:width], sums[1][:, half:width], sums[0][:, width:] + sums[1][:, width:]],
        axis=1,
    ).reshape(far, tok, 2 * width + META)
    total = full[0]
    for f in range(1, far):
        total = total + shift(full[f].astype(BF), near * f).astype(F32)
    return (
        total[:, :width].astype(BF),
        total[:, width : 2 * width].astype(BF),
        total[:, 2 * width : 2 * width + topk],
    )


def solution(mesh):
    rows = P(("group", "local"), None)
    weights = P("group", "local", None, None)
    return jax.shard_map(
        body,
        mesh=mesh,
        in_specs=(rows, rows, rows, rows, rows, weights, weights, weights),
        out_specs=(rows, rows, rows),
        check_vma=False,
    )
```

time: 281 us -> 246 us (0.88)
  starting transfers between devices: 146 us -> 103 us
  waiting for transfers between devices: 86.1 us -> 55.5 us
  blocking collectives: 22.3 us -> 50.8 us
  between operations: 1.56 us -> 9.6 us
  matrix products: 6.19 us -> 10.1 us
  other arithmetic: 12.1 us -> 8.98 us
    ppermute x20 -> x15, starting transfers between devices: 131 us -> 69.7 us  [shift(): lax.ppermute(array, 'local', [(i, (i + by) % n_local) for i in range(n_lo...]
    all_gather x0 -> x1, blocking collectives: none -> 50.8 us  [body(): lax.all_gather(own, 'local', axis=0, tiled=True, axis_index_groups=[[b +...]
    ppermute x20 -> x15, waiting for transfers between devices: 63.8 us -> 27.4 us  [shift(): lax.ppermute(array, 'local', [(i, (i + by) % n_local) for i in range(n_lo...]
    all_to_all x1 -> x0, blocking collectives: 22.3 us -> none  [body(): got = lax.all_to_all(send, 'group', split_axis=0, concat_axis=0, tiled=True)]
    all_to_all x1 -> x2, starting transfers between devices: 7.63 us -> 19.2 us  [body(): got = lax.all_to_all(send, 'group', split_axis=0, concat_axis=0, tiled=True)]
    all_to_all x1 -> x2, waiting for transfers between devices: 17.6 us -> 25.7 us  [body(): got = lax.all_to_all(send, 'group', split_axis=0, concat_axis=0, tiled=True)]
    ppermute x0 -> x2, starting transfers between devices: none -> 6.57 us  [hop(): return lax.ppermute(array, ('group', 'local'), pairs)]
    dot_general x15 -> x22, matrix products: 6.19 us -> 10.1 us  [dot(): return lax.dot_general(a, b, (dims, ((), ())), preferred_element_type=F32)]
  transfers between devices with their start and end apart: 23 -> 21, of which waited for: 9 -> 11; matrix products, arithmetic and copies ran while one was open for 0% -> 2% of each run, Pallas kernels for 0% -> 0%
where the time goes in v2:
time: 246 us; the launch traced here: 245 us
  starting transfers between devices  103 us (42%)
  waiting for transfers between devices  55.5 us (23%)
  blocking collectives  50.8 us (21%)
  matrix products  10.1 us (4%)
  between operations  9.6 us (4%)
  other arithmetic  8.98 us (4%)
  local copies, waits for them, and re-layouts  7.04 us (3%)
    ppermute x15, starting transfers between devices, shift(): lax.ppermute(array, 'local', [(i, (i + by) % n_local) for i in range(n_lo...  69.7 us
    all_gather x1, blocking collectives, body(): lax.all_gather(own, 'local', axis=0, tiled=True, axis_index_groups=[[b +...  50.8 us
    ppermute x15, waiting for transfers between devices, shift(): lax.ppermute(array, 'local', [(i, (i + by) % n_local) for i in range(n_lo...  27.4 us
    all_to_all x2, waiting for transfers between devices, body(): got = lax.all_to_all(send, 'group', split_axis=0, concat_axis=0, tiled=True)  25.7 us
    all_to_all x2, starting transfers between devices, body(): got = lax.all_to_all(send, 'group', split_axis=0, concat_axis=0, tiled=True)  19.2 us
    dot_general x22, matrix products, dot(): return lax.dot_general(a, b, (dims, ((), ())), preferred_element_type=F32)  10.1 us
    ppermute x2, starting transfers between devices, swap(): return lax.ppermute(array, 'group', [(i, i ^ 1) for i in range(n_group)])  7.57 us
    ppermute x2, starting transfers between devices, hop(): return lax.ppermute(array, ('group', 'local'), pairs)  6.57 us
  transfers between devices with their start and end apart: 21, of which 11 were waited for; matrix products, arithmetic and copies ran while one was open for 2% of the time, Pallas kernels for 0%

profile of v2, /device:TPU:1, one launch (start us, length us, event | category | flops | bytes accessed | tf_op | source)
XLA Modules:
  0.0 245.1 jit_solution(16250168638142713935)
XLA Ops:
  0.6 0.8 slice_bitcast_fusion.7
  1.5 0.7 fusion.75
  2.4 0.8 fusion.88
  3.1 0.8 pad_maximum_fusion.4
  3.9 50.8 %all_gather.3 = bf16[32,4224]{1,0:T(8,128)(2,1)S(1)} all-gather(bf16[8,4224]{1,0:T(8,128)(2,1)S(1)} %pad_maximum_fusion.4), channel_id=1, replica_groups={{0,8,16,24},{1,9,17,25},{2,10,18,26},{3,11,19,27},{4,12,20,28},{5,13,21..., dimensions={0}, use_global_device_ids=true | all-gather | bytes 337920 | tf_op jit(solution)/shard_map/all_gather | solution.py:64
  54.9 0.7 fusion.106
  56.2 1.1 pad_maximum_fusion
  57.3 10.7 %all-to-all-start = ((bf16[32,8,2176]{2,1,0:T(8,128)(2,1)}), bf16[32,8,2176]{2,1,0:T(8,128)(2,1)S(1)}, u32[]{:S(2)}, u32[]{:S(2)}) async-start(bf16[32,8,2176]{2,1,0:T(8,128)(2,1)} %bitcast.17), calls=%async_computation | async-start | bytes 2228224 | tf_op jit(solution)/shard_map/all_to_all | solution.py:82
  68.2 17.5 %all-to-all-done = bf16[32,8,2176]{2,1,0:T(8,128)(2,1)S(1)} async-done(((bf16[32,8,2176]{2,1,0:T(8,128)(2,1)}), bf16[32,8,2176]{2,1,0:T(8,128)(2,1)S(1)}, u32[]{:S(2)}, u32[]{:S(2)}) %all-to-all-start) | async-done | bytes 1114144 | tf_op jit(solution)/shard_map/all_to_all | solution.py:82
  87.1 1.9 collective-permute-start
  89.1 3.4 %collective-permute-start.1 = (bf16[32,2048]{1,0:T(8,128)(2,1)S(1)}, bf16[32,2048]{1,0:T(8,128)(2,1)S(1)}, u32[]{:S(2)}, u32[]{:S(2)}) collective-permute-start(bf16[32,2048]{1,0:T(8,128)(2,1)S(1)} %get-tuple-element.40), channel_id=1, source_target_pairs={{0,3},{1,4},{2,5},{3,6},{4,7},{5,8},{6,9},{7,10},{8,11},{9,12},{10... | collective-permute-start | bytes 393224 | tf_op jit(solution)/shard_map/ppermute | solution.py:35
  92.5 4.8 %collective-permute-start.2 = (bf16[32,2048]{1,0:T(8,128)(2,1)S(1)}, bf16[32,2048]{1,0:T(8,128)(2,1)S(1)}, u32[]{:S(2)}, u32[]{:S(2)}) collective-permute-start(bf16[32,2048]{1,0:T(8,128)(2,1)S(1)} %get-tuple-element.41), channel_id=1, source_target_pairs={{0,29},{1,30},{2,31},{3,0},{4,1},{5,2},{6,3},{7,4},{8,5},{9,6},{10... | collective-permute-start | bytes 393224 | tf_op jit(solution)/shard_map/ppermute | solution.py:35
  97.4 4.0 %collective-permute-start.3 = (bf16[32,2048]{1,0:T(8,128)(2,1)S(1)}, bf16[32,2048]{1,0:T(8,128)(2,1)S(1)}, u32[]{:S(2)}, u32[]{:S(2)}) collective-permute-start(bf16[32,2048]{1,0:T(8,128)(2,1)S(1)} %get-tuple-element.42), channel_id=1, source_target_pairs={{0,2},{1,3},{2,4},{3,5},{4,6},{5,7},{6,8},{7,9},{8,10},{9,11},{10,... | collective-permute-start | bytes 393224 | tf_op jit(solution)/shard_map/ppermute | solution.py:35
  101.4 3.4 %collective-permute-start.4 = (bf16[32,2048]{1,0:T(8,128)(2,1)S(1)}, bf16[32,2048]{1,0:T(8,128)(2,1)S(1)}, u32[]{:S(2)}, u32[]{:S(2)}) collective-permute-start(bf16[32,2048]{1,0:T(8,128)(2,1)S(1)} %get-tuple-element.43), channel_id=1, source_target_pairs={{0,30},{1,31},{2,0},{3,1},{4,2},{5,3},{6,4},{7,5},{8,6},{9,7},{10,... | collective-permute-start | bytes 393224 | tf_op jit(solution)/shard_map/ppermute | solution.py:35
  104.8 3.1 %collective-permute-start.5 = (bf16[32,2048]{1,0:T(8,128)(2,1)S(1)}, bf16[32,2048]{1,0:T(8,128)(2,1)S(1)}, u32[]{:S(2)}, u32[]{:S(2)}) collective-permute-start(bf16[32,2048]{1,0:T(8,128)(2,1)S(1)} %get-tuple-element.44), channel_id=1, source_target_pairs={{0,1},{1,2},{2,3},{3,4},{4,5},{5,6},{6,7},{7,8},{8,9},{9,10},{10,1... | collective-permute-start | bytes 393224 | tf_op jit(solution)/shard_map/ppermute | solution.py:35
  107.9 3.4 %collective-permute-start.6 = (bf16[32,2048]{1,0:T(8,128)(2,1)S(1)}, bf16[32,2048]{1,0:T(8,128)(2,1)S(1)}, u32[]{:S(2)}, u32[]{:S(2)}) collective-permute-start(bf16[32,2048]{1,0:T(8,128)(2,1)S(1)} %get-tuple-element.38), channel_id=1, source_target_pairs={{0,31},{1,0},{2,1},{3,2},{4,3},{5,4},{6,5},{7,6},{8,7},{9,8},{10,9... | collective-permute-start | bytes 393224 | tf_op jit(solution)/shard_map/ppermute | solution.py:35
  111.4 0.7 collective-permute-done.3
  112.1 1.7 collective-permute-done.4
  113.9 1.1 collective-permute-done.6
  115.0 5.3 %collective-permute-start.7 = (bf16[256,2048]{1,0:T(8,128)(2,1)S(1)}, bf16[256,2048]{1,0:T(8,128)(2,1)S(1)}, u32[]{:S(2)}, u32[]{:S(2)}) collective-permute-start(bf16[256,2048]{1,0:T(8,128)(2,1)S(1)} %fusion.62), channel_id=1, source_target_pairs={{0,32},{32,0},{64,96},{96,64},{128,160},{160,128},{192,224},{224,1... | collective-permute-start | bytes 3145736 | tf_op jit(solution)/shard_map/ppermute | solution.py:50
  120.3 2.3 collective-permute-done.7
  123.3 0.8 copy-done
  124.8 0.9 copy-done.1
  127.4 1.1 pad_maximum_fusion.1
  128.5 2.3 collective-permute-start.8
  132.1 1.2 fusion.25
  133.4 1.8 multiply_reduce_fusion
  135.2 0.7 broadcast_in_dim.139
  136.0 0.9 fusion.42
  136.9 1.4 add_convert_fusion
  138.5 4.6 %collective-permute-start.9 = (bf16[32,2048]{1,0:T(8,128)(2,1)S(1)}, bf16[32,2048]{1,0:T(8,128)(2,1)S(1)}, u32[]{:S(2)}, u32[]{:S(2)}) collective-permute-start(bf16[32,2048]{1,0:T(8,128)(2,1)S(1)} %get-tuple-element.37), channel_id=1, source_target_pairs={{0,28},{1,29},{2,30},{3,31},{4,0},{5,1},{6,2},{7,3},{8,4},{9,5},{1... | collective-permute-start | bytes 393224 | tf_op jit(solution)/shard_map/ppermute | solution.py:47
  143.2 2.7 %collective-permute-start.10 = (bf16[32,2048]{1,0:T(8,128)(2,1)S(1)}, bf16[32,2048]{1,0:T(8,128)(2,1)S(1)}, u32[]{:S(2)}, u32[]{:S(2)}) collective-permute-start(bf16[32,2048]{1,0:T(8,128)(2,1)S(1)} %get-tuple-element.36), channel_id=1, source_target_pairs={{0,29},{1,30},{2,31},{3,0},{4,1},{5,2},{6,3},{7,4},{8,5},{9,6},{10... | collective-permute-start | bytes 393224 | tf_op jit(solution)/shard_map/ppermute | solution.py:35
  145.8 4.4 %collective-permute-start.11 = (bf16[32,2048]{1,0:T(8,128)(2,1)S(1)}, bf16[32,2048]{1,0:T(8,128)(2,1)S(1)}, u32[]{:S(2)}, u32[]{:S(2)}) collective-permute-start(bf16[32,2048]{1,0:T(8,128)(2,1)S(1)} %get-tuple-element.35), channel_id=1, source_target_pairs={{0,3},{1,4},{2,5},{3,6},{4,7},{5,8},{6,9},{7,10},{8,11},{9,12},{10... | collective-permute-start | bytes 393224 | tf_op jit(solution)/shard_map/ppermute | solution.py:35
  150.3 4.4 %collective-permute-start.12 = (bf16[32,2048]{1,0:T(8,128)(2,1)S(1)}, bf16[32,2048]{1,0:T(8,128)(2,1)S(1)}, u32[]{:S(2)}, u32[]{:S(2)}) collective-permute-start(bf16[32,2048]{1,0:T(8,128)(2,1)S(1)} %get-tuple-element.34), channel_id=1, source_target_pairs={{0,30},{1,31},{2,0},{3,1},{4,2},{5,3},{6,4},{7,5},{8,6},{9,7},{10,... | collective-permute-start | bytes 393224 | tf_op jit(solution)/shard_map/ppermute | solution.py:35
  154.7 1.9 collective-permute-start.13
  156.6 6.4 %collective-permute-start.14 = (bf16[32,2048]{1,0:T(8,128)(2,1)S(1)}, bf16[32,2048]{1,0:T(8,128)(2,1)S(1)}, u32[]{:S(2)}, u32[]{:S(2)}) collective-permute-start(bf16[32,2048]{1,0:T(8,128)(2,1)S(1)} %get-tuple-element.32), channel_id=1, source_target_pairs={{0,31},{1,0},{2,1},{3,2},{4,3},{5,4},{6,5},{7,6},{8,7},{9,8},{10,9... | collective-permute-start | bytes 393224 | tf_op jit(solution)/shard_map/ppermute | solution.py:35
  163.0 1.9 collective-permute-start.15
  165.1 2.1 collective-permute-done.14
  167.2 2.7 %collective-permute-done.15 = bf16[32,2048]{1,0:T(8,128)(2,1)S(1)} collective-permute-done((bf16[32,2048]{1,0:T(8,128)(2,1)S(1)}, bf16[32,2048]{1,0:T(8,128)(2,1)S(1)}, u32[]{:S(2)}, u32[]{:S(2)}) %collective-permute-start.15) | collective-permute-done | bytes 131104 | tf_op jit(solution)/shard_map/ppermute | solution.py:35
  171.2 1.1 maximum_bitcast_fusion
  172.3 8.5 %all-to-all-start.1 = ((bf16[32,8,2176]{2,1,0:T(8,128)(2,1)}), bf16[32,8,2176]{2,1,0:T(8,128)(2,1)S(1)}, u32[]{:S(2)}, u32[]{:S(2)}) async-start(bf16[32,8,2176]{2,1,0:T(8,128)(2,1)} %maximum_bitcast_fusion), calls=%async_computation.1 | async-start | bytes 2228224 | tf_op jit(solution)/shard_map/all_to_all | solution.py:158
  180.8 0.7 fusion.111
  190.2 8.2 %all-to-all-done.1 = bf16[32,8,2176]{2,1,0:T(8,128)(2,1)S(1)} async-done(((bf16[32,8,2176]{2,1,0:T(8,128)(2,1)}), bf16[32,8,2176]{2,1,0:T(8,128)(2,1)S(1)}, u32[]{:S(2)}, u32[]{:S(2)}) %all-to-all-start.1) | async-done | bytes 1114144 | tf_op jit(solution)/shard_map/all_to_all | solution.py:158
  199.0 5.9 %collective-permute-start.16 = (bf16[8,4224]{1,0:T(8,128)(2,1)S(1)}, bf16[8,4224]{1,0:T(8,128)(2,1)S(1)}, u32[]{:S(2)}, u32[]{:S(2)}) collective-permute-start(bf16[8,4224]{1,0:T(8,128)(2,1)S(1)} %get-tuple-element.48), channel_id=1, source_target_pairs={{0,8},{1,9},{2,10},{3,11},{4,12},{5,13},{6,14},{7,15},{8,16},{9,17... | collective-permute-start | bytes 202760 | tf_op jit(solution)/shard_map/ppermute | solution.py:35
  204.9 11.8 %collective-permute-start.17 = (bf16[8,4224]{1,0:T(8,128)(2,1)S(1)}, bf16[8,4224]{1,0:T(8,128)(2,1)S(1)}, u32[]{:S(2)}, u32[]{:S(2)}) collective-permute-start(bf16[8,4224]{1,0:T(8,128)(2,1)S(1)} %get-tuple-element.50), channel_id=1, source_target_pairs={{0,16},{1,17},{2,18},{3,19},{4,20},{5,21},{6,22},{7,23},{8,24},{9,... | collective-permute-start | bytes 202760 | tf_op jit(solution)/shard_map/ppermute | solution.py:35
  216.7 8.1 %collective-permute-start.18 = (bf16[8,4224]{1,0:T(8,128)(2,1)S(1)}, bf16[8,4224]{1,0:T(8,128)(2,1)S(1)}, u32[]{:S(2)}, u32[]{:S(2)}) collective-permute-start(bf16[8,4224]{1,0:T(8,128)(2,1)S(1)} %get-tuple-element.49), channel_id=1, source_target_pairs={{0,24},{1,25},{2,26},{3,27},{4,28},{5,29},{6,30},{7,31},{8,0},{9,1... | collective-permute-start | bytes 202760 | tf_op jit(solution)/shard_map/ppermute | solution.py:35
  224.8 5.3 %collective-permute-done.17 = bf16[8,4224]{1,0:T(8,128)(2,1)S(1)} collective-permute-done((bf16[8,4224]{1,0:T(8,128)(2,1)S(1)}, bf16[8,4224]{1,0:T(8,128)(2,1)S(1)}, u32[]{:S(2)}, u32[]{:S(2)}) %collective-permute-start.17) | collective-permute-done | bytes 67616 | tf_op jit(solution)/shard_map/ppermute | solution.py:35
  230.1 13.7 %collective-permute-done.18 = bf16[8,4224]{1,0:T(8,128)(2,1)S(1)} collective-permute-done((bf16[8,4224]{1,0:T(8,128)(2,1)S(1)}, bf16[8,4224]{1,0:T(8,128)(2,1)S(1)}, u32[]{:S(2)}, u32[]{:S(2)}) %collective-permute-start.18) | collective-permute-done | bytes 67616 | tf_op jit(solution)/shard_map/ppermute | solution.py:35
  (131 shorter events, 10.8 us)
Async XLA Ops:
  57.3 10.8 %copy-start.15 = (s32[8]{0:T(128)S(1)}, s32[8]{0:T(128)}, u32[]{:S(2)}) copy-start(s32[8]{0:T(128)} %constant.194.clone) | copy-start | bytes 100
  57.3 28.4 %all-to-all-start = ((bf16[32,8,2176]{2,1,0:T(8,128)(2,1)}), bf16[32,8,2176]{2,1,0:T(8,128)(2,1)S(1)}, u32[]{:S(2)}, u32[]{:S(2)}) async-start(bf16[32,8,2176]{2,1,0:T(8,128)(2,1)} %bitcast.17), calls=%async_computation | async-start | bytes 2228224 | tf_op jit(solution)/shard_map/all_to_all | solution.py:82
  68.1 18.1 %copy-start.12 = (bf16[8]{0:T(256)(128)(2,1)}, bf16[8]{0:T(256)(128)(2,1)S(1)}, u32[]{:S(2)}) copy-start(bf16[8]{0:T(256)(128)(2,1)S(1)} %fusion.95) | copy-start | bytes 52
  68.2 18.2 %copy-start.10 = (pred[4,256]{1,0:T(4,128)(4,1)}, pred[4,256]{1,0:T(4,128)(4,1)S(1)}, u32[]{:S(2)}) copy-start(pred[4,256]{1,0:T(4,128)(4,1)S(1)} %iota_compare_fusion.6) | copy-start | bytes 3076
  85.8 1.2 copy-start.4
  85.9 0.9 copy-start.6
  87.1 17.6 %collective-permute-start = (bf16[32,2048]{1,0:T(8,128)(2,1)S(1)}, bf16[32,2048]{1,0:T(8,128)(2,1)S(1)}, u32[]{:S(2)}, u32[]{:S(2)}) collective-permute-start(bf16[32,2048]{1,0:T(8,128)(2,1)S(1)} %get-tuple-element.39), channel_id=1, source_target_pairs={{0,4},{1,5},{2,6},{3,7},{4,8},{5,9},{6,10},{7,11},{8,12},{9,13},{1... | collective-permute-start | bytes 393224 | tf_op jit(solution)/shard_map/ppermute | solution.py:47
  89.1 18.9 %collective-permute-start.1 = (bf16[32,2048]{1,0:T(8,128)(2,1)S(1)}, bf16[32,2048]{1,0:T(8,128)(2,1)S(1)}, u32[]{:S(2)}, u32[]{:S(2)}) collective-permute-start(bf16[32,2048]{1,0:T(8,128)(2,1)S(1)} %get-tuple-element.40), channel_id=1, source_target_pairs={{0,3},{1,4},{2,5},{3,6},{4,7},{5,8},{6,9},{7,10},{8,11},{9,12},{10... | collective-permute-start | bytes 393224 | tf_op jit(solution)/shard_map/ppermute | solution.py:35
  92.5 18.8 %collective-permute-start.2 = (bf16[32,2048]{1,0:T(8,128)(2,1)S(1)}, bf16[32,2048]{1,0:T(8,128)(2,1)S(1)}, u32[]{:S(2)}, u32[]{:S(2)}) collective-permute-start(bf16[32,2048]{1,0:T(8,128)(2,1)S(1)} %get-tuple-element.41), channel_id=1, source_target_pairs={{0,29},{1,30},{2,31},{3,0},{4,1},{5,2},{6,3},{7,4},{8,5},{9,6},{10... | collective-permute-start | bytes 393224 | tf_op jit(solution)/shard_map/ppermute | solution.py:35
  97.4 14.8 %collective-permute-start.3 = (bf16[32,2048]{1,0:T(8,128)(2,1)S(1)}, bf16[32,2048]{1,0:T(8,128)(2,1)S(1)}, u32[]{:S(2)}, u32[]{:S(2)}) collective-permute-start(bf16[32,2048]{1,0:T(8,128)(2,1)S(1)} %get-tuple-element.42), channel_id=1, source_target_pairs={{0,2},{1,3},{2,4},{3,5},{4,6},{5,7},{6,8},{7,9},{8,10},{9,11},{10,... | collective-permute-start | bytes 393224 | tf_op jit(solution)/shard_map/ppermute | solution.py:35
  101.4 12.5 %collective-permute-start.4 = (bf16[32,2048]{1,0:T(8,128)(2,1)S(1)}, bf16[32,2048]{1,0:T(8,128)(2,1)S(1)}, u32[]{:S(2)}, u32[]{:S(2)}) collective-permute-start(bf16[32,2048]{1,0:T(8,128)(2,1)S(1)} %get-tuple-element.43), channel_id=1, source_target_pairs={{0,30},{1,31},{2,0},{3,1},{4,2},{5,3},{6,4},{7,5},{8,6},{9,7},{10,... | collective-permute-start | bytes 393224 | tf_op jit(solution)/shard_map/ppermute | solution.py:35
  104.8 9.1 %collective-permute-start.5 = (bf16[32,2048]{1,0:T(8,128)(2,1)S(1)}, bf16[32,2048]{1,0:T(8,128)(2,1)S(1)}, u32[]{:S(2)}, u32[]{:S(2)}) collective-permute-start(bf16[32,2048]{1,0:T(8,128)(2,1)S(1)} %get-tuple-element.44), channel_id=1, source_target_pairs={{0,1},{1,2},{2,3},{3,4},{4,5},{5,6},{6,7},{7,8},{8,9},{9,10},{10,1... | collective-permute-start | bytes 393224 | tf_op jit(solution)/shard_map/ppermute | solution.py:35
  107.9 7.1 %collective-permute-start.6 = (bf16[32,2048]{1,0:T(8,128)(2,1)S(1)}, bf16[32,2048]{1,0:T(8,128)(2,1)S(1)}, u32[]{:S(2)}, u32[]{:S(2)}) collective-permute-start(bf16[32,2048]{1,0:T(8,128)(2,1)S(1)} %get-tuple-element.38), channel_id=1, source_target_pairs={{0,31},{1,0},{2,1},{3,2},{4,3},{5,4},{6,5},{7,6},{8,7},{9,8},{10,9... | collective-permute-start | bytes 393224 | tf_op jit(solution)/shard_map/ppermute | solution.py:35
  111.4 11.2 %copy-start.14 = (bf16[1,1,256,2048]{3,2,1,0:T(8,128)(2,1)S(1)}, bf16[1,1,256,2048]{3,2,1,0:T(8,128)(2,1)}, u32[]{:S(2)}) copy-start(bf16[1,1,256,2048]{3,2,1,0:T(8,128)(2,1)} %param.20) | copy-start | bytes 3145732
  115.0 11.0 %copy-start.8 = (bf16[256,2048]{1,0:T(8,128)(2,1)}, bf16[256,2048]{1,0:T(8,128)(2,1)S(1)}, u32[]{:S(2)}) copy-start(bf16[256,2048]{1,0:T(8,128)(2,1)S(1)} %fusion.62) | copy-start | bytes 3145732
  115.0 7.6 %collective-permute-start.7 = (bf16[256,2048]{1,0:T(8,128)(2,1)S(1)}, bf16[256,2048]{1,0:T(8,128)(2,1)S(1)}, u32[]{:S(2)}, u32[]{:S(2)}) collective-permute-start(bf16[256,2048]{1,0:T(8,128)(2,1)S(1)} %fusion.62), channel_id=1, source_target_pairs={{0,32},{32,0},{64,96},{96,64},{128,160},{160,128},{192,224},{224,1... | collective-permute-start | bytes 3145736 | tf_op jit(solution)/shard_map/ppermute | solution.py:50
  122.9 1.2 copy-start
  124.5 1.2 copy-start.1
  126.4 0.7 copy-start.2
  126.4 0.7 copy-start.16
  128.5 4.9 %collective-permute-start.8 = (bf16[256,2048]{1,0:T(8,128)(2,1)}, bf16[256,2048]{1,0:T(8,128)(2,1)}, u32[]{:S(2)}, u32[]{:S(2)}) collective-permute-start(bf16[256,2048]{1,0:T(8,128)(2,1)} %pad_maximum_fusion.1), channel_id=1, source_target_pairs={{0,32},{32,0},{64,96},{96,64},{128,160},{160,128},{192,224},{224,1... | collective-permute-start | bytes 3145736 | tf_op jit(solution)/shard_map/ppermute | solution.py:50
  131.5 1.9 copy-start.9
  138.5 18.1 %collective-permute-start.9 = (bf16[32,2048]{1,0:T(8,128)(2,1)S(1)}, bf16[32,2048]{1,0:T(8,128)(2,1)S(1)}, u32[]{:S(2)}, u32[]{:S(2)}) collective-permute-start(bf16[32,2048]{1,0:T(8,128)(2,1)S(1)} %get-tuple-element.37), channel_id=1, source_target_pairs={{0,28},{1,29},{2,30},{3,31},{4,0},{5,1},{6,2},{7,3},{8,4},{9,5},{1... | collective-permute-start | bytes 393224 | tf_op jit(solution)/shard_map/ppermute | solution.py:47
  143.2 19.9 %collective-permute-start.10 = (bf16[32,2048]{1,0:T(8,128)(2,1)S(1)}, bf16[32,2048]{1,0:T(8,128)(2,1)S(1)}, u32[]{:S(2)}, u32[]{:S(2)}) collective-permute-start(bf16[32,2048]{1,0:T(8,128)(2,1)S(1)} %get-tuple-element.36), channel_id=1, source_target_pairs={{0,29},{1,30},{2,31},{3,0},{4,1},{5,2},{6,3},{7,4},{8,5},{9,6},{10... | collective-permute-start | bytes 393224 | tf_op jit(solution)/shard_map/ppermute | solution.py:35
  145.8 19.2 %collective-permute-start.11 = (bf16[32,2048]{1,0:T(8,128)(2,1)S(1)}, bf16[32,2048]{1,0:T(8,128)(2,1)S(1)}, u32[]{:S(2)}, u32[]{:S(2)}) collective-permute-start(bf16[32,2048]{1,0:T(8,128)(2,1)S(1)} %get-tuple-element.35), channel_id=1, source_target_pairs={{0,3},{1,4},{2,5},{3,6},{4,7},{5,8},{6,9},{7,10},{8,11},{9,12},{10... | collective-permute-start | bytes 393224 | tf_op jit(solution)/shard_map/ppermute | solution.py:35
  150.3 14.8 %collective-permute-start.12 = (bf16[32,2048]{1,0:T(8,128)(2,1)S(1)}, bf16[32,2048]{1,0:T(8,128)(2,1)S(1)}, u32[]{:S(2)}, u32[]{:S(2)}) collective-permute-start(bf16[32,2048]{1,0:T(8,128)(2,1)S(1)} %get-tuple-element.34), channel_id=1, source_target_pairs={{0,30},{1,31},{2,0},{3,1},{4,2},{5,3},{6,4},{7,5},{8,6},{9,7},{10,... | collective-permute-start | bytes 393224 | tf_op jit(solution)/shard_map/ppermute | solution.py:35
  154.7 10.3 %collective-permute-start.13 = (bf16[32,2048]{1,0:T(8,128)(2,1)S(1)}, bf16[32,2048]{1,0:T(8,128)(2,1)S(1)}, u32[]{:S(2)}, u32[]{:S(2)}) collective-permute-start(bf16[32,2048]{1,0:T(8,128)(2,1)S(1)} %get-tuple-element.33), channel_id=1, source_target_pairs={{0,2},{1,3},{2,4},{3,5},{4,6},{5,7},{6,8},{7,9},{8,10},{9,11},{10,... | collective-permute-start | bytes 393224 | tf_op jit(solution)/shard_map/ppermute | solution.py:35
  156.6 10.6 %collective-permute-start.14 = (bf16[32,2048]{1,0:T(8,128)(2,1)S(1)}, bf16[32,2048]{1,0:T(8,128)(2,1)S(1)}, u32[]{:S(2)}, u32[]{:S(2)}) collective-permute-start(bf16[32,2048]{1,0:T(8,128)(2,1)S(1)} %get-tuple-element.32), channel_id=1, source_target_pairs={{0,31},{1,0},{2,1},{3,2},{4,3},{5,4},{6,5},{7,6},{8,7},{9,8},{10,9... | collective-permute-start | bytes 393224 | tf_op jit(solution)/shard_map/ppermute | solution.py:35
  163.0 6.9 %collective-permute-start.15 = (bf16[32,2048]{1,0:T(8,128)(2,1)S(1)}, bf16[32,2048]{1,0:T(8,128)(2,1)S(1)}, u32[]{:S(2)}, u32[]{:S(2)}) collective-permute-start(bf16[32,2048]{1,0:T(8,128)(2,1)S(1)} %get-tuple-element.31), channel_id=1, source_target_pairs={{0,1},{1,2},{2,3},{3,4},{4,5},{5,6},{6,7},{7,8},{8,9},{9,10},{10,1... | collective-permute-start | bytes 393224 | tf_op jit(solution)/shard_map/ppermute | solution.py:35
  170.0 0.8 copy-start.11
  170.0 0.9 copy-start.5
  170.0 0.9 copy-start.7
  170.0 0.9 copy-start.13
  172.3 17.1 %copy-start.3 = (bf16[16,4,2,32]{3,2,1,0:T(2,128)(2,1)S(1)}, bf16[16,4,2,32]{3,2,1,0:T(2,128)(2,1)}, u32[]{:S(2)}) copy-start(bf16[16,4,2,32]{3,2,1,0:T(2,128)(2,1)} %get-tuple-element.29) | copy-start | bytes 24580
  172.3 26.1 %all-to-all-start.1 = ((bf16[32,8,2176]{2,1,0:T(8,128)(2,1)}), bf16[32,8,2176]{2,1,0:T(8,128)(2,1)S(1)}, u32[]{:S(2)}, u32[]{:S(2)}) async-start(bf16[32,8,2176]{2,1,0:T(8,128)(2,1)} %maximum_bitcast_fusion), calls=%async_computation.1 | async-start | bytes 2228224 | tf_op jit(solution)/shard_map/all_to_all | solution.py:158
  199.0 25.9 %collective-permute-start.16 = (bf16[8,4224]{1,0:T(8,128)(2,1)S(1)}, bf16[8,4224]{1,0:T(8,128)(2,1)S(1)}, u32[]{:S(2)}, u32[]{:S(2)}) collective-permute-start(bf16[8,4224]{1,0:T(8,128)(2,1)S(1)} %get-tuple-element.48), channel_id=1, source_target_pairs={{0,8},{1,9},{2,10},{3,11},{4,12},{5,13},{6,14},{7,15},{8,16},{9,17... | collective-permute-start | bytes 202760 | tf_op jit(solution)/shard_map/ppermute | solution.py:35
  204.9 25.2 %collective-permute-start.17 = (bf16[8,4224]{1,0:T(8,128)(2,1)S(1)}, bf16[8,4224]{1,0:T(8,128)(2,1)S(1)}, u32[]{:S(2)}, u32[]{:S(2)}) collective-permute-start(bf16[8,4224]{1,0:T(8,128)(2,1)S(1)} %get-tuple-element.50), channel_id=1, source_target_pairs={{0,16},{1,17},{2,18},{3,19},{4,20},{5,21},{6,22},{7,23},{8,24},{9,... | collective-permute-start | bytes 202760 | tf_op jit(solution)/shard_map/ppermute | solution.py:35
  216.7 27.2 %collective-permute-start.18 = (bf16[8,4224]{1,0:T(8,128)(2,1)S(1)}, bf16[8,4224]{1,0:T(8,128)(2,1)S(1)}, u32[]{:S(2)}, u32[]{:S(2)}) collective-permute-start(bf16[8,4224]{1,0:T(8,128)(2,1)S(1)} %get-tuple-element.49), channel_id=1, source_target_pairs={{0,24},{1,25},{2,26},{3,27},{4,28},{5,29},{6,30},{7,31},{8,0},{9,1... | collective-permute-start | bytes 202760 | tf_op jit(solution)/shard_map/ppermute | solution.py:35

commit v3 on v2

--- a/solution.py
+++ b/solution.py
@@ -1,6 +1,10 @@
+import functools
+
 import jax
 import jax.numpy as jnp
 from jax import lax
+from jax.experimental import pallas as pl
+from jax.experimental.pallas import tpu as pltpu
 from jax.sharding import PartitionSpec as P
 
 BF = jnp.bfloat16
@@ -10,6 +14,99 @@
 
 def dot(a, b, dims):
     return lax.dot_general(a, b, (dims, ((), ())), preferred_element_type=F32)
+
+
+def whole(kernel, outs, flops, *args, scalars=0):
+    vmem = pl.BlockSpec(memory_space=pltpu.VMEM)
+    smem = pl.BlockSpec(memory_space=pltpu.SMEM)
+    moved = sum(a.size * a.dtype.itemsize for a in args)
+    return pl.pallas_call(
+        kernel,
+        out_shape=outs,
+        in_specs=[smem] * scalars + [vmem] * (len(args) - scalars),
+        out_specs=jax.tree.map(lambda _: vmem, outs),
+        compiler_params=pltpu.CompilerParams(vmem_limit_bytes=24 * 1024 * 1024),
+        cost_estimate=pl.CostEstimate(flops=flops, bytes_accessed=moved, transcendentals=0),
+    )(*args)
+
+
+def pack_kernel(n_local, groups, x_ref, dy_ref, gate_ref, group_ref, expert_ref, own_ref):
+    tok, width = x_ref.shape
+    topk = expert_ref.shape[1]
+    member = jnp.zeros((tok, groups), F32)
+    iota = lax.broadcasted_iota(jnp.int32, (tok, groups), 1)
+    for n in range(group_ref.shape[1]):
+        member = jnp.where(group_ref[:, n : n + 1] == iota, 1.0, member)
+    lower = lax.broadcasted_iota(jnp.int32, (tok, tok), 1) < lax.broadcasted_iota(jnp.int32, (tok, tok), 0)
+    placed = dot(jnp.where(lower, 1.0, 0.0).astype(BF), member.astype(BF), ((1,), (0,)))
+    code = jnp.where(member > 0, placed, -1.0)
+    ids = expert_ref[...]
+    shift = n_local.bit_length() - 1
+    pieces = (
+        lax.shift_right_logical(ids, shift).astype(F32).astype(BF),
+        (ids & (n_local - 1)).astype(F32).astype(BF),
+        gate_ref[...],
+        code.astype(BF),
+    )
+    meta = jnp.zeros((tok, META), F32)
+    start = 0
+    for piece in pieces:
+        n = piece.shape[1]
+        spot = lax.broadcasted_iota(jnp.int32, (n, META), 1) == lax.broadcasted_iota(jnp.int32, (n, META), 0) + start
+        meta = meta + dot(piece, jnp.where(spot, 1.0, 0.0).astype(BF), ((1,), (0,)))
+        start += n
+    own_ref[:, :width] = x_ref[...]
+    own_ref[:, width : 2 * width] = dy_ref[...]
+    own_ref[:, 2 * width :] = meta.astype(BF)
+
+
+def halves_of(core_ref, half):
+    own = pl.multiple_of(core_ref[0] * half, half)
+    other = pl.multiple_of((1 - core_ref[0]) * half, half)
+    return pl.ds(own, half), pl.ds(other, half)
+
+
+def expert_kernel(core_ref, mine, other, w_in, w_lin, w_out, hidden_ref, pre_ref, lin_ref, give_ref):
+    half = mine.shape[1] // 2
+    own, far = halves_of(core_ref, half)
+    mine_x, other_x = mine[:, :half], other[:, :half]
+    pre_gate = dot(mine_x, w_in[own, :], ((1,), (0,))) + dot(other_x, w_in[far, :], ((1,), (0,)))
+    pre_up = dot(mine_x, w_lin[own, :], ((1,), (0,))) + dot(other_x, w_lin[far, :], ((1,), (0,)))
+    sigmoid = jax.nn.sigmoid(pre_gate)
+    active = pre_gate * sigmoid
+    hidden = (active * pre_up).astype(BF)
+    hidden_ref[...] = hidden
+    grad_hidden = dot(mine[:, half:], w_out[:, own], ((1,), (1,))) + dot(other[:, half:], w_out[:, far], ((1,), (1,)))
+    grad_pre = (grad_hidden * pre_up * sigmoid * (1.0 + pre_gate * (1.0 - sigmoid))).astype(BF)
+    grad_lin = (grad_hidden * active).astype(BF)
+    pre_ref[...] = grad_pre
+    lin_ref[...] = grad_lin
+    give_ref[:, :half] = dot(hidden, w_out[:, far], ((1,), (0,))).astype(BF)
+    back = dot(grad_pre, w_in[far, :], ((1,), (1,))) + dot(grad_lin, w_lin[far, :], ((1,), (1,)))
+    give_ref[:, half:] = back.astype(BF)
+
+
+def keep_kernel(core_ref, hidden, grad_pre, grad_lin, w_in, w_lin, w_out, keep_ref):
+    half = w_in.shape[0] // 2
+    own, _ = halves_of(core_ref, half)
+    keep_ref[:, :half] = dot(hidden[...], w_out[:, own], ((1,), (0,)))
+    back = dot(grad_pre[...], w_in[own, :], ((1,), (1,))) + dot(grad_lin[...], w_lin[own, :], ((1,), (1,)))
+    keep_ref[:, half:] = back
+
+
+def merge_kernel(pad, keep, gave, mine, ret_ref):
+    n_slots, width = mine.shape
+    half = width // 2
+    sum_out = keep[:, :half] + gave[:, :half].astype(F32)
+    term = jnp.sum(mine[:, half:].astype(F32) * sum_out, axis=1, keepdims=True)
+    row = lax.broadcasted_iota(jnp.int32, (n_slots, META), 0) & (pad - 1)
+    lane = lax.broadcasted_iota(jnp.int32, (n_slots, META), 1)
+    spots = jnp.where(lane == row, jnp.broadcast_to(term, (n_slots, META)), 0.0)
+    spare = jnp.sum(spots.reshape(n_slots // pad, pad, META), axis=1, keepdims=True)
+    spare = jnp.broadcast_to(spare, (n_slots // pad, pad, META)).reshape(n_slots, META)
+    ret_ref[:, :half] = sum_out.astype(BF)
+    ret_ref[:, :META] = jnp.where(row == pad - 1, spare, sum_out[:, :META]).astype(BF)
+    ret_ref[:, half:] = (keep[:, half:] + gave[:, half:].astype(F32)).astype(BF)
 
 
 def body(tokens, grad_mixed, gates, group_ids, expert_ids, w_gate, w_up, w_down):
@@ -49,18 +146,16 @@
     def swap(array):
         return lax.ppermute(array, "group", [(i, i ^ 1) for i in range(n_group)])
 
-    group_iota = jnp.arange(groups, dtype=jnp.int32)[None, :]
-    member = jnp.zeros((tok, groups), F32)
-    for n in range(named):
-        member = jnp.maximum(member, (group_ids[:, n : n + 1] == group_iota).astype(F32))
-    order = jnp.arange(tok, dtype=jnp.int32)
-    placed = dot((order[None, :] < order[:, None]).astype(BF), member.astype(BF), ((1,), (0,)))
-    code = jnp.where(member > 0, placed, -1.0)
-    meta = jnp.concatenate(
-        [(expert_ids // n_local).astype(BF), (expert_ids % n_local).astype(BF), gates, code.astype(BF)], axis=1
-    )
-    meta = jnp.pad(meta, ((0, 0), (0, META - meta.shape[1])))
-    own = jnp.concatenate([tokens, grad_mixed, meta], axis=1)
+    own = whole(
+        functools.partial(pack_kernel, n_local, groups),
+        jax.ShapeDtypeStruct((tok, 2 * width + META), BF),
+        4 * tok * META * topk,
+        tokens,
+        grad_mixed,
+        gates,
+        group_ids,
+        expert_ids,
+    )
     rows = lax.all_gather(
         own, "local", axis=0, tiled=True, axis_index_groups=[[b + near * f for f in range(far)] for b in range(near)]
     )
@@ -111,38 +206,31 @@
         [hop(slots[i], s, 1) for i, s in enumerate(steps)], axis=0
     )
 
-    def own_first(array, axis):
-        low = lax.slice_in_dim(array, 0, half, axis=axis)
-        high = lax.slice_in_dim(array, half, width, axis=axis)
-        return jnp.where(core == 0, low, high), jnp.where(core == 0, high, low)
-
-    in_own, in_other = own_first(w_gate[0, 0], 0)
-    lin_own, lin_other = own_first(w_up[0, 0], 0)
-    out_own, out_other = own_first(w_down[0, 0], 1)
     other = swap(mine)
-    pre_gate = dot(mine[:, :half], in_own, ((1,), (0,))) + dot(other[:, :half], in_other, ((1,), (0,)))
-    pre_up = dot(mine[:, :half], lin_own, ((1,), (0,))) + dot(other[:, :half], lin_other, ((1,), (0,)))
-    sigmoid = jax.nn.sigmoid(pre_gate)
-    active = pre_gate * sigmoid
-    hidden = (active * pre_up).astype(BF)
-    grad_hidden = dot(mine[:, half:], out_own, ((1,), (1,))) + dot(other[:, half:], out_other, ((1,), (1,)))
-    grad_pre = (grad_hidden * pre_up * sigmoid * (1.0 + pre_gate * (1.0 - sigmoid))).astype(BF)
-    grad_lin = (grad_hidden * active).astype(BF)
-
-    give_out = dot(hidden, out_other, ((1,), (0,))).astype(BF)
-    give_back = (dot(grad_pre, in_other, ((1,), (1,))) + dot(grad_lin, lin_other, ((1,), (1,)))).astype(BF)
-    gave = swap(jnp.concatenate([give_out, give_back], axis=1))
-    sum_out = dot(hidden, out_own, ((1,), (0,))) + gave[:, :half].astype(F32)
-    sum_back = (
-        dot(grad_pre, in_own, ((1,), (1,))) + dot(grad_lin, lin_own, ((1,), (1,))) + gave[:, half:].astype(F32)
-    )
-    term = jnp.sum(mine[:, half:].astype(F32) * sum_out, axis=1, keepdims=True)
-    spots = (jnp.arange(META, dtype=jnp.int32)[None, :] == jnp.arange(n_slots, dtype=jnp.int32)[:, None] % pad)
-    spare = jnp.sum(jnp.where(spots, term, 0.0).reshape(near * far, pad, META), axis=1, keepdims=True)
-    spare = jnp.where((jnp.arange(pad) == pad - 1)[None, :, None], spare, sum_out[:, :META].reshape(near * far, pad, META))
-    ret = jnp.concatenate(
-        [spare.reshape(n_slots, META).astype(BF), sum_out[:, META:].astype(BF), sum_back.astype(BF)], axis=1
-    ).reshape(near, far * pad, width)
+    which = core.reshape(1)
+    weights = (w_gate[0, 0], w_up[0, 0], w_down[0, 0])
+    hid = w_up.shape[3]
+    narrow = jax.ShapeDtypeStruct((n_slots, hid), BF)
+    wide = jax.ShapeDtypeStruct((n_slots, width), BF)
+    products = 2 * n_slots * width * hid
+    hidden, grad_pre, grad_lin, give = whole(
+        expert_kernel, (narrow, narrow, narrow, wide), 9 * products // 2, which, mine, other, *weights, scalars=1
+    )
+
+    gave = swap(give)
+    keep = whole(
+        keep_kernel,
+        jax.ShapeDtypeStruct((n_slots, width), F32),
+        3 * products // 2,
+        which,
+        hidden,
+        grad_pre,
+        grad_lin,
+        *weights,
+        scalars=1,
+    )
+    ret = whole(functools.partial(merge_kernel, pad), wide, 4 * n_slots * width, keep, gave, mine)
+    ret = ret.reshape(near, far * pad, width)
     ret = jnp.concatenate(
         [hop(ret[i], s, -1) for i, s in enumerate(steps)], axis=0
     )
@@ -169,8 +257,15 @@
         axis=1,
     ).reshape(far, tok, 2 * width + META)
     total = full[0]
-    for f in range(1, far):
-        total = total + shift(full[f].astype(BF), near * f).astype(F32)
+    if far == 4:
+        up = shift(full[2][:, :width].astype(BF), near).astype(F32)
+        down = shift(full[2][:, width:].astype(BF), -near).astype(F32)
+        above = jnp.concatenate([full[1][:, :width] + up, full[1][:, width:]], axis=1)
+        below = jnp.concatenate([full[3][:, :width], full[3][:, width:] + down], axis=1)
+        total = total + shift(above.astype(BF), near).astype(F32) + shift(below.astype(BF), -near).astype(F32)
+    else:
+        for f in range(1, far):
+            total = total + shift(full[f].astype(BF), near * f).astype(F32)
     return (
         total[:, :width].astype(BF),
         total[:, width : 2 * width].astype(BF),

time: 246 us -> 252 us (1.024)
  waiting for transfers between devices: 55.5 us -> 75.6 us
  matrix products: 10.1 us -> 2.48 us
  other arithmetic: 8.98 us -> 3.52 us
  starting transfers between devices: 103 us -> 99.3 us
  Pallas kernels: 0 us -> 3.34 us
    ppermute x15 -> x16, waiting for transfers between devices: 27.4 us -> 45.7 us  [shift(): lax.ppermute(array, 'local', [(i, (i + by) % n_local) for i in range(n_lo...]
    dot_general x22 -> x9, matrix products: 10.1 us -> 2.48 us  [dot(): return lax.dot_general(a, b, (dims, ((), ())), preferred_element_type=F32)]
    pallas_call x0 -> x4, Pallas kernels: none -> 3.34 us  [whole(): pl.pallas_call(kernel, out_shape=outs, in_specs=[smem] * scalars + [vmem]...]
    concatenate x4 -> x2, other arithmetic: 2.72 us -> 0.02 us  [the longest x1 0.01 us: body(): jnp.concatenate([full[1][:, :width] + up, full[1][:, width:]], axis=1)]
    ppermute x15 -> x16, starting transfers between devices: 69.7 us -> 69.4 us  [shift(): lax.ppermute(array, 'local', [(i, (i + by) % n_local) for i in range(n_lo...]
  transfers between devices with their start and end apart: 21 -> 22, of which waited for: 11 -> 11; matrix products, arithmetic and copies ran while one was open for 2% -> 1% of each run, Pallas kernels for 0% -> 0%
where the time goes in v3:
time: 252 us; the launch traced here: 251 us
  starting transfers between devices  99.3 us (39%)
  waiting for transfers between devices  75.6 us (30%)
  blocking collectives  50.8 us (20%)
  between operations  9.23 us (4%)
  local copies, waits for them, and re-layouts  6.66 us (3%)
  other arithmetic  3.52 us (1%)
  Pallas kernels  3.34 us (1%)
    ppermute x16, starting transfers between devices, shift(): lax.ppermute(array, 'local', [(i, (i + by) % n_local) for i in range(n_lo...  69.4 us
    all_gather x1, blocking collectives, body(): lax.all_gather(own, 'local', axis=0, tiled=True, axis_index_groups=[[b +...  50.8 us
    ppermute x16, waiting for transfers between devices, shift(): lax.ppermute(array, 'local', [(i, (i + by) % n_local) for i in range(n_lo...  45.7 us
    all_to_all x2, waiting for transfers between devices, body(): got = lax.all_to_all(send, 'group', split_axis=0, concat_axis=0, tiled=True)  26 us
    all_to_all x2, starting transfers between devices, body(): got = lax.all_to_all(send, 'group', split_axis=0, concat_axis=0, tiled=True)  17.3 us
    ppermute x2, starting transfers between devices, swap(): return lax.ppermute(array, 'group', [(i, i ^ 1) for i in range(n_group)])  6.85 us
    ppermute x2, starting transfers between devices, hop(): return lax.ppermute(array, ('group', 'local'), pairs)  5.76 us
  transfers between devices with their start and end apart: 22, of which 11 were waited for; matrix products, arithmetic and copies ran while one was open for 1% of the time, Pallas kernels for 0%

profile of v3, /device:TPU:1, one launch (start us, length us, event | category | flops | bytes accessed | tf_op | source)
XLA Modules:
  0.0 251.0 jit_solution(3836547862555632960)
XLA Ops:
  0.6 0.8 copy.87.group_ref
  1.4 0.8 copy-done.3
  2.2 0.8 copy-done.4
  2.9 0.7 copy-done.5
  3.6 0.7 copy-done.6
  4.6 50.8 %all_gather.3 = bf16[32,4224]{1,0:T(8,128)(2,1)S(1)} all-gather(bf16[8,4224]{1,0:T(8,128)(2,1)S(1)} %shard_map.112), channel_id=1, replica_groups={{0,8,16,24},{1,9,17,25},{2,10,18,26},{3,11,19,27},{4,12,20,28},{5,13,21..., dimensions={0}, use_global_device_ids=true | all-gather | bytes 337920 | tf_op jit(solution)/shard_map/all_gather | solution.py:159
  56.3 1.1 pad_maximum_fusion
  57.4 10.7 %all-to-all-start = ((bf16[32,8,2176]{2,1,0:T(8,128)(2,1)}), bf16[32,8,2176]{2,1,0:T(8,128)(2,1)S(1)}, u32[]{:S(2)}, u32[]{:S(2)}) async-start(bf16[32,8,2176]{2,1,0:T(8,128)(2,1)} %bitcast.13), calls=%async_computation | async-start | bytes 2228224 | tf_op jit(solution)/shard_map/all_to_all | solution.py:177
  68.2 17.5 %all-to-all-done = bf16[32,8,2176]{2,1,0:T(8,128)(2,1)S(1)} async-done(((bf16[32,8,2176]{2,1,0:T(8,128)(2,1)}), bf16[32,8,2176]{2,1,0:T(8,128)(2,1)S(1)}, u32[]{:S(2)}, u32[]{:S(2)}) %all-to-all-start) | async-done | bytes 1114144 | tf_op jit(solution)/shard_map/all_to_all | solution.py:177
  87.2 2.1 collective-permute-start
  89.3 1.9 collective-permute-start.6
  91.2 3.4 %collective-permute-start.1 = (bf16[32,2048]{1,0:T(8,128)(2,1)S(1)}, bf16[32,2048]{1,0:T(8,128)(2,1)S(1)}, u32[]{:S(2)}, u32[]{:S(2)}) collective-permute-start(bf16[32,2048]{1,0:T(8,128)(2,1)S(1)} %get-tuple-element.50), channel_id=1, source_target_pairs={{0,3},{1,4},{2,5},{3,6},{4,7},{5,8},{6,9},{7,10},{8,11},{9,12},{10... | collective-permute-start | bytes 393224 | tf_op jit(solution)/shard_map/ppermute | solution.py:132
  94.6 4.9 %collective-permute-start.2 = (bf16[32,2048]{1,0:T(8,128)(2,1)S(1)}, bf16[32,2048]{1,0:T(8,128)(2,1)S(1)}, u32[]{:S(2)}, u32[]{:S(2)}) collective-permute-start(bf16[32,2048]{1,0:T(8,128)(2,1)S(1)} %get-tuple-element.51), channel_id=1, source_target_pairs={{0,29},{1,30},{2,31},{3,0},{4,1},{5,2},{6,3},{7,4},{8,5},{9,6},{10... | collective-permute-start | bytes 393224 | tf_op jit(solution)/shard_map/ppermute | solution.py:132
  99.5 4.3 %collective-permute-start.3 = (bf16[32,2048]{1,0:T(8,128)(2,1)S(1)}, bf16[32,2048]{1,0:T(8,128)(2,1)S(1)}, u32[]{:S(2)}, u32[]{:S(2)}) collective-permute-start(bf16[32,2048]{1,0:T(8,128)(2,1)S(1)} %get-tuple-element.52), channel_id=1, source_target_pairs={{0,2},{1,3},{2,4},{3,5},{4,6},{5,7},{6,8},{7,9},{8,10},{9,11},{10,... | collective-permute-start | bytes 393224 | tf_op jit(solution)/shard_map/ppermute | solution.py:132
  103.8 3.1 %collective-permute-start.4 = (bf16[32,2048]{1,0:T(8,128)(2,1)S(1)}, bf16[32,2048]{1,0:T(8,128)(2,1)S(1)}, u32[]{:S(2)}, u32[]{:S(2)}) collective-permute-start(bf16[32,2048]{1,0:T(8,128)(2,1)S(1)} %get-tuple-element.53), channel_id=1, source_target_pairs={{0,30},{1,31},{2,0},{3,1},{4,2},{5,3},{6,4},{7,5},{8,6},{9,7},{10,... | collective-permute-start | bytes 393224 | tf_op jit(solution)/shard_map/ppermute | solution.py:132
  106.9 1.8 collective-permute-done.1
  108.8 1.9 collective-permute-start.5
  110.8 3.2 %collective-permute-done.3 = bf16[32,2048]{1,0:T(8,128)(2,1)S(1)} collective-permute-done((bf16[32,2048]{1,0:T(8,128)(2,1)S(1)}, bf16[32,2048]{1,0:T(8,128)(2,1)S(1)}, u32[]{:S(2)}, u32[]{:S(2)}) %collective-permute-start.3) | collective-permute-done | bytes 131104 | tf_op jit(solution)/shard_map/ppermute | solution.py:132
  114.0 2.0 collective-permute-done.5
  116.1 4.6 %collective-permute-start.7 = (bf16[256,2048]{1,0:T(8,128)(2,1)S(1)}, bf16[256,2048]{1,0:T(8,128)(2,1)S(1)}, u32[]{:S(2)}, u32[]{:S(2)}) collective-permute-start(bf16[256,2048]{1,0:T(8,128)(2,1)S(1)} %fusion.29.mine), channel_id=1, source_target_pairs={{0,32},{32,0},{64,96},{96,64},{128,160},{160,128},{192,224},{224,1... | collective-permute-start | bytes 3145736 | tf_op jit(solution)/shard_map/ppermute | solution.py:147
  120.7 2.3 collective-permute-done.7.other
  122.9 2.0 shard_map.113
  124.9 2.3 collective-permute-start.8
  127.2 0.6 shard_map.114.keep
  127.8 1.7 collective-permute-done.8.gave
  129.5 0.5 shard_map.115
  130.1 3.7 %collective-permute-start.9 = (bf16[32,2048]{1,0:T(8,128)(2,1)S(1)}, bf16[32,2048]{1,0:T(8,128)(2,1)S(1)}, u32[]{:S(2)}, u32[]{:S(2)}) collective-permute-start(bf16[32,2048]{1,0:T(8,128)(2,1)S(1)} %get-tuple-element.47), channel_id=1, source_target_pairs={{0,28},{1,29},{2,30},{3,31},{4,0},{5,1},{6,2},{7,3},{8,4},{9,5},{1... | collective-permute-start | bytes 393224 | tf_op jit(solution)/shard_map/ppermute | solution.py:144
  133.8 2.5 collective-permute-start.15
  136.3 4.0 %collective-permute-start.14 = (bf16[32,2048]{1,0:T(8,128)(2,1)S(1)}, bf16[32,2048]{1,0:T(8,128)(2,1)S(1)}, u32[]{:S(2)}, u32[]{:S(2)}) collective-permute-start(bf16[32,2048]{1,0:T(8,128)(2,1)S(1)} %get-tuple-element.42), channel_id=1, source_target_pairs={{0,31},{1,0},{2,1},{3,2},{4,3},{5,4},{6,5},{7,6},{8,7},{9,8},{10,9... | collective-permute-start | bytes 393224 | tf_op jit(solution)/shard_map/ppermute | solution.py:132
  140.3 1.9 collective-permute-start.13
  142.2 5.5 %collective-permute-start.12 = (bf16[32,2048]{1,0:T(8,128)(2,1)S(1)}, bf16[32,2048]{1,0:T(8,128)(2,1)S(1)}, u32[]{:S(2)}, u32[]{:S(2)}) collective-permute-start(bf16[32,2048]{1,0:T(8,128)(2,1)S(1)} %get-tuple-element.44), channel_id=1, source_target_pairs={{0,30},{1,31},{2,0},{3,1},{4,2},{5,3},{6,4},{7,5},{8,6},{9,7},{10,... | collective-permute-start | bytes 393224 | tf_op jit(solution)/shard_map/ppermute | solution.py:132
  147.7 3.7 %collective-permute-start.10 = (bf16[32,2048]{1,0:T(8,128)(2,1)S(1)}, bf16[32,2048]{1,0:T(8,128)(2,1)S(1)}, u32[]{:S(2)}, u32[]{:S(2)}) collective-permute-start(bf16[32,2048]{1,0:T(8,128)(2,1)S(1)} %get-tuple-element.46), channel_id=1, source_target_pairs={{0,29},{1,30},{2,31},{3,0},{4,1},{5,2},{6,3},{7,4},{8,5},{9,6},{10... | collective-permute-start | bytes 393224 | tf_op jit(solution)/shard_map/ppermute | solution.py:132
  151.4 9.5 %collective-permute-done.10 = bf16[32,2048]{1,0:T(8,128)(2,1)S(1)} collective-permute-done((bf16[32,2048]{1,0:T(8,128)(2,1)S(1)}, bf16[32,2048]{1,0:T(8,128)(2,1)S(1)}, u32[]{:S(2)}, u32[]{:S(2)}) %collective-permute-start.10) | collective-permute-done | bytes 131104 | tf_op jit(solution)/shard_map/ppermute | solution.py:132
  161.0 4.4 %collective-permute-start.11 = (bf16[32,2048]{1,0:T(8,128)(2,1)S(1)}, bf16[32,2048]{1,0:T(8,128)(2,1)S(1)}, u32[]{:S(2)}, u32[]{:S(2)}) collective-permute-start(bf16[32,2048]{1,0:T(8,128)(2,1)S(1)} %get-tuple-element.45), channel_id=1, source_target_pairs={{0,3},{1,4},{2,5},{3,6},{4,7},{5,8},{6,9},{7,10},{8,11},{9,12},{10... | collective-permute-start | bytes 393224 | tf_op jit(solution)/shard_map/ppermute | solution.py:132
  165.3 7.5 %collective-permute-done.11 = bf16[32,2048]{1,0:T(8,128)(2,1)S(1)} collective-permute-done((bf16[32,2048]{1,0:T(8,128)(2,1)S(1)}, bf16[32,2048]{1,0:T(8,128)(2,1)S(1)}, u32[]{:S(2)}, u32[]{:S(2)}) %collective-permute-start.11) | collective-permute-done | bytes 131104 | tf_op jit(solution)/shard_map/ppermute | solution.py:132
  173.3 0.4 convolution_convert_fusion.4
  174.1 1.1 maximum_bitcast_fusion
  175.2 6.5 %all-to-all-start.1 = ((bf16[32,8,2176]{2,1,0:T(8,128)(2,1)}), bf16[32,8,2176]{2,1,0:T(8,128)(2,1)S(1)}, u32[]{:S(2)}, u32[]{:S(2)}) async-start(bf16[32,8,2176]{2,1,0:T(8,128)(2,1)} %maximum_bitcast_fusion), calls=%async_computation.1 | async-start | bytes 2228224 | tf_op jit(solution)/shard_map/all_to_all | solution.py:246
  181.8 0.6 fusion.58
  190.9 8.4 %all-to-all-done.1 = bf16[32,8,2176]{2,1,0:T(8,128)(2,1)S(1)} async-done(((bf16[32,8,2176]{2,1,0:T(8,128)(2,1)}), bf16[32,8,2176]{2,1,0:T(8,128)(2,1)S(1)}, u32[]{:S(2)}, u32[]{:S(2)}) %all-to-all-start.1) | async-done | bytes 1114144 | tf_op jit(solution)/shard_map/all_to_all | solution.py:246
  200.0 9.1 %collective-permute-start.16 = (bf16[8,2048]{1,0:T(8,128)(2,1)S(1)}, bf16[8,2048]{1,0:T(8,128)(2,1)S(1)}, u32[]{:S(2)}, u32[]{:S(2)}) collective-permute-start(bf16[8,2048]{1,0:T(8,128)(2,1)S(1)} %get-tuple-element.66), channel_id=1, source_target_pairs={{0,8},{1,9},{2,10},{3,11},{4,12},{5,13},{6,14},{7,15},{8,16},{9,17... | collective-permute-start | bytes 98312 | tf_op jit(solution)/shard_map/ppermute | solution.py:132
  209.2 4.9 %collective-permute-start.18 = (bf16[8,2176]{1,0:T(8,128)(2,1)S(1)}, bf16[8,2176]{1,0:T(8,128)(2,1)S(1)}, u32[]{:S(2)}, u32[]{:S(2)}) collective-permute-start(bf16[8,2176]{1,0:T(8,128)(2,1)S(1)} %get-tuple-element.65), channel_id=1, source_target_pairs={{0,24},{1,25},{2,26},{3,27},{4,28},{5,29},{6,30},{7,31},{8,0},{9,1... | collective-permute-start | bytes 104456 | tf_op jit(solution)/shard_map/ppermute | solution.py:132
  214.1 9.1 %collective-permute-start.17 = (bf16[8,4224]{1,0:T(8,128)(2,1)S(1)}, bf16[8,4224]{1,0:T(8,128)(2,1)S(1)}, u32[]{:S(2)}, u32[]{:S(2)}) collective-permute-start(bf16[8,4224]{1,0:T(8,128)(2,1)S(1)} %pad_maximum_fusion.4), channel_id=1, source_target_pairs={{0,8},{1,9},{2,10},{3,11},{4,12},{5,13},{6,14},{7,15},{8,16},{9,17... | collective-permute-start | bytes 202760 | tf_op jit(solution)/shard_map/ppermute | solution.py:132
  223.3 4.9 %collective-permute-start.19 = (bf16[8,4224]{1,0:T(8,128)(2,1)S(1)}, bf16[8,4224]{1,0:T(8,128)(2,1)S(1)}, u32[]{:S(2)}, u32[]{:S(2)}) collective-permute-start(bf16[8,4224]{1,0:T(8,128)(2,1)S(1)} %pad_maximum_fusion.5), channel_id=1, source_target_pairs={{0,24},{1,25},{2,26},{3,27},{4,28},{5,29},{6,30},{7,31},{8,0},{9,1... | collective-permute-start | bytes 202760 | tf_op jit(solution)/shard_map/ppermute | solution.py:132
  228.2 0.6 collective-permute-done.17
  228.8 20.9 %collective-permute-done.19 = bf16[8,4224]{1,0:T(8,128)(2,1)S(1)} collective-permute-done((bf16[8,4224]{1,0:T(8,128)(2,1)S(1)}, bf16[8,4224]{1,0:T(8,128)(2,1)S(1)}, u32[]{:S(2)}, u32[]{:S(2)}) %collective-permute-start.19) | collective-permute-done | bytes 67616 | tf_op jit(solution)/shard_map/ppermute | solution.py:132
  249.7 0.6 fusion.57
  250.4 0.6 slice.332
  (101 shorter events, 5.0 us)
Async XLA Ops:
  1.4 0.8 copy-start.3
  2.2 0.8 copy-start.4
  2.9 0.7 copy-start.5
  3.6 0.7 copy-start.6
  57.4 10.8 %copy-start.7 = (s32[8]{0:T(128)S(1)}, s32[8]{0:T(128)}, u32[]{:S(2)}) copy-start(s32[8]{0:T(128)} %constant.154.clone) | copy-start | bytes 100
  57.4 28.4 %all-to-all-start = ((bf16[32,8,2176]{2,1,0:T(8,128)(2,1)}), bf16[32,8,2176]{2,1,0:T(8,128)(2,1)S(1)}, u32[]{:S(2)}, u32[]{:S(2)}) async-start(bf16[32,8,2176]{2,1,0:T(8,128)(2,1)} %bitcast.13), calls=%async_computation | async-start | bytes 2228224 | tf_op jit(solution)/shard_map/all_to_all | solution.py:177
  87.1 35.8 %copy-start.2 = (bf16[1,1,256,2048]{3,2,1,0:T(8,128)(2,1)S(1)}, bf16[1,1,256,2048]{3,2,1,0:T(8,128)(2,1)}, u32[]{:S(2)}) copy-start(bf16[1,1,256,2048]{3,2,1,0:T(8,128)(2,1)} %param.20) | copy-start | bytes 3145732
  87.2 16.6 %collective-permute-start = (bf16[32,2048]{1,0:T(8,128)(2,1)S(1)}, bf16[32,2048]{1,0:T(8,128)(2,1)S(1)}, u32[]{:S(2)}, u32[]{:S(2)}) collective-permute-start(bf16[32,2048]{1,0:T(8,128)(2,1)S(1)} %get-tuple-element.49), channel_id=1, source_target_pairs={{0,4},{1,5},{2,6},{3,7},{4,8},{5,9},{6,10},{7,11},{8,12},{9,13},{1... | collective-permute-start | bytes 393224 | tf_op jit(solution)/shard_map/ppermute | solution.py:144
  89.3 26.8 %collective-permute-start.6 = (bf16[32,2048]{1,0:T(8,128)(2,1)S(1)}, bf16[32,2048]{1,0:T(8,128)(2,1)S(1)}, u32[]{:S(2)}, u32[]{:S(2)}) collective-permute-start(bf16[32,2048]{1,0:T(8,128)(2,1)S(1)} %get-tuple-element.48), channel_id=1, source_target_pairs={{0,31},{1,0},{2,1},{3,2},{4,3},{5,4},{6,5},{7,6},{8,7},{9,8},{10,9... | collective-permute-start | bytes 393224 | tf_op jit(solution)/shard_map/ppermute | solution.py:132
  91.2 17.6 %collective-permute-start.1 = (bf16[32,2048]{1,0:T(8,128)(2,1)S(1)}, bf16[32,2048]{1,0:T(8,128)(2,1)S(1)}, u32[]{:S(2)}, u32[]{:S(2)}) collective-permute-start(bf16[32,2048]{1,0:T(8,128)(2,1)S(1)} %get-tuple-element.50), channel_id=1, source_target_pairs={{0,3},{1,4},{2,5},{3,6},{4,7},{5,8},{6,9},{7,10},{8,11},{9,12},{10... | collective-permute-start | bytes 393224 | tf_op jit(solution)/shard_map/ppermute | solution.py:132
  94.6 16.1 %collective-permute-start.2 = (bf16[32,2048]{1,0:T(8,128)(2,1)S(1)}, bf16[32,2048]{1,0:T(8,128)(2,1)S(1)}, u32[]{:S(2)}, u32[]{:S(2)}) collective-permute-start(bf16[32,2048]{1,0:T(8,128)(2,1)S(1)} %get-tuple-element.51), channel_id=1, source_target_pairs={{0,29},{1,30},{2,31},{3,0},{4,1},{5,2},{6,3},{7,4},{8,5},{9,6},{10... | collective-permute-start | bytes 393224 | tf_op jit(solution)/shard_map/ppermute | solution.py:132
  99.5 14.5 %collective-permute-start.3 = (bf16[32,2048]{1,0:T(8,128)(2,1)S(1)}, bf16[32,2048]{1,0:T(8,128)(2,1)S(1)}, u32[]{:S(2)}, u32[]{:S(2)}) collective-permute-start(bf16[32,2048]{1,0:T(8,128)(2,1)S(1)} %get-tuple-element.52), channel_id=1, source_target_pairs={{0,2},{1,3},{2,4},{3,5},{4,6},{5,7},{6,8},{7,9},{8,10},{9,11},{10,... | collective-permute-start | bytes 393224 | tf_op jit(solution)/shard_map/ppermute | solution.py:132
  103.8 10.2 %collective-permute-start.4 = (bf16[32,2048]{1,0:T(8,128)(2,1)S(1)}, bf16[32,2048]{1,0:T(8,128)(2,1)S(1)}, u32[]{:S(2)}, u32[]{:S(2)}) collective-permute-start(bf16[32,2048]{1,0:T(8,128)(2,1)S(1)} %get-tuple-element.53), channel_id=1, source_target_pairs={{0,30},{1,31},{2,0},{3,1},{4,2},{5,3},{6,4},{7,5},{8,6},{9,7},{10,... | collective-permute-start | bytes 393224 | tf_op jit(solution)/shard_map/ppermute | solution.py:132
  108.8 7.3 %collective-permute-start.5 = (bf16[32,2048]{1,0:T(8,128)(2,1)S(1)}, bf16[32,2048]{1,0:T(8,128)(2,1)S(1)}, u32[]{:S(2)}, u32[]{:S(2)}) collective-permute-start(bf16[32,2048]{1,0:T(8,128)(2,1)S(1)} %get-tuple-element.54), channel_id=1, source_target_pairs={{0,1},{1,2},{2,3},{3,4},{4,5},{5,6},{6,7},{7,8},{8,9},{9,10},{10,1... | collective-permute-start | bytes 393224 | tf_op jit(solution)/shard_map/ppermute | solution.py:132
  110.7 12.2 %copy-start = (bf16[1,1,2048,256]{3,2,1,0:T(8,128)(2,1)S(1)}, bf16[1,1,2048,256]{3,2,1,0:T(8,128)(2,1)}, u32[]{:S(2)}) copy-start(bf16[1,1,2048,256]{3,2,1,0:T(8,128)(2,1)} %param.18) | copy-start | bytes 3145732
  110.7 12.2 %copy-start.1 = (bf16[1,1,2048,256]{3,2,1,0:T(8,128)(2,1)S(1)}, bf16[1,1,2048,256]{3,2,1,0:T(8,128)(2,1)}, u32[]{:S(2)}) copy-start(bf16[1,1,2048,256]{3,2,1,0:T(8,128)(2,1)} %param.19) | copy-start | bytes 3145732
  116.1 6.8 %collective-permute-start.7 = (bf16[256,2048]{1,0:T(8,128)(2,1)S(1)}, bf16[256,2048]{1,0:T(8,128)(2,1)S(1)}, u32[]{:S(2)}, u32[]{:S(2)}) collective-permute-start(bf16[256,2048]{1,0:T(8,128)(2,1)S(1)} %fusion.29.mine), channel_id=1, source_target_pairs={{0,32},{32,0},{64,96},{96,64},{128,160},{160,128},{192,224},{224,1... | collective-permute-start | bytes 3145736 | tf_op jit(solution)/shard_map/ppermute | solution.py:147
  124.9 4.6 %collective-permute-start.8 = (bf16[256,2048]{1,0:T(8,128)(2,1)S(1)}, bf16[256,2048]{1,0:T(8,128)(2,1)S(1)}, u32[]{:S(2)}, u32[]{:S(2)}) collective-permute-start(bf16[256,2048]{1,0:T(8,128)(2,1)S(1)} %get-tuple-element.23), channel_id=1, source_target_pairs={{0,32},{32,0},{64,96},{96,64},{128,160},{160,128},{192,224},{224,1... | collective-permute-start | bytes 3145736 | tf_op jit(solution)/shard_map/ppermute | solution.py:147
  130.1 17.6 %collective-permute-start.9 = (bf16[32,2048]{1,0:T(8,128)(2,1)S(1)}, bf16[32,2048]{1,0:T(8,128)(2,1)S(1)}, u32[]{:S(2)}, u32[]{:S(2)}) collective-permute-start(bf16[32,2048]{1,0:T(8,128)(2,1)S(1)} %get-tuple-element.47), channel_id=1, source_target_pairs={{0,28},{1,29},{2,30},{3,31},{4,0},{5,1},{6,2},{7,3},{8,4},{9,5},{1... | collective-permute-start | bytes 393224 | tf_op jit(solution)/shard_map/ppermute | solution.py:144
  133.8 39.2 %collective-permute-start.15 = (bf16[32,2048]{1,0:T(8,128)(2,1)S(1)}, bf16[32,2048]{1,0:T(8,128)(2,1)S(1)}, u32[]{:S(2)}, u32[]{:S(2)}) collective-permute-start(bf16[32,2048]{1,0:T(8,128)(2,1)S(1)} %get-tuple-element.41), channel_id=1, source_target_pairs={{0,1},{1,2},{2,3},{3,4},{4,5},{5,6},{6,7},{7,8},{8,9},{9,10},{10,1... | collective-permute-start | bytes 393224 | tf_op jit(solution)/shard_map/ppermute | solution.py:132
  136.3 36.6 %collective-permute-start.14 = (bf16[32,2048]{1,0:T(8,128)(2,1)S(1)}, bf16[32,2048]{1,0:T(8,128)(2,1)S(1)}, u32[]{:S(2)}, u32[]{:S(2)}) collective-permute-start(bf16[32,2048]{1,0:T(8,128)(2,1)S(1)} %get-tuple-element.42), channel_id=1, source_target_pairs={{0,31},{1,0},{2,1},{3,2},{4,3},{5,4},{6,5},{7,6},{8,7},{9,8},{10,9... | collective-permute-start | bytes 393224 | tf_op jit(solution)/shard_map/ppermute | solution.py:132
  140.3 32.6 %collective-permute-start.13 = (bf16[32,2048]{1,0:T(8,128)(2,1)S(1)}, bf16[32,2048]{1,0:T(8,128)(2,1)S(1)}, u32[]{:S(2)}, u32[]{:S(2)}) collective-permute-start(bf16[32,2048]{1,0:T(8,128)(2,1)S(1)} %get-tuple-element.43), channel_id=1, source_target_pairs={{0,2},{1,3},{2,4},{3,5},{4,6},{5,7},{6,8},{7,9},{8,10},{9,11},{10,... | collective-permute-start | bytes 393224 | tf_op jit(solution)/shard_map/ppermute | solution.py:132
  142.2 30.7 %collective-permute-start.12 = (bf16[32,2048]{1,0:T(8,128)(2,1)S(1)}, bf16[32,2048]{1,0:T(8,128)(2,1)S(1)}, u32[]{:S(2)}, u32[]{:S(2)}) collective-permute-start(bf16[32,2048]{1,0:T(8,128)(2,1)S(1)} %get-tuple-element.44), channel_id=1, source_target_pairs={{0,30},{1,31},{2,0},{3,1},{4,2},{5,3},{6,4},{7,5},{8,6},{9,7},{10,... | collective-permute-start | bytes 393224 | tf_op jit(solution)/shard_map/ppermute | solution.py:132
  147.7 13.3 %collective-permute-start.10 = (bf16[32,2048]{1,0:T(8,128)(2,1)S(1)}, bf16[32,2048]{1,0:T(8,128)(2,1)S(1)}, u32[]{:S(2)}, u32[]{:S(2)}) collective-permute-start(bf16[32,2048]{1,0:T(8,128)(2,1)S(1)} %get-tuple-element.46), channel_id=1, source_target_pairs={{0,29},{1,30},{2,31},{3,0},{4,1},{5,2},{6,3},{7,4},{8,5},{9,6},{10... | collective-permute-start | bytes 393224 | tf_op jit(solution)/shard_map/ppermute | solution.py:132
  161.0 11.9 %collective-permute-start.11 = (bf16[32,2048]{1,0:T(8,128)(2,1)S(1)}, bf16[32,2048]{1,0:T(8,128)(2,1)S(1)}, u32[]{:S(2)}, u32[]{:S(2)}) collective-permute-start(bf16[32,2048]{1,0:T(8,128)(2,1)S(1)} %get-tuple-element.45), channel_id=1, source_target_pairs={{0,3},{1,4},{2,5},{3,6},{4,7},{5,8},{6,9},{7,10},{8,11},{9,12},{10... | collective-permute-start | bytes 393224 | tf_op jit(solution)/shard_map/ppermute | solution.py:132
  175.2 24.2 %all-to-all-start.1 = ((bf16[32,8,2176]{2,1,0:T(8,128)(2,1)}), bf16[32,8,2176]{2,1,0:T(8,128)(2,1)S(1)}, u32[]{:S(2)}, u32[]{:S(2)}) async-start(bf16[32,8,2176]{2,1,0:T(8,128)(2,1)} %maximum_bitcast_fusion), calls=%async_computation.1 | async-start | bytes 2228224 | tf_op jit(solution)/shard_map/all_to_all | solution.py:246
  200.0 14.1 %collective-permute-start.16 = (bf16[8,2048]{1,0:T(8,128)(2,1)S(1)}, bf16[8,2048]{1,0:T(8,128)(2,1)S(1)}, u32[]{:S(2)}, u32[]{:S(2)}) collective-permute-start(bf16[8,2048]{1,0:T(8,128)(2,1)S(1)} %get-tuple-element.66), channel_id=1, source_target_pairs={{0,8},{1,9},{2,10},{3,11},{4,12},{5,13},{6,14},{7,15},{8,16},{9,17... | collective-permute-start | bytes 98312 | tf_op jit(solution)/shard_map/ppermute | solution.py:132
  209.2 14.1 %collective-permute-start.18 = (bf16[8,2176]{1,0:T(8,128)(2,1)S(1)}, bf16[8,2176]{1,0:T(8,128)(2,1)S(1)}, u32[]{:S(2)}, u32[]{:S(2)}) collective-permute-start(bf16[8,2176]{1,0:T(8,128)(2,1)S(1)} %get-tuple-element.65), channel_id=1, source_target_pairs={{0,24},{1,25},{2,26},{3,27},{4,28},{5,29},{6,30},{7,31},{8,0},{9,1... | collective-permute-start | bytes 104456 | tf_op jit(solution)/shard_map/ppermute | solution.py:132
  214.1 14.7 %collective-permute-start.17 = (bf16[8,4224]{1,0:T(8,128)(2,1)S(1)}, bf16[8,4224]{1,0:T(8,128)(2,1)S(1)}, u32[]{:S(2)}, u32[]{:S(2)}) collective-permute-start(bf16[8,4224]{1,0:T(8,128)(2,1)S(1)} %pad_maximum_fusion.4), channel_id=1, source_target_pairs={{0,8},{1,9},{2,10},{3,11},{4,12},{5,13},{6,14},{7,15},{8,16},{9,17... | collective-permute-start | bytes 202760 | tf_op jit(solution)/shard_map/ppermute | solution.py:132
  223.3 26.4 %collective-permute-start.19 = (bf16[8,4224]{1,0:T(8,128)(2,1)S(1)}, bf16[8,4224]{1,0:T(8,128)(2,1)S(1)}, u32[]{:S(2)}, u32[]{:S(2)}) collective-permute-start(bf16[8,4224]{1,0:T(8,128)(2,1)S(1)} %pad_maximum_fusion.5), channel_id=1, source_target_pairs={{0,24},{1,25},{2,26},{3,27},{4,28},{5,29},{6,30},{7,31},{8,0},{9,1... | collective-permute-start | bytes 202760 | tf_op jit(solution)/shard_map/ppermute | solution.py:132

commit v4 on v3

--- a/solution.py
+++ b/solution.py
@@ -94,7 +94,7 @@
     keep_ref[:, half:] = back
 
 
-def merge_kernel(pad, keep, gave, mine, ret_ref):
+def merge_kernel(pad, keep, gave, mine, *ret_refs):
     n_slots, width = mine.shape
     half = width // 2
     sum_out = keep[:, :half] + gave[:, :half].astype(F32)
@@ -104,9 +104,14 @@
     spots = jnp.where(lane == row, jnp.broadcast_to(term, (n_slots, META)), 0.0)
     spare = jnp.sum(spots.reshape(n_slots // pad, pad, META), axis=1, keepdims=True)
     spare = jnp.broadcast_to(spare, (n_slots // pad, pad, META)).reshape(n_slots, META)
-    ret_ref[:, :half] = sum_out.astype(BF)
-    ret_ref[:, :META] = jnp.where(row == pad - 1, spare, sum_out[:, :META]).astype(BF)
-    ret_ref[:, half:] = (keep[:, half:] + gave[:, half:].astype(F32)).astype(BF)
+    first = jnp.where(row == pad - 1, spare, sum_out[:, :META])
+    back = keep[:, half:] + gave[:, half:].astype(F32)
+    rows = n_slots // len(ret_refs)
+    for i, ref in enumerate(ret_refs):
+        at = slice(i * rows, (i + 1) * rows)
+        ref[:, :META] = first[at].astype(BF)
+        ref[:, META:half] = sum_out[at, META:].astype(BF)
+        ref[:, half:] = back[at].astype(BF)
 
 
 def body(tokens, grad_mixed, gates, group_ids, expert_ids, w_gate, w_up, w_down):
@@ -229,8 +234,8 @@
         *weights,
         scalars=1,
     )
-    ret = whole(functools.partial(merge_kernel, pad), wide, 4 * n_slots * width, keep, gave, mine)
-    ret = ret.reshape(near, far * pad, width)
+    block = jax.ShapeDtypeStruct((far * pad, width), BF)
+    ret = whole(functools.partial(merge_kernel, pad), (block,) * near, 4 * n_slots * width, keep, gave, mine)
     ret = jnp.concatenate(
         [hop(ret[i], s, -1) for i, s in enumerate(steps)], axis=0
     )
@@ -257,15 +262,8 @@
         axis=1,
     ).reshape(far, tok, 2 * width + META)
     total = full[0]
-    if far == 4:
-        up = shift(full[2][:, :width].astype(BF), near).astype(F32)
-        down = shift(full[2][:, width:].astype(BF), -near).astype(F32)
-        above = jnp.concatenate([full[1][:, :width] + up, full[1][:, width:]], axis=1)
-        below = jnp.concatenate([full[3][:, :width], full[3][:, width:] + down], axis=1)
-        total = total + shift(above.astype(BF), near).astype(F32) + shift(below.astype(BF), -near).astype(F32)
-    else:
-        for f in range(1, far):
-            total = total + shift(full[f].astype(BF), near * f).astype(F32)
+    for f in sorted(range(1, far), key=lambda f: -min(f, far - f)):
+        total = total + shift(full[f].astype(BF), near * f).astype(F32)
     return (
         total[:, :width].astype(BF),
         total[:, width : 2 * width].astype(BF),

time: 252 us -> 233 us (0.925)
  waiting for transfers between devices: 75.6 us -> 60.1 us
  starting transfers between devices: 99.3 us -> 96.2 us
    ppermute x16 -> x15, waiting for transfers between devices: 45.7 us -> 30.2 us  [shift(): lax.ppermute(array, 'local', [(i, (i + by) % n_local) for i in range(n_lo...]
    ppermute x16 -> x15, starting transfers between devices: 69.4 us -> 65.4 us  [shift(): lax.ppermute(array, 'local', [(i, (i + by) % n_local) for i in range(n_lo...]
  transfers between devices with their start and end apart: 22 -> 21, of which waited for: 11 -> 13; matrix products, arithmetic and copies ran while one was open for 1% -> 1% of each run, Pallas kernels for 0% -> 0%
where the time goes in v4:
time: 233 us; the launch traced here: 232 us
  starting transfers between devices  96.2 us (41%)
  waiting for transfers between devices  60.1 us (26%)
  blocking collectives  50.8 us (22%)
  between operations  9.11 us (4%)
  local copies, waits for them, and re-layouts  6.57 us (3%)
  other arithmetic  3.51 us (2%)
  Pallas kernels  3.27 us (1%)
  matrix products  2.48 us (1%)
    ppermute x15, starting transfers between devices, shift(): lax.ppermute(array, 'local', [(i, (i + by) % n_local) for i in range(n_lo...  65.4 us
    all_gather x1, blocking collectives, body(): lax.all_gather(own, 'local', axis=0, tiled=True, axis_index_groups=[[b +...  50.8 us
    ppermute x15, waiting for transfers between devices, shift(): lax.ppermute(array, 'local', [(i, (i + by) % n_local) for i in range(n_lo...  30.2 us
    all_to_all x2, waiting for transfers between devices, body(): got = lax.all_to_all(send, 'group', split_axis=0, concat_axis=0, tiled=True)  26 us
    all_to_all x2, starting transfers between devices, body(): got = lax.all_to_all(send, 'group', split_axis=0, concat_axis=0, tiled=True)  18.2 us
    ppermute x2, starting transfers between devices, swap(): return lax.ppermute(array, 'group', [(i, i ^ 1) for i in range(n_group)])  6.85 us
    ppermute x2, starting transfers between devices, hop(): return lax.ppermute(array, ('group', 'local'), pairs)  5.77 us
  transfers between devices with their start and end apart: 21, of which 13 were waited for; matrix products, arithmetic and copies ran while one was open for 1% of the time, Pallas kernels for 0%

profile of v4, /device:TPU:1, one launch (start us, length us, event | category | flops | bytes accessed | tf_op | source)
XLA Modules:
  0.0 232.1 jit_solution(5419160837766828842)
XLA Ops:
  0.6 0.8 copy.87.group_ref
  1.4 0.8 copy-done.3
  2.2 0.8 copy-done.4
  2.9 0.7 copy-done.5
  3.6 0.7 copy-done.6
  4.6 50.8 %all_gather.3 = bf16[32,4224]{1,0:T(8,128)(2,1)S(1)} all-gather(bf16[8,4224]{1,0:T(8,128)(2,1)S(1)} %shard_map.112), channel_id=1, replica_groups={{0,8,16,24},{1,9,17,25},{2,10,18,26},{3,11,19,27},{4,12,20,28},{5,13,21..., dimensions={0}, use_global_device_ids=true | all-gather | bytes 337920 | tf_op jit(solution)/shard_map/all_gather | solution.py:164
  56.3 1.1 pad_maximum_fusion
  57.4 10.7 %all-to-all-start = ((bf16[32,8,2176]{2,1,0:T(8,128)(2,1)}), bf16[32,8,2176]{2,1,0:T(8,128)(2,1)S(1)}, u32[]{:S(2)}, u32[]{:S(2)}) async-start(bf16[32,8,2176]{2,1,0:T(8,128)(2,1)} %bitcast.13), calls=%async_computation | async-start | bytes 2228224 | tf_op jit(solution)/shard_map/all_to_all | solution.py:182
  68.3 17.5 %all-to-all-done = bf16[32,8,2176]{2,1,0:T(8,128)(2,1)S(1)} async-done(((bf16[32,8,2176]{2,1,0:T(8,128)(2,1)}), bf16[32,8,2176]{2,1,0:T(8,128)(2,1)S(1)}, u32[]{:S(2)}, u32[]{:S(2)}) %all-to-all-start) | async-done | bytes 1114144 | tf_op jit(solution)/shard_map/all_to_all | solution.py:182
  87.2 2.1 collective-permute-start
  89.3 1.9 collective-permute-start.6
  91.2 3.4 %collective-permute-start.1 = (bf16[32,2048]{1,0:T(8,128)(2,1)S(1)}, bf16[32,2048]{1,0:T(8,128)(2,1)S(1)}, u32[]{:S(2)}, u32[]{:S(2)}) collective-permute-start(bf16[32,2048]{1,0:T(8,128)(2,1)S(1)} %get-tuple-element.57), channel_id=1, source_target_pairs={{0,3},{1,4},{2,5},{3,6},{4,7},{5,8},{6,9},{7,10},{8,11},{9,12},{10... | collective-permute-start | bytes 393224 | tf_op jit(solution)/shard_map/ppermute | solution.py:137
  94.7 4.9 %collective-permute-start.2 = (bf16[32,2048]{1,0:T(8,128)(2,1)S(1)}, bf16[32,2048]{1,0:T(8,128)(2,1)S(1)}, u32[]{:S(2)}, u32[]{:S(2)}) collective-permute-start(bf16[32,2048]{1,0:T(8,128)(2,1)S(1)} %get-tuple-element.58), channel_id=1, source_target_pairs={{0,29},{1,30},{2,31},{3,0},{4,1},{5,2},{6,3},{7,4},{8,5},{9,6},{10... | collective-permute-start | bytes 393224 | tf_op jit(solution)/shard_map/ppermute | solution.py:137
  99.5 4.3 %collective-permute-start.3 = (bf16[32,2048]{1,0:T(8,128)(2,1)S(1)}, bf16[32,2048]{1,0:T(8,128)(2,1)S(1)}, u32[]{:S(2)}, u32[]{:S(2)}) collective-permute-start(bf16[32,2048]{1,0:T(8,128)(2,1)S(1)} %get-tuple-element.59), channel_id=1, source_target_pairs={{0,2},{1,3},{2,4},{3,5},{4,6},{5,7},{6,8},{7,9},{8,10},{9,11},{10,... | collective-permute-start | bytes 393224 | tf_op jit(solution)/shard_map/ppermute | solution.py:137
  103.8 3.1 %collective-permute-start.4 = (bf16[32,2048]{1,0:T(8,128)(2,1)S(1)}, bf16[32,2048]{1,0:T(8,128)(2,1)S(1)}, u32[]{:S(2)}, u32[]{:S(2)}) collective-permute-start(bf16[32,2048]{1,0:T(8,128)(2,1)S(1)} %get-tuple-element.60), channel_id=1, source_target_pairs={{0,30},{1,31},{2,0},{3,1},{4,2},{5,3},{6,4},{7,5},{8,6},{9,7},{10,... | collective-permute-start | bytes 393224 | tf_op jit(solution)/shard_map/ppermute | solution.py:137
  107.0 1.8 collective-permute-done.1
  108.8 1.9 collective-permute-start.5
  110.8 3.2 %collective-permute-done.3 = bf16[32,2048]{1,0:T(8,128)(2,1)S(1)} collective-permute-done((bf16[32,2048]{1,0:T(8,128)(2,1)S(1)}, bf16[32,2048]{1,0:T(8,128)(2,1)S(1)}, u32[]{:S(2)}, u32[]{:S(2)}) %collective-permute-start.3) | collective-permute-done | bytes 131104 | tf_op jit(solution)/shard_map/ppermute | solution.py:137
  114.1 2.0 collective-permute-done.5
  116.1 4.6 %collective-permute-start.7 = (bf16[256,2048]{1,0:T(8,128)(2,1)S(1)}, bf16[256,2048]{1,0:T(8,128)(2,1)S(1)}, u32[]{:S(2)}, u32[]{:S(2)}) collective-permute-start(bf16[256,2048]{1,0:T(8,128)(2,1)S(1)} %fusion.29.mine), channel_id=1, source_target_pairs={{0,32},{32,0},{64,96},{96,64},{128,160},{160,128},{192,224},{224,1... | collective-permute-start | bytes 3145736 | tf_op jit(solution)/shard_map/ppermute | solution.py:152
  120.7 2.3 collective-permute-done.7.other
  122.9 2.0 shard_map.113
  125.0 2.3 collective-permute-start.8
  127.3 0.6 shard_map.114.keep
  127.8 1.7 collective-permute-done.8.gave
  129.5 0.4 shard_map.115
  129.9 3.7 %collective-permute-start.9 = (bf16[32,2048]{1,0:T(8,128)(2,1)S(1)}, bf16[32,2048]{1,0:T(8,128)(2,1)S(1)}, u32[]{:S(2)}, u32[]{:S(2)}) collective-permute-start(bf16[32,2048]{1,0:T(8,128)(2,1)S(1)} %get-tuple-element.32), channel_id=1, source_target_pairs={{0,28},{1,29},{2,30},{3,31},{4,0},{5,1},{6,2},{7,3},{8,4},{9,5},{1... | collective-permute-start | bytes 393224 | tf_op jit(solution)/shard_map/ppermute | solution.py:149
  133.6 4.9 %collective-permute-start.10 = (bf16[32,2048]{1,0:T(8,128)(2,1)S(1)}, bf16[32,2048]{1,0:T(8,128)(2,1)S(1)}, u32[]{:S(2)}, u32[]{:S(2)}) collective-permute-start(bf16[32,2048]{1,0:T(8,128)(2,1)S(1)} %get-tuple-element.33), channel_id=1, source_target_pairs={{0,29},{1,30},{2,31},{3,0},{4,1},{5,2},{6,3},{7,4},{8,5},{9,6},{10... | collective-permute-start | bytes 393224 | tf_op jit(solution)/shard_map/ppermute | solution.py:137
  138.6 2.2 collective-permute-start.11
  140.7 5.1 %collective-permute-start.12 = (bf16[32,2048]{1,0:T(8,128)(2,1)S(1)}, bf16[32,2048]{1,0:T(8,128)(2,1)S(1)}, u32[]{:S(2)}, u32[]{:S(2)}) collective-permute-start(bf16[32,2048]{1,0:T(8,128)(2,1)S(1)} %get-tuple-element.35), channel_id=1, source_target_pairs={{0,30},{1,31},{2,0},{3,1},{4,2},{5,3},{6,4},{7,5},{8,6},{9,7},{10,... | collective-permute-start | bytes 393224 | tf_op jit(solution)/shard_map/ppermute | solution.py:137
  145.9 1.9 collective-permute-start.13
  147.8 4.1 %collective-permute-start.14 = (bf16[32,2048]{1,0:T(8,128)(2,1)S(1)}, bf16[32,2048]{1,0:T(8,128)(2,1)S(1)}, u32[]{:S(2)}, u32[]{:S(2)}) collective-permute-start(bf16[32,2048]{1,0:T(8,128)(2,1)S(1)} %get-tuple-element.37), channel_id=1, source_target_pairs={{0,31},{1,0},{2,1},{3,2},{4,3},{5,4},{6,5},{7,6},{8,7},{9,8},{10,9... | collective-permute-start | bytes 393224 | tf_op jit(solution)/shard_map/ppermute | solution.py:137
  152.0 1.9 collective-permute-start.15
  153.9 2.4 %collective-permute-done.11 = bf16[32,2048]{1,0:T(8,128)(2,1)S(1)} collective-permute-done((bf16[32,2048]{1,0:T(8,128)(2,1)S(1)}, bf16[32,2048]{1,0:T(8,128)(2,1)S(1)}, u32[]{:S(2)}, u32[]{:S(2)}) %collective-permute-start.11) | collective-permute-done | bytes 131104 | tf_op jit(solution)/shard_map/ppermute | solution.py:137
  156.3 1.1 collective-permute-done.13
  157.5 1.4 collective-permute-done.14
  158.9 1.0 collective-permute-done.15
  161.0 1.1 maximum_bitcast_fusion
  162.1 7.4 %all-to-all-start.1 = ((bf16[32,8,2176]{2,1,0:T(8,128)(2,1)}), bf16[32,8,2176]{2,1,0:T(8,128)(2,1)S(1)}, u32[]{:S(2)}, u32[]{:S(2)}) async-start(bf16[32,8,2176]{2,1,0:T(8,128)(2,1)} %maximum_bitcast_fusion), calls=%async_computation.1 | async-start | bytes 2228224 | tf_op jit(solution)/shard_map/all_to_all | solution.py:251
  169.6 0.7 fusion.49
  178.8 8.4 %all-to-all-done.1 = bf16[32,8,2176]{2,1,0:T(8,128)(2,1)S(1)} async-done(((bf16[32,8,2176]{2,1,0:T(8,128)(2,1)}), bf16[32,8,2176]{2,1,0:T(8,128)(2,1)S(1)}, u32[]{:S(2)}, u32[]{:S(2)}) %all-to-all-start.1) | async-done | bytes 1114144 | tf_op jit(solution)/shard_map/all_to_all | solution.py:251
  187.8 11.7 %collective-permute-start.16 = (bf16[8,4224]{1,0:T(8,128)(2,1)S(1)}, bf16[8,4224]{1,0:T(8,128)(2,1)S(1)}, u32[]{:S(2)}, u32[]{:S(2)}) collective-permute-start(bf16[8,4224]{1,0:T(8,128)(2,1)S(1)} %get-tuple-element.62), channel_id=1, source_target_pairs={{0,16},{1,17},{2,18},{3,19},{4,20},{5,21},{6,22},{7,23},{8,24},{9,... | collective-permute-start | bytes 202760 | tf_op jit(solution)/shard_map/ppermute | solution.py:137
  199.5 6.3 %collective-permute-start.18 = (bf16[8,4224]{1,0:T(8,128)(2,1)S(1)}, bf16[8,4224]{1,0:T(8,128)(2,1)S(1)}, u32[]{:S(2)}, u32[]{:S(2)}) collective-permute-start(bf16[8,4224]{1,0:T(8,128)(2,1)S(1)} %get-tuple-element.63), channel_id=1, source_target_pairs={{0,24},{1,25},{2,26},{3,27},{4,28},{5,29},{6,30},{7,31},{8,0},{9,1... | collective-permute-start | bytes 202760 | tf_op jit(solution)/shard_map/ppermute | solution.py:137
  205.8 7.7 %collective-permute-start.17 = (bf16[8,4224]{1,0:T(8,128)(2,1)S(1)}, bf16[8,4224]{1,0:T(8,128)(2,1)S(1)}, u32[]{:S(2)}, u32[]{:S(2)}) collective-permute-start(bf16[8,4224]{1,0:T(8,128)(2,1)S(1)} %get-tuple-element.64), channel_id=1, source_target_pairs={{0,8},{1,9},{2,10},{3,11},{4,12},{5,13},{6,14},{7,15},{8,16},{9,17... | collective-permute-start | bytes 202760 | tf_op jit(solution)/shard_map/ppermute | solution.py:137
  213.5 15.0 %collective-permute-done.18 = bf16[8,4224]{1,0:T(8,128)(2,1)S(1)} collective-permute-done((bf16[8,4224]{1,0:T(8,128)(2,1)S(1)}, bf16[8,4224]{1,0:T(8,128)(2,1)S(1)}, u32[]{:S(2)}, u32[]{:S(2)}) %collective-permute-start.18) | collective-permute-done | bytes 67616 | tf_op jit(solution)/shard_map/ppermute | solution.py:137
  228.5 2.3 collective-permute-done.17
  230.9 0.6 fusion.48
  231.5 0.6 slice.249
  (91 shorter events, 5.1 us)
Async XLA Ops:
  1.4 0.8 copy-start.3
  2.2 0.8 copy-start.4
  2.9 0.7 copy-start.5
  3.6 0.7 copy-start.6
  57.4 10.8 %copy-start.7 = (s32[8]{0:T(128)S(1)}, s32[8]{0:T(128)}, u32[]{:S(2)}) copy-start(s32[8]{0:T(128)} %constant.154.clone) | copy-start | bytes 100
  57.4 28.4 %all-to-all-start = ((bf16[32,8,2176]{2,1,0:T(8,128)(2,1)}), bf16[32,8,2176]{2,1,0:T(8,128)(2,1)S(1)}, u32[]{:S(2)}, u32[]{:S(2)}) async-start(bf16[32,8,2176]{2,1,0:T(8,128)(2,1)} %bitcast.13), calls=%async_computation | async-start | bytes 2228224 | tf_op jit(solution)/shard_map/all_to_all | solution.py:182
  87.1 35.8 %copy-start.2 = (bf16[1,1,256,2048]{3,2,1,0:T(8,128)(2,1)S(1)}, bf16[1,1,256,2048]{3,2,1,0:T(8,128)(2,1)}, u32[]{:S(2)}) copy-start(bf16[1,1,256,2048]{3,2,1,0:T(8,128)(2,1)} %param.20) | copy-start | bytes 3145732
  87.2 16.6 %collective-permute-start = (bf16[32,2048]{1,0:T(8,128)(2,1)S(1)}, bf16[32,2048]{1,0:T(8,128)(2,1)S(1)}, u32[]{:S(2)}, u32[]{:S(2)}) collective-permute-start(bf16[32,2048]{1,0:T(8,128)(2,1)S(1)} %get-tuple-element.56), channel_id=1, source_target_pairs={{0,4},{1,5},{2,6},{3,7},{4,8},{5,9},{6,10},{7,11},{8,12},{9,13},{1... | collective-permute-start | bytes 393224 | tf_op jit(solution)/shard_map/ppermute | solution.py:149
  89.3 26.8 %collective-permute-start.6 = (bf16[32,2048]{1,0:T(8,128)(2,1)S(1)}, bf16[32,2048]{1,0:T(8,128)(2,1)S(1)}, u32[]{:S(2)}, u32[]{:S(2)}) collective-permute-start(bf16[32,2048]{1,0:T(8,128)(2,1)S(1)} %get-tuple-element.55), channel_id=1, source_target_pairs={{0,31},{1,0},{2,1},{3,2},{4,3},{5,4},{6,5},{7,6},{8,7},{9,8},{10,9... | collective-permute-start | bytes 393224 | tf_op jit(solution)/shard_map/ppermute | solution.py:137
  91.2 17.6 %collective-permute-start.1 = (bf16[32,2048]{1,0:T(8,128)(2,1)S(1)}, bf16[32,2048]{1,0:T(8,128)(2,1)S(1)}, u32[]{:S(2)}, u32[]{:S(2)}) collective-permute-start(bf16[32,2048]{1,0:T(8,128)(2,1)S(1)} %get-tuple-element.57), channel_id=1, source_target_pairs={{0,3},{1,4},{2,5},{3,6},{4,7},{5,8},{6,9},{7,10},{8,11},{9,12},{10... | collective-permute-start | bytes 393224 | tf_op jit(solution)/shard_map/ppermute | solution.py:137
  94.7 16.1 %collective-permute-start.2 = (bf16[32,2048]{1,0:T(8,128)(2,1)S(1)}, bf16[32,2048]{1,0:T(8,128)(2,1)S(1)}, u32[]{:S(2)}, u32[]{:S(2)}) collective-permute-start(bf16[32,2048]{1,0:T(8,128)(2,1)S(1)} %get-tuple-element.58), channel_id=1, source_target_pairs={{0,29},{1,30},{2,31},{3,0},{4,1},{5,2},{6,3},{7,4},{8,5},{9,6},{10... | collective-permute-start | bytes 393224 | tf_op jit(solution)/shard_map/ppermute | solution.py:137
  99.5 14.5 %collective-permute-start.3 = (bf16[32,2048]{1,0:T(8,128)(2,1)S(1)}, bf16[32,2048]{1,0:T(8,128)(2,1)S(1)}, u32[]{:S(2)}, u32[]{:S(2)}) collective-permute-start(bf16[32,2048]{1,0:T(8,128)(2,1)S(1)} %get-tuple-element.59), channel_id=1, source_target_pairs={{0,2},{1,3},{2,4},{3,5},{4,6},{5,7},{6,8},{7,9},{8,10},{9,11},{10,... | collective-permute-start | bytes 393224 | tf_op jit(solution)/shard_map/ppermute | solution.py:137
  103.8 10.2 %collective-permute-start.4 = (bf16[32,2048]{1,0:T(8,128)(2,1)S(1)}, bf16[32,2048]{1,0:T(8,128)(2,1)S(1)}, u32[]{:S(2)}, u32[]{:S(2)}) collective-permute-start(bf16[32,2048]{1,0:T(8,128)(2,1)S(1)} %get-tuple-element.60), channel_id=1, source_target_pairs={{0,30},{1,31},{2,0},{3,1},{4,2},{5,3},{6,4},{7,5},{8,6},{9,7},{10,... | collective-permute-start | bytes 393224 | tf_op jit(solution)/shard_map/ppermute | solution.py:137
  108.8 7.3 %collective-permute-start.5 = (bf16[32,2048]{1,0:T(8,128)(2,1)S(1)}, bf16[32,2048]{1,0:T(8,128)(2,1)S(1)}, u32[]{:S(2)}, u32[]{:S(2)}) collective-permute-start(bf16[32,2048]{1,0:T(8,128)(2,1)S(1)} %get-tuple-element.61), channel_id=1, source_target_pairs={{0,1},{1,2},{2,3},{3,4},{4,5},{5,6},{6,7},{7,8},{8,9},{9,10},{10,1... | collective-permute-start | bytes 393224 | tf_op jit(solution)/shard_map/ppermute | solution.py:137
  110.7 12.2 %copy-start = (bf16[1,1,2048,256]{3,2,1,0:T(8,128)(2,1)S(1)}, bf16[1,1,2048,256]{3,2,1,0:T(8,128)(2,1)}, u32[]{:S(2)}) copy-start(bf16[1,1,2048,256]{3,2,1,0:T(8,128)(2,1)} %param.18) | copy-start | bytes 3145732
  110.8 12.2 %copy-start.1 = (bf16[1,1,2048,256]{3,2,1,0:T(8,128)(2,1)S(1)}, bf16[1,1,2048,256]{3,2,1,0:T(8,128)(2,1)}, u32[]{:S(2)}) copy-start(bf16[1,1,2048,256]{3,2,1,0:T(8,128)(2,1)} %param.19) | copy-start | bytes 3145732
  116.1 6.8 %collective-permute-start.7 = (bf16[256,2048]{1,0:T(8,128)(2,1)S(1)}, bf16[256,2048]{1,0:T(8,128)(2,1)S(1)}, u32[]{:S(2)}, u32[]{:S(2)}) collective-permute-start(bf16[256,2048]{1,0:T(8,128)(2,1)S(1)} %fusion.29.mine), channel_id=1, source_target_pairs={{0,32},{32,0},{64,96},{96,64},{128,160},{160,128},{192,224},{224,1... | collective-permute-start | bytes 3145736 | tf_op jit(solution)/shard_map/ppermute | solution.py:152
  125.0 4.6 %collective-permute-start.8 = (bf16[256,2048]{1,0:T(8,128)(2,1)S(1)}, bf16[256,2048]{1,0:T(8,128)(2,1)S(1)}, u32[]{:S(2)}, u32[]{:S(2)}) collective-permute-start(bf16[256,2048]{1,0:T(8,128)(2,1)S(1)} %get-tuple-element.31), channel_id=1, source_target_pairs={{0,32},{32,0},{64,96},{96,64},{128,160},{160,128},{192,224},{224,1... | collective-permute-start | bytes 3145736 | tf_op jit(solution)/shard_map/ppermute | solution.py:152
  129.9 17.9 %collective-permute-start.9 = (bf16[32,2048]{1,0:T(8,128)(2,1)S(1)}, bf16[32,2048]{1,0:T(8,128)(2,1)S(1)}, u32[]{:S(2)}, u32[]{:S(2)}) collective-permute-start(bf16[32,2048]{1,0:T(8,128)(2,1)S(1)} %get-tuple-element.32), channel_id=1, source_target_pairs={{0,28},{1,29},{2,30},{3,31},{4,0},{5,1},{6,2},{7,3},{8,4},{9,5},{1... | collective-permute-start | bytes 393224 | tf_op jit(solution)/shard_map/ppermute | solution.py:149
  133.6 18.3 %collective-permute-start.10 = (bf16[32,2048]{1,0:T(8,128)(2,1)S(1)}, bf16[32,2048]{1,0:T(8,128)(2,1)S(1)}, u32[]{:S(2)}, u32[]{:S(2)}) collective-permute-start(bf16[32,2048]{1,0:T(8,128)(2,1)S(1)} %get-tuple-element.33), channel_id=1, source_target_pairs={{0,29},{1,30},{2,31},{3,0},{4,1},{5,2},{6,3},{7,4},{8,5},{9,6},{10... | collective-permute-start | bytes 393224 | tf_op jit(solution)/shard_map/ppermute | solution.py:137
  138.6 17.7 %collective-permute-start.11 = (bf16[32,2048]{1,0:T(8,128)(2,1)S(1)}, bf16[32,2048]{1,0:T(8,128)(2,1)S(1)}, u32[]{:S(2)}, u32[]{:S(2)}) collective-permute-start(bf16[32,2048]{1,0:T(8,128)(2,1)S(1)} %get-tuple-element.34), channel_id=1, source_target_pairs={{0,3},{1,4},{2,5},{3,6},{4,7},{5,8},{6,9},{7,10},{8,11},{9,12},{10... | collective-permute-start | bytes 393224 | tf_op jit(solution)/shard_map/ppermute | solution.py:137
  140.7 15.6 %collective-permute-start.12 = (bf16[32,2048]{1,0:T(8,128)(2,1)S(1)}, bf16[32,2048]{1,0:T(8,128)(2,1)S(1)}, u32[]{:S(2)}, u32[]{:S(2)}) collective-permute-start(bf16[32,2048]{1,0:T(8,128)(2,1)S(1)} %get-tuple-element.35), channel_id=1, source_target_pairs={{0,30},{1,31},{2,0},{3,1},{4,2},{5,3},{6,4},{7,5},{8,6},{9,7},{10,... | collective-permute-start | bytes 393224 | tf_op jit(solution)/shard_map/ppermute | solution.py:137
  145.9 11.6 %collective-permute-start.13 = (bf16[32,2048]{1,0:T(8,128)(2,1)S(1)}, bf16[32,2048]{1,0:T(8,128)(2,1)S(1)}, u32[]{:S(2)}, u32[]{:S(2)}) collective-permute-start(bf16[32,2048]{1,0:T(8,128)(2,1)S(1)} %get-tuple-element.36), channel_id=1, source_target_pairs={{0,2},{1,3},{2,4},{3,5},{4,6},{5,7},{6,8},{7,9},{8,10},{9,11},{10,... | collective-permute-start | bytes 393224 | tf_op jit(solution)/shard_map/ppermute | solution.py:137
  147.8 11.1 %collective-permute-start.14 = (bf16[32,2048]{1,0:T(8,128)(2,1)S(1)}, bf16[32,2048]{1,0:T(8,128)(2,1)S(1)}, u32[]{:S(2)}, u32[]{:S(2)}) collective-permute-start(bf16[32,2048]{1,0:T(8,128)(2,1)S(1)} %get-tuple-element.37), channel_id=1, source_target_pairs={{0,31},{1,0},{2,1},{3,2},{4,3},{5,4},{6,5},{7,6},{8,7},{9,8},{10,9... | collective-permute-start | bytes 393224 | tf_op jit(solution)/shard_map/ppermute | solution.py:137
  152.0 7.9 %collective-permute-start.15 = (bf16[32,2048]{1,0:T(8,128)(2,1)S(1)}, bf16[32,2048]{1,0:T(8,128)(2,1)S(1)}, u32[]{:S(2)}, u32[]{:S(2)}) collective-permute-start(bf16[32,2048]{1,0:T(8,128)(2,1)S(1)} %get-tuple-element.38), channel_id=1, source_target_pairs={{0,1},{1,2},{2,3},{3,4},{4,5},{5,6},{6,7},{7,8},{8,9},{9,10},{10,1... | collective-permute-start | bytes 393224 | tf_op jit(solution)/shard_map/ppermute | solution.py:137
  162.1 25.1 %all-to-all-start.1 = ((bf16[32,8,2176]{2,1,0:T(8,128)(2,1)}), bf16[32,8,2176]{2,1,0:T(8,128)(2,1)S(1)}, u32[]{:S(2)}, u32[]{:S(2)}) async-start(bf16[32,8,2176]{2,1,0:T(8,128)(2,1)} %maximum_bitcast_fusion), calls=%async_computation.1 | async-start | bytes 2228224 | tf_op jit(solution)/shard_map/all_to_all | solution.py:251
  187.8 25.8 %collective-permute-start.16 = (bf16[8,4224]{1,0:T(8,128)(2,1)S(1)}, bf16[8,4224]{1,0:T(8,128)(2,1)S(1)}, u32[]{:S(2)}, u32[]{:S(2)}) collective-permute-start(bf16[8,4224]{1,0:T(8,128)(2,1)S(1)} %get-tuple-element.62), channel_id=1, source_target_pairs={{0,16},{1,17},{2,18},{3,19},{4,20},{5,21},{6,22},{7,23},{8,24},{9,... | collective-permute-start | bytes 202760 | tf_op jit(solution)/shard_map/ppermute | solution.py:137
  199.5 29.0 %collective-permute-start.18 = (bf16[8,4224]{1,0:T(8,128)(2,1)S(1)}, bf16[8,4224]{1,0:T(8,128)(2,1)S(1)}, u32[]{:S(2)}, u32[]{:S(2)}) collective-permute-start(bf16[8,4224]{1,0:T(8,128)(2,1)S(1)} %get-tuple-element.63), channel_id=1, source_target_pairs={{0,24},{1,25},{2,26},{3,27},{4,28},{5,29},{6,30},{7,31},{8,0},{9,1... | collective-permute-start | bytes 202760 | tf_op jit(solution)/shard_map/ppermute | solution.py:137
  205.8 25.0 %collective-permute-start.17 = (bf16[8,4224]{1,0:T(8,128)(2,1)S(1)}, bf16[8,4224]{1,0:T(8,128)(2,1)S(1)}, u32[]{:S(2)}, u32[]{:S(2)}) collective-permute-start(bf16[8,4224]{1,0:T(8,128)(2,1)S(1)} %get-tuple-element.64), channel_id=1, source_target_pairs={{0,8},{1,9},{2,10},{3,11},{4,12},{5,13},{6,14},{7,15},{8,16},{9,17... | collective-permute-start | bytes 202760 | tf_op jit(solution)/shard_map/ppermute | solution.py:137

commit v5 on v4

--- a/solution.py
+++ b/solution.py
@@ -30,15 +30,21 @@
     )(*args)
 
 
-def pack_kernel(n_local, groups, x_ref, dy_ref, gate_ref, group_ref, expert_ref, own_ref):
+def pack_kernel(n_local, groups, *refs):
+    own_ref, sems = refs[5], refs[11]
+    copies = [pltpu.make_async_copy(refs[i], refs[6 + i], sems.at[i]) for i in range(5)]
+    for copy in copies:
+        copy.start()
+    for copy in copies:
+        copy.wait()
+    x_ref, dy_ref, gate_ref, group_ref, expert_ref = refs[6:11]
     tok, width = x_ref.shape
-    topk = expert_ref.shape[1]
-    member = jnp.zeros((tok, groups), F32)
-    iota = lax.broadcasted_iota(jnp.int32, (tok, groups), 1)
-    for n in range(group_ref.shape[1]):
-        member = jnp.where(group_ref[:, n : n + 1] == iota, 1.0, member)
-    lower = lax.broadcasted_iota(jnp.int32, (tok, tok), 1) < lax.broadcasted_iota(jnp.int32, (tok, tok), 0)
-    placed = dot(jnp.where(lower, 1.0, 0.0).astype(BF), member.astype(BF), ((1,), (0,)))
+    member = jnp.zeros((groups, tok), F32)
+    iota = lax.broadcasted_iota(jnp.int32, (groups, tok), 0)
+    for n in range(group_ref.shape[0]):
+        member = jnp.where(group_ref[n : n + 1, :] == iota, 1.0, member)
+    upper = lax.broadcasted_iota(jnp.int32, (tok, tok), 0) < lax.broadcasted_iota(jnp.int32, (tok, tok), 1)
+    placed = dot(member.astype(BF), jnp.where(upper, 1.0, 0.0).astype(BF), ((1,), (0,)))
     code = jnp.where(member > 0, placed, -1.0)
     ids = expert_ref[...]
     shift = n_local.bit_length() - 1
@@ -46,7 +52,7 @@
         lax.shift_right_logical(ids, shift).astype(F32).astype(BF),
         (ids & (n_local - 1)).astype(F32).astype(BF),
         gate_ref[...],
-        code.astype(BF),
+        code.T.astype(BF),
     )
     meta = jnp.zeros((tok, META), F32)
     start = 0
@@ -151,16 +157,15 @@
     def swap(array):
         return lax.ppermute(array, "group", [(i, i ^ 1) for i in range(n_group)])
 
-    own = whole(
+    parts = (tokens, grad_mixed, gates, group_ids.T, expert_ids)
+    own = pl.pallas_call(
         functools.partial(pack_kernel, n_local, groups),
-        jax.ShapeDtypeStruct((tok, 2 * width + META), BF),
-        4 * tok * META * topk,
-        tokens,
-        grad_mixed,
-        gates,
-        group_ids,
-        expert_ids,
-    )
+        out_shape=jax.ShapeDtypeStruct((tok, 2 * width + META), BF),
+        in_specs=[pl.BlockSpec(memory_space=pl.ANY)] * 5,
+        out_specs=pl.BlockSpec(memory_space=pltpu.VMEM),
+        scratch_shapes=[pltpu.VMEM(p.shape, p.dtype) for p in parts] + [pltpu.SemaphoreType.DMA((5,))],
+        cost_estimate=pl.CostEstimate(flops=tok * META * 100, bytes_accessed=8 * tok * width, transcendentals=0),
+    )(*parts)
     rows = lax.all_gather(
         own, "local", axis=0, tiled=True, axis_index_groups=[[b + near * f for f in range(far)] for b in range(near)]
     )
@@ -168,7 +173,8 @@
     codes = rows[:, 2 * width + 3 * topk : 2 * width + 3 * topk + groups].T
     codes = codes.astype(F32)[:, None, None, :] == jnp.arange(per_group, dtype=F32)[None, None, :, None]
     row_plane = jnp.arange(far * tok, dtype=jnp.int32) // tok
-    planes = jnp.arange(far, dtype=jnp.int32)
+    away = sorted(range(far), key=lambda f: -min(f, far - f))
+    planes = (z // near + jnp.array(away, jnp.int32)) % far
     chooser = (codes & (row_plane[None, :] == planes[:, None])[None, :, None, :]).astype(BF)
     chooser = chooser.reshape(groups * far * per_group, far * tok)
     parts = []
@@ -198,8 +204,9 @@
     ranked = dot(counted.astype(BF), ahead, ((1,), (0,))).astype(jnp.int32)
     kept = counted & (ranked < capacity)
     slot = jnp.where(kept, ranked, -1)
+    plane_at = (z // near + sum(jnp.where(plane_of == q, f, 0) for q, f in enumerate(away))) % far
     hit = (slot[:, None, None, :] == jnp.arange(pad, dtype=jnp.int32)[None, None, :, None]) & (
-        plane_of[None, None, None, :] == jnp.arange(far, dtype=jnp.int32)[None, :, None, None]
+        plane_at[None, None, None, :] == jnp.arange(far, dtype=jnp.int32)[None, :, None, None]
     )
     n_slots = near * far * pad
     plain = hit.astype(BF).reshape(n_slots, n_rows)
@@ -248,22 +255,35 @@
     term_k = jnp.pad(term_k, ((0, META - topk), (0, 0))).T
     send = jnp.concatenate([row_out.astype(BF), row_back.astype(BF), term_k.astype(BF)], axis=1)
     send = send.reshape(n_group, far * per_group, width + META)
-    got = lax.all_to_all(send, "group", split_axis=0, concat_axis=0, tiled=True)
-
-    wanted = (z // near + planes) % far
-    turned = chooser.reshape(groups * far * per_group, far, tok)
-    turned = jnp.concatenate([jnp.take(turned, wanted[d], axis=1) for d in range(far)], axis=1)
-    got = got.reshape(groups, 2, far * per_group, width + META)
-    sums = [
-        dot(turned, got[:, c].reshape(groups * far * per_group, width + META), ((0,), (0,))) for c in range(2)
-    ]
-    full = jnp.concatenate(
-        [sums[0][:, :half], sums[1][:, :half], sums[0][:, half:width], sums[1][:, half:width], sums[0][:, width:] + sums[1][:, width:]],
-        axis=1,
-    ).reshape(far, tok, 2 * width + META)
-    total = full[0]
-    for f in sorted(range(1, far), key=lambda f: -min(f, far - f)):
-        total = total + shift(full[f].astype(BF), near * f).astype(F32)
+
+    lone = jnp.sum(chooser.reshape(groups, far, per_group, far, tok), axis=3)
+
+    def to_tokens(low, high):
+        got = lax.all_to_all(
+            send[:, low * per_group : high * per_group], "group", split_axis=0, concat_axis=0, tiled=True
+        )
+        count = high - low
+        picks = lone[:, low:high, :, None, :] * jnp.eye(count, dtype=BF)[None, :, None, :, None]
+        picks = picks.reshape(groups * count * per_group, count * tok)
+        got = got.reshape(groups, 2, count * per_group, width + META)
+        sums = [dot(picks, got[:, c].reshape(groups * count * per_group, width + META), ((0,), (0,))) for c in range(2)]
+        return jnp.concatenate(
+            [
+                sums[0][:, :half],
+                sums[1][:, :half],
+                sums[0][:, half:width],
+                sums[1][:, half:width],
+                sums[0][:, width:] + sums[1][:, width:],
+            ],
+            axis=1,
+        )
+
+    first = shift(to_tokens(0, 1).astype(BF), near * away[0])
+    full = to_tokens(1, far).reshape(far - 1, tok, 2 * width + META)
+    total = full[far - 2]
+    for q in range(1, far - 1):
+        total = total + shift(full[q - 1].astype(BF), near * away[q]).astype(F32)
+    total = total + first.astype(F32)
     return (
         total[:, :width].astype(BF),
         total[:, width : 2 * width].astype(BF),

time: 233 us -> 233 us (level)
  starting transfers between devices: 96.2 us -> 107 us
  between operations: 9.11 us -> 1.51 us
    all_to_all x0 -> x2, waiting for transfers between devices: none -> 12.8 us  [to_tokens(): lax.all_to_all(send[:, low * per_group:high * per_group], 'group', split_...]
    all_to_all x0 -> x2, starting transfers between devices: none -> 12.1 us  [to_tokens(): lax.all_to_all(send[:, low * per_group:high * per_group], 'group', split_...]
    all_to_all x2 -> x1, waiting for transfers between devices: 26 us -> 17.5 us  [body(): got = lax.all_to_all(send, 'group', split_axis=0, concat_axis=0, tiled=True)]
    all_to_all x2 -> x1, starting transfers between devices: 18.2 us -> 10.7 us  [body(): got = lax.all_to_all(send, 'group', split_axis=0, concat_axis=0, tiled=True)]
    ppermute x15, waiting for transfers between devices: 30.2 us -> 24 us  [shift(): lax.ppermute(array, 'local', [(i, (i + by) % n_local) for i in range(n_lo...]
    ppermute x15, starting transfers between devices: 65.4 us -> 69.7 us  [shift(): lax.ppermute(array, 'local', [(i, (i + by) % n_local) for i in range(n_lo...]
    unnamed x36 -> x34, local copies, waits for them, and re-layouts: 3.96 us -> 0.42 us
  transfers between devices with their start and end apart: 21 -> 22, of which waited for: 13 -> 12; matrix products, arithmetic and copies ran while one was open for 1% -> 1% of each run, Pallas kernels for 0% -> 0%
where the time goes in v5:
time: 233 us; the launch traced here: 232 us
  starting transfers between devices  107 us (46%)
  waiting for transfers between devices  58.2 us (25%)
  blocking collectives  51 us (22%)
  local copies, waits for them, and re-layouts  4.74 us (2%)
  Pallas kernels  4.69 us (2%)
  matrix products  2.88 us (1%)
  other arithmetic  2.49 us (1%)
    ppermute x15, starting transfers between devices, shift(): lax.ppermute(array, 'local', [(i, (i + by) % n_local) for i in range(n_lo...  69.7 us
    all_gather x1, blocking collectives, body(): lax.all_gather(own, 'local', axis=0, tiled=True, axis_index_groups=[[b +...  51 us
    ppermute x15, waiting for transfers between devices, shift(): lax.ppermute(array, 'local', [(i, (i + by) % n_local) for i in range(n_lo...  24 us
    all_to_all x1, waiting for transfers between devices, body(): got = lax.all_to_all(send, 'group', split_axis=0, concat_axis=0, tiled=True)  17.5 us
    all_to_all x2, waiting for transfers between devices, to_tokens(): lax.all_to_all(send[:, low * per_group:high * per_group], 'group', split_...  12.8 us
    all_to_all x2, starting transfers between devices, to_tokens(): lax.all_to_all(send[:, low * per_group:high * per_group], 'group', split_...  12.1 us
    all_to_all x1, starting transfers between devices, body(): got = lax.all_to_all(send, 'group', split_axis=0, concat_axis=0, tiled=True)  10.7 us
    ppermute x2, starting transfers between devices, swap(): return lax.ppermute(array, 'group', [(i, i ^ 1) for i in range(n_group)])  7.53 us
  transfers between devices with their start and end apart: 22, of which 12 were waited for; matrix products, arithmetic and copies ran while one was open for 1% of the time, Pallas kernels for 0%

profile of v5, /device:TPU:1, one launch (start us, length us, event | category | flops | bytes accessed | tf_op | source)
XLA Modules:
  0.0 232.4 jit_solution(1358296026216098267)
XLA Ops:
  0.7 1.8 shard_map.121
  2.4 51.0 %all_gather.3 = bf16[32,4224]{1,0:T(8,128)(2,1)S(1)} all-gather(bf16[8,4224]{1,0:T(8,128)(2,1)} %shard_map.121), channel_id=1, replica_groups={{0,8,16,24},{1,9,17,25},{2,10,18,26},{3,11,19,27},{4,12,20,28},{5,13,21..., dimensions={0}, use_global_device_ids=true | all-gather | bytes 337920 | tf_op jit(solution)/shard_map/all_gather | solution.py:169
  54.4 1.1 pad_maximum_fusion
  55.6 10.7 %all-to-all-start = ((bf16[32,8,2176]{2,1,0:T(8,128)(2,1)}), bf16[32,8,2176]{2,1,0:T(8,128)(2,1)S(1)}, u32[]{:S(2)}, u32[]{:S(2)}) async-start(bf16[32,8,2176]{2,1,0:T(8,128)(2,1)} %bitcast.7), calls=%async_computation | async-start | bytes 2228224 | tf_op jit(solution)/shard_map/all_to_all | solution.py:188
  66.4 17.5 %all-to-all-done = bf16[32,8,2176]{2,1,0:T(8,128)(2,1)S(1)} async-done(((bf16[32,8,2176]{2,1,0:T(8,128)(2,1)}), bf16[32,8,2176]{2,1,0:T(8,128)(2,1)S(1)}, u32[]{:S(2)}, u32[]{:S(2)}) %all-to-all-start) | async-done | bytes 1114144 | tf_op jit(solution)/shard_map/all_to_all | solution.py:188
  84.6 0.3 convolution_convert_fusion.3
  84.9 0.3 convolution_convert_fusion.5
  85.4 2.1 collective-permute-start
  87.4 3.4 %collective-permute-start.1 = (bf16[32,2048]{1,0:T(8,128)(2,1)S(1)}, bf16[32,2048]{1,0:T(8,128)(2,1)S(1)}, u32[]{:S(2)}, u32[]{:S(2)}) collective-permute-start(bf16[32,2048]{1,0:T(8,128)(2,1)S(1)} %get-tuple-element.45), channel_id=1, source_target_pairs={{0,3},{1,4},{2,5},{3,6},{4,7},{5,8},{6,9},{7,10},{8,11},{9,12},{10... | collective-permute-start | bytes 393224 | tf_op jit(solution)/shard_map/ppermute | solution.py:143
  90.9 4.8 %collective-permute-start.2 = (bf16[32,2048]{1,0:T(8,128)(2,1)S(1)}, bf16[32,2048]{1,0:T(8,128)(2,1)S(1)}, u32[]{:S(2)}, u32[]{:S(2)}) collective-permute-start(bf16[32,2048]{1,0:T(8,128)(2,1)S(1)} %get-tuple-element.46), channel_id=1, source_target_pairs={{0,29},{1,30},{2,31},{3,0},{4,1},{5,2},{6,3},{7,4},{8,5},{9,6},{10... | collective-permute-start | bytes 393224 | tf_op jit(solution)/shard_map/ppermute | solution.py:143
  95.7 4.0 %collective-permute-start.3 = (bf16[32,2048]{1,0:T(8,128)(2,1)S(1)}, bf16[32,2048]{1,0:T(8,128)(2,1)S(1)}, u32[]{:S(2)}, u32[]{:S(2)}) collective-permute-start(bf16[32,2048]{1,0:T(8,128)(2,1)S(1)} %get-tuple-element.47), channel_id=1, source_target_pairs={{0,2},{1,3},{2,4},{3,5},{4,6},{5,7},{6,8},{7,9},{8,10},{9,11},{10,... | collective-permute-start | bytes 393224 | tf_op jit(solution)/shard_map/ppermute | solution.py:143
  99.7 3.4 %collective-permute-start.4 = (bf16[32,2048]{1,0:T(8,128)(2,1)S(1)}, bf16[32,2048]{1,0:T(8,128)(2,1)S(1)}, u32[]{:S(2)}, u32[]{:S(2)}) collective-permute-start(bf16[32,2048]{1,0:T(8,128)(2,1)S(1)} %get-tuple-element.48), channel_id=1, source_target_pairs={{0,30},{1,31},{2,0},{3,1},{4,2},{5,3},{6,4},{7,5},{8,6},{9,7},{10,... | collective-permute-start | bytes 393224 | tf_op jit(solution)/shard_map/ppermute | solution.py:143
  103.1 3.1 %collective-permute-start.5 = (bf16[32,2048]{1,0:T(8,128)(2,1)S(1)}, bf16[32,2048]{1,0:T(8,128)(2,1)S(1)}, u32[]{:S(2)}, u32[]{:S(2)}) collective-permute-start(bf16[32,2048]{1,0:T(8,128)(2,1)S(1)} %get-tuple-element.49), channel_id=1, source_target_pairs={{0,1},{1,2},{2,3},{3,4},{4,5},{5,6},{6,7},{7,8},{8,9},{9,10},{10,1... | collective-permute-start | bytes 393224 | tf_op jit(solution)/shard_map/ppermute | solution.py:143
  106.3 3.4 %collective-permute-start.6 = (bf16[32,2048]{1,0:T(8,128)(2,1)S(1)}, bf16[32,2048]{1,0:T(8,128)(2,1)S(1)}, u32[]{:S(2)}, u32[]{:S(2)}) collective-permute-start(bf16[32,2048]{1,0:T(8,128)(2,1)S(1)} %get-tuple-element.43), channel_id=1, source_target_pairs={{0,31},{1,0},{2,1},{3,2},{4,3},{5,4},{6,5},{7,6},{8,7},{9,8},{10,9... | collective-permute-start | bytes 393224 | tf_op jit(solution)/shard_map/ppermute | solution.py:143
  109.8 0.8 collective-permute-done.3
  110.5 1.7 collective-permute-done.4
  112.3 1.1 collective-permute-done.6
  113.4 5.2 %collective-permute-start.7 = (bf16[256,2048]{1,0:T(8,128)(2,1)S(1)}, bf16[256,2048]{1,0:T(8,128)(2,1)S(1)}, u32[]{:S(2)}, u32[]{:S(2)}) collective-permute-start(bf16[256,2048]{1,0:T(8,128)(2,1)S(1)} %fusion.27.mine), channel_id=1, source_target_pairs={{0,32},{32,0},{64,96},{96,64},{128,160},{160,128},{192,224},{224,1... | collective-permute-start | bytes 3145736 | tf_op jit(solution)/shard_map/ppermute | solution.py:158
  118.6 2.3 collective-permute-done.7.other
  120.9 2.0 shard_map.122
  122.9 2.3 collective-permute-start.8
  125.2 0.6 shard_map.123.keep
  125.8 1.7 collective-permute-done.8.gave
  127.5 0.4 shard_map.124
  127.9 4.7 %collective-permute-start.9 = (bf16[32,2048]{1,0:T(8,128)(2,1)S(1)}, bf16[32,2048]{1,0:T(8,128)(2,1)S(1)}, u32[]{:S(2)}, u32[]{:S(2)}) collective-permute-start(bf16[32,2048]{1,0:T(8,128)(2,1)S(1)} %get-tuple-element.31), channel_id=1, source_target_pairs={{0,28},{1,29},{2,30},{3,31},{4,0},{5,1},{6,2},{7,3},{8,4},{9,5},{1... | collective-permute-start | bytes 393224 | tf_op jit(solution)/shard_map/ppermute | solution.py:155
  132.7 2.6 %collective-permute-start.10 = (bf16[32,2048]{1,0:T(8,128)(2,1)S(1)}, bf16[32,2048]{1,0:T(8,128)(2,1)S(1)}, u32[]{:S(2)}, u32[]{:S(2)}) collective-permute-start(bf16[32,2048]{1,0:T(8,128)(2,1)S(1)} %get-tuple-element.32), channel_id=1, source_target_pairs={{0,29},{1,30},{2,31},{3,0},{4,1},{5,2},{6,3},{7,4},{8,5},{9,6},{10... | collective-permute-start | bytes 393224 | tf_op jit(solution)/shard_map/ppermute | solution.py:143
  135.3 4.4 %collective-permute-start.11 = (bf16[32,2048]{1,0:T(8,128)(2,1)S(1)}, bf16[32,2048]{1,0:T(8,128)(2,1)S(1)}, u32[]{:S(2)}, u32[]{:S(2)}) collective-permute-start(bf16[32,2048]{1,0:T(8,128)(2,1)S(1)} %get-tuple-element.33), channel_id=1, source_target_pairs={{0,3},{1,4},{2,5},{3,6},{4,7},{5,8},{6,9},{7,10},{8,11},{9,12},{10... | collective-permute-start | bytes 393224 | tf_op jit(solution)/shard_map/ppermute | solution.py:143
  139.8 4.4 %collective-permute-start.12 = (bf16[32,2048]{1,0:T(8,128)(2,1)S(1)}, bf16[32,2048]{1,0:T(8,128)(2,1)S(1)}, u32[]{:S(2)}, u32[]{:S(2)}) collective-permute-start(bf16[32,2048]{1,0:T(8,128)(2,1)S(1)} %get-tuple-element.34), channel_id=1, source_target_pairs={{0,30},{1,31},{2,0},{3,1},{4,2},{5,3},{6,4},{7,5},{8,6},{9,7},{10,... | collective-permute-start | bytes 393224 | tf_op jit(solution)/shard_map/ppermute | solution.py:143
  144.2 1.9 collective-permute-start.13
  146.2 6.4 %collective-permute-start.14 = (bf16[32,2048]{1,0:T(8,128)(2,1)S(1)}, bf16[32,2048]{1,0:T(8,128)(2,1)S(1)}, u32[]{:S(2)}, u32[]{:S(2)}) collective-permute-start(bf16[32,2048]{1,0:T(8,128)(2,1)S(1)} %get-tuple-element.36), channel_id=1, source_target_pairs={{0,31},{1,0},{2,1},{3,2},{4,3},{5,4},{6,5},{7,6},{8,7},{9,8},{10,9... | collective-permute-start | bytes 393224 | tf_op jit(solution)/shard_map/ppermute | solution.py:143
  152.6 1.9 collective-permute-start.15
  154.6 2.3 collective-permute-done.14
  156.9 2.6 %collective-permute-done.15 = bf16[32,2048]{1,0:T(8,128)(2,1)S(1)} collective-permute-done((bf16[32,2048]{1,0:T(8,128)(2,1)S(1)}, bf16[32,2048]{1,0:T(8,128)(2,1)S(1)}, u32[]{:S(2)}, u32[]{:S(2)}) %collective-permute-start.15) | collective-permute-done | bytes 131104 | tf_op jit(solution)/shard_map/ppermute | solution.py:143
  159.5 0.3 convolution_convert_fusion.2
  159.9 0.4 convolution_convert_fusion.4
  160.7 0.9 slice.270
  161.6 8.3 %all-to-all-start.2 = ((bf16[32,2,2176]{2,1,0:T(2,128)(2,1)}), bf16[32,2,2176]{2,1,0:T(2,128)(2,1)S(1)}, u32[]{:S(2)}, u32[]{:S(2)}) async-start(bf16[32,2,2176]{2,1,0:T(2,128)(2,1)} %slice.270), calls=%async_computation.2 | async-start | bytes 557056 | tf_op jit(solution)/shard_map/all_to_all | solution.py:262
  170.3 1.3 slice.257
  171.5 7.5 %all-to-all-done.2 = bf16[32,2,2176]{2,1,0:T(2,128)(2,1)S(1)} async-done(((bf16[32,2,2176]{2,1,0:T(2,128)(2,1)}), bf16[32,2,2176]{2,1,0:T(2,128)(2,1)S(1)}, u32[]{:S(2)}, u32[]{:S(2)}) %all-to-all-start.2) | async-done | bytes 278560 | tf_op jit(solution)/shard_map/all_to_all | solution.py:262
  179.1 3.7 %all-to-all-start.1 = ((bf16[32,6,2176]{2,1,0:T(8,128)(2,1)}), bf16[32,6,2176]{2,1,0:T(8,128)(2,1)S(1)}, u32[]{:S(2)}, u32[]{:S(2)}) async-start(bf16[32,6,2176]{2,1,0:T(8,128)(2,1)} %slice.257), calls=%async_computation.1 | async-start | bytes 2228224 | tf_op jit(solution)/shard_map/all_to_all | solution.py:262
  183.5 11.8 %collective-permute-start.18 = (bf16[8,4224]{1,0:T(8,128)(2,1)S(1)}, bf16[8,4224]{1,0:T(8,128)(2,1)S(1)}, u32[]{:S(2)}, u32[]{:S(2)}) collective-permute-start(bf16[8,4224]{1,0:T(8,128)(2,1)S(1)} %constant_dynamic-update-slice_fusion.16), channel_id=1, source_target_pairs={{0,16},{1,17},{2,18},{3,19},{4,20},{5,21},{6,22},{7,23},{8,24},{9,... | collective-permute-start | bytes 202760 | tf_op jit(solution)/shard_map/ppermute | solution.py:143
  195.3 5.2 %all-to-all-done.1 = bf16[32,6,2176]{2,1,0:T(8,128)(2,1)S(1)} async-done(((bf16[32,6,2176]{2,1,0:T(8,128)(2,1)}), bf16[32,6,2176]{2,1,0:T(8,128)(2,1)S(1)}, u32[]{:S(2)}, u32[]{:S(2)}) %all-to-all-start.1) | async-done | bytes 835616 | tf_op jit(solution)/shard_map/all_to_all | solution.py:262
  201.5 5.9 %collective-permute-start.16 = (bf16[8,4224]{1,0:T(8,128)(2,1)S(1)}, bf16[8,4224]{1,0:T(8,128)(2,1)S(1)}, u32[]{:S(2)}, u32[]{:S(2)}) collective-permute-start(bf16[8,4224]{1,0:T(8,128)(2,1)S(1)} %get-tuple-element.57), channel_id=1, source_target_pairs={{0,8},{1,9},{2,10},{3,11},{4,12},{5,13},{6,14},{7,15},{8,16},{9,17... | collective-permute-start | bytes 202760 | tf_op jit(solution)/shard_map/ppermute | solution.py:143
  207.4 8.1 %collective-permute-start.17 = (bf16[8,4224]{1,0:T(8,128)(2,1)S(1)}, bf16[8,4224]{1,0:T(8,128)(2,1)S(1)}, u32[]{:S(2)}, u32[]{:S(2)}) collective-permute-start(bf16[8,4224]{1,0:T(8,128)(2,1)S(1)} %get-tuple-element.58), channel_id=1, source_target_pairs={{0,24},{1,25},{2,26},{3,27},{4,28},{5,29},{6,30},{7,31},{8,0},{9,1... | collective-permute-start | bytes 202760 | tf_op jit(solution)/shard_map/ppermute | solution.py:143
  215.5 7.4 %collective-permute-done.16 = bf16[8,4224]{1,0:T(8,128)(2,1)S(1)} collective-permute-done((bf16[8,4224]{1,0:T(8,128)(2,1)S(1)}, bf16[8,4224]{1,0:T(8,128)(2,1)S(1)}, u32[]{:S(2)}, u32[]{:S(2)}) %collective-permute-start.16) | collective-permute-done | bytes 67616 | tf_op jit(solution)/shard_map/ppermute | solution.py:143
  223.0 8.1 %collective-permute-done.17 = bf16[8,4224]{1,0:T(8,128)(2,1)S(1)} collective-permute-done((bf16[8,4224]{1,0:T(8,128)(2,1)S(1)}, bf16[8,4224]{1,0:T(8,128)(2,1)S(1)}, u32[]{:S(2)}, u32[]{:S(2)}) %collective-permute-start.17) | collective-permute-done | bytes 67616 | tf_op jit(solution)/shard_map/ppermute | solution.py:143
  231.1 0.6 fusion.52
  231.8 0.6 slice.281
  (102 shorter events, 4.4 us)
Async XLA Ops:
  0.6 53.0 %copy-start.3 = (s32[4]{0:T(128)S(1)}, s32[4]{0:T(128)}, u32[]{:S(2)}) copy-start(s32[4]{0:T(128)} %constant.163.clone) | copy-start | bytes 52
  55.6 10.8 %copy-start.4 = (s32[8]{0:T(128)S(1)}, s32[8]{0:T(128)}, u32[]{:S(2)}) copy-start(s32[8]{0:T(128)} %constant.164.clone) | copy-start | bytes 100
  55.6 28.4 %all-to-all-start = ((bf16[32,8,2176]{2,1,0:T(8,128)(2,1)}), bf16[32,8,2176]{2,1,0:T(8,128)(2,1)S(1)}, u32[]{:S(2)}, u32[]{:S(2)}) async-start(bf16[32,8,2176]{2,1,0:T(8,128)(2,1)} %bitcast.7), calls=%async_computation | async-start | bytes 2228224 | tf_op jit(solution)/shard_map/all_to_all | solution.py:188
  85.3 35.7 %copy-start.2 = (bf16[1,1,256,2048]{3,2,1,0:T(8,128)(2,1)S(1)}, bf16[1,1,256,2048]{3,2,1,0:T(8,128)(2,1)}, u32[]{:S(2)}) copy-start(bf16[1,1,256,2048]{3,2,1,0:T(8,128)(2,1)} %param.19) | copy-start | bytes 3145732
  85.4 17.8 %collective-permute-start = (bf16[32,2048]{1,0:T(8,128)(2,1)S(1)}, bf16[32,2048]{1,0:T(8,128)(2,1)S(1)}, u32[]{:S(2)}, u32[]{:S(2)}) collective-permute-start(bf16[32,2048]{1,0:T(8,128)(2,1)S(1)} %get-tuple-element.44), channel_id=1, source_target_pairs={{0,4},{1,5},{2,6},{3,7},{4,8},{5,9},{6,10},{7,11},{8,12},{9,13},{1... | collective-permute-start | bytes 393224 | tf_op jit(solution)/shard_map/ppermute | solution.py:155
  87.4 18.9 %collective-permute-start.1 = (bf16[32,2048]{1,0:T(8,128)(2,1)S(1)}, bf16[32,2048]{1,0:T(8,128)(2,1)S(1)}, u32[]{:S(2)}, u32[]{:S(2)}) collective-permute-start(bf16[32,2048]{1,0:T(8,128)(2,1)S(1)} %get-tuple-element.45), channel_id=1, source_target_pairs={{0,3},{1,4},{2,5},{3,6},{4,7},{5,8},{6,9},{7,10},{8,11},{9,12},{10... | collective-permute-start | bytes 393224 | tf_op jit(solution)/shard_map/ppermute | solution.py:143
  90.9 18.8 %collective-permute-start.2 = (bf16[32,2048]{1,0:T(8,128)(2,1)S(1)}, bf16[32,2048]{1,0:T(8,128)(2,1)S(1)}, u32[]{:S(2)}, u32[]{:S(2)}) collective-permute-start(bf16[32,2048]{1,0:T(8,128)(2,1)S(1)} %get-tuple-element.46), channel_id=1, source_target_pairs={{0,29},{1,30},{2,31},{3,0},{4,1},{5,2},{6,3},{7,4},{8,5},{9,6},{10... | collective-permute-start | bytes 393224 | tf_op jit(solution)/shard_map/ppermute | solution.py:143
  95.7 14.8 %collective-permute-start.3 = (bf16[32,2048]{1,0:T(8,128)(2,1)S(1)}, bf16[32,2048]{1,0:T(8,128)(2,1)S(1)}, u32[]{:S(2)}, u32[]{:S(2)}) collective-permute-start(bf16[32,2048]{1,0:T(8,128)(2,1)S(1)} %get-tuple-element.47), channel_id=1, source_target_pairs={{0,2},{1,3},{2,4},{3,5},{4,6},{5,7},{6,8},{7,9},{8,10},{9,11},{10,... | collective-permute-start | bytes 393224 | tf_op jit(solution)/shard_map/ppermute | solution.py:143
  99.7 12.5 %collective-permute-start.4 = (bf16[32,2048]{1,0:T(8,128)(2,1)S(1)}, bf16[32,2048]{1,0:T(8,128)(2,1)S(1)}, u32[]{:S(2)}, u32[]{:S(2)}) collective-permute-start(bf16[32,2048]{1,0:T(8,128)(2,1)S(1)} %get-tuple-element.48), channel_id=1, source_target_pairs={{0,30},{1,31},{2,0},{3,1},{4,2},{5,3},{6,4},{7,5},{8,6},{9,7},{10,... | collective-permute-start | bytes 393224 | tf_op jit(solution)/shard_map/ppermute | solution.py:143
  103.1 9.1 %collective-permute-start.5 = (bf16[32,2048]{1,0:T(8,128)(2,1)S(1)}, bf16[32,2048]{1,0:T(8,128)(2,1)S(1)}, u32[]{:S(2)}, u32[]{:S(2)}) collective-permute-start(bf16[32,2048]{1,0:T(8,128)(2,1)S(1)} %get-tuple-element.49), channel_id=1, source_target_pairs={{0,1},{1,2},{2,3},{3,4},{4,5},{5,6},{6,7},{7,8},{8,9},{9,10},{10,1... | collective-permute-start | bytes 393224 | tf_op jit(solution)/shard_map/ppermute | solution.py:143
  106.3 7.1 %collective-permute-start.6 = (bf16[32,2048]{1,0:T(8,128)(2,1)S(1)}, bf16[32,2048]{1,0:T(8,128)(2,1)S(1)}, u32[]{:S(2)}, u32[]{:S(2)}) collective-permute-start(bf16[32,2048]{1,0:T(8,128)(2,1)S(1)} %get-tuple-element.43), channel_id=1, source_target_pairs={{0,31},{1,0},{2,1},{3,2},{4,3},{5,4},{6,5},{7,6},{8,7},{9,8},{10,9... | collective-permute-start | bytes 393224 | tf_op jit(solution)/shard_map/ppermute | solution.py:143
  109.7 11.2 %copy-start = (bf16[1,1,2048,256]{3,2,1,0:T(8,128)(2,1)S(1)}, bf16[1,1,2048,256]{3,2,1,0:T(8,128)(2,1)}, u32[]{:S(2)}) copy-start(bf16[1,1,2048,256]{3,2,1,0:T(8,128)(2,1)} %param.17) | copy-start | bytes 3145732
  109.7 11.2 %copy-start.1 = (bf16[1,1,2048,256]{3,2,1,0:T(8,128)(2,1)S(1)}, bf16[1,1,2048,256]{3,2,1,0:T(8,128)(2,1)}, u32[]{:S(2)}) copy-start(bf16[1,1,2048,256]{3,2,1,0:T(8,128)(2,1)} %param.18) | copy-start | bytes 3145732
  113.4 7.5 %collective-permute-start.7 = (bf16[256,2048]{1,0:T(8,128)(2,1)S(1)}, bf16[256,2048]{1,0:T(8,128)(2,1)S(1)}, u32[]{:S(2)}, u32[]{:S(2)}) collective-permute-start(bf16[256,2048]{1,0:T(8,128)(2,1)S(1)} %fusion.27.mine), channel_id=1, source_target_pairs={{0,32},{32,0},{64,96},{96,64},{128,160},{160,128},{192,224},{224,1... | collective-permute-start | bytes 3145736 | tf_op jit(solution)/shard_map/ppermute | solution.py:158
  122.9 4.6 %collective-permute-start.8 = (bf16[256,2048]{1,0:T(8,128)(2,1)S(1)}, bf16[256,2048]{1,0:T(8,128)(2,1)S(1)}, u32[]{:S(2)}, u32[]{:S(2)}) collective-permute-start(bf16[256,2048]{1,0:T(8,128)(2,1)S(1)} %get-tuple-element.30), channel_id=1, source_target_pairs={{0,32},{32,0},{64,96},{96,64},{128,160},{160,128},{192,224},{224,1... | collective-permute-start | bytes 3145736 | tf_op jit(solution)/shard_map/ppermute | solution.py:158
  127.9 18.3 %collective-permute-start.9 = (bf16[32,2048]{1,0:T(8,128)(2,1)S(1)}, bf16[32,2048]{1,0:T(8,128)(2,1)S(1)}, u32[]{:S(2)}, u32[]{:S(2)}) collective-permute-start(bf16[32,2048]{1,0:T(8,128)(2,1)S(1)} %get-tuple-element.31), channel_id=1, source_target_pairs={{0,28},{1,29},{2,30},{3,31},{4,0},{5,1},{6,2},{7,3},{8,4},{9,5},{1... | collective-permute-start | bytes 393224 | tf_op jit(solution)/shard_map/ppermute | solution.py:155
  132.7 19.9 %collective-permute-start.10 = (bf16[32,2048]{1,0:T(8,128)(2,1)S(1)}, bf16[32,2048]{1,0:T(8,128)(2,1)S(1)}, u32[]{:S(2)}, u32[]{:S(2)}) collective-permute-start(bf16[32,2048]{1,0:T(8,128)(2,1)S(1)} %get-tuple-element.32), channel_id=1, source_target_pairs={{0,29},{1,30},{2,31},{3,0},{4,1},{5,2},{6,3},{7,4},{8,5},{9,6},{10... | collective-permute-start | bytes 393224 | tf_op jit(solution)/shard_map/ppermute | solution.py:143
  135.3 19.2 %collective-permute-start.11 = (bf16[32,2048]{1,0:T(8,128)(2,1)S(1)}, bf16[32,2048]{1,0:T(8,128)(2,1)S(1)}, u32[]{:S(2)}, u32[]{:S(2)}) collective-permute-start(bf16[32,2048]{1,0:T(8,128)(2,1)S(1)} %get-tuple-element.33), channel_id=1, source_target_pairs={{0,3},{1,4},{2,5},{3,6},{4,7},{5,8},{6,9},{7,10},{8,11},{9,12},{10... | collective-permute-start | bytes 393224 | tf_op jit(solution)/shard_map/ppermute | solution.py:143
  139.8 14.8 %collective-permute-start.12 = (bf16[32,2048]{1,0:T(8,128)(2,1)S(1)}, bf16[32,2048]{1,0:T(8,128)(2,1)S(1)}, u32[]{:S(2)}, u32[]{:S(2)}) collective-permute-start(bf16[32,2048]{1,0:T(8,128)(2,1)S(1)} %get-tuple-element.34), channel_id=1, source_target_pairs={{0,30},{1,31},{2,0},{3,1},{4,2},{5,3},{6,4},{7,5},{8,6},{9,7},{10,... | collective-permute-start | bytes 393224 | tf_op jit(solution)/shard_map/ppermute | solution.py:143
  144.2 10.4 %collective-permute-start.13 = (bf16[32,2048]{1,0:T(8,128)(2,1)S(1)}, bf16[32,2048]{1,0:T(8,128)(2,1)S(1)}, u32[]{:S(2)}, u32[]{:S(2)}) collective-permute-start(bf16[32,2048]{1,0:T(8,128)(2,1)S(1)} %get-tuple-element.35), channel_id=1, source_target_pairs={{0,2},{1,3},{2,4},{3,5},{4,6},{5,7},{6,8},{7,9},{8,10},{9,11},{10,... | collective-permute-start | bytes 393224 | tf_op jit(solution)/shard_map/ppermute | solution.py:143
  146.2 10.8 %collective-permute-start.14 = (bf16[32,2048]{1,0:T(8,128)(2,1)S(1)}, bf16[32,2048]{1,0:T(8,128)(2,1)S(1)}, u32[]{:S(2)}, u32[]{:S(2)}) collective-permute-start(bf16[32,2048]{1,0:T(8,128)(2,1)S(1)} %get-tuple-element.36), channel_id=1, source_target_pairs={{0,31},{1,0},{2,1},{3,2},{4,3},{5,4},{6,5},{7,6},{8,7},{9,8},{10,9... | collective-permute-start | bytes 393224 | tf_op jit(solution)/shard_map/ppermute | solution.py:143
  152.6 6.9 %collective-permute-start.15 = (bf16[32,2048]{1,0:T(8,128)(2,1)S(1)}, bf16[32,2048]{1,0:T(8,128)(2,1)S(1)}, u32[]{:S(2)}, u32[]{:S(2)}) collective-permute-start(bf16[32,2048]{1,0:T(8,128)(2,1)S(1)} %get-tuple-element.37), channel_id=1, source_target_pairs={{0,1},{1,2},{2,3},{3,4},{4,5},{5,6},{6,7},{7,8},{8,9},{9,10},{10,1... | collective-permute-start | bytes 393224 | tf_op jit(solution)/shard_map/ppermute | solution.py:143
  161.6 17.5 %all-to-all-start.2 = ((bf16[32,2,2176]{2,1,0:T(2,128)(2,1)}), bf16[32,2,2176]{2,1,0:T(2,128)(2,1)S(1)}, u32[]{:S(2)}, u32[]{:S(2)}) async-start(bf16[32,2,2176]{2,1,0:T(2,128)(2,1)} %slice.270), calls=%async_computation.2 | async-start | bytes 557056 | tf_op jit(solution)/shard_map/all_to_all | solution.py:262
  179.1 21.5 %all-to-all-start.1 = ((bf16[32,6,2176]{2,1,0:T(8,128)(2,1)}), bf16[32,6,2176]{2,1,0:T(8,128)(2,1)S(1)}, u32[]{:S(2)}, u32[]{:S(2)}) async-start(bf16[32,6,2176]{2,1,0:T(8,128)(2,1)} %slice.257), calls=%async_computation.1 | async-start | bytes 2228224 | tf_op jit(solution)/shard_map/all_to_all | solution.py:262
  183.5 32.0 %collective-permute-start.18 = (bf16[8,4224]{1,0:T(8,128)(2,1)S(1)}, bf16[8,4224]{1,0:T(8,128)(2,1)S(1)}, u32[]{:S(2)}, u32[]{:S(2)}) collective-permute-start(bf16[8,4224]{1,0:T(8,128)(2,1)S(1)} %constant_dynamic-update-slice_fusion.16), channel_id=1, source_target_pairs={{0,16},{1,17},{2,18},{3,19},{4,20},{5,21},{6,22},{7,23},{8,24},{9,... | collective-permute-start | bytes 202760 | tf_op jit(solution)/shard_map/ppermute | solution.py:143
  201.5 21.5 %collective-permute-start.16 = (bf16[8,4224]{1,0:T(8,128)(2,1)S(1)}, bf16[8,4224]{1,0:T(8,128)(2,1)S(1)}, u32[]{:S(2)}, u32[]{:S(2)}) collective-permute-start(bf16[8,4224]{1,0:T(8,128)(2,1)S(1)} %get-tuple-element.57), channel_id=1, source_target_pairs={{0,8},{1,9},{2,10},{3,11},{4,12},{5,13},{6,14},{7,15},{8,16},{9,17... | collective-permute-start | bytes 202760 | tf_op jit(solution)/shard_map/ppermute | solution.py:143
  207.4 23.7 %collective-permute-start.17 = (bf16[8,4224]{1,0:T(8,128)(2,1)S(1)}, bf16[8,4224]{1,0:T(8,128)(2,1)S(1)}, u32[]{:S(2)}, u32[]{:S(2)}) collective-permute-start(bf16[8,4224]{1,0:T(8,128)(2,1)S(1)} %get-tuple-element.58), channel_id=1, source_target_pairs={{0,24},{1,25},{2,26},{3,27},{4,28},{5,29},{6,30},{7,31},{8,0},{9,1... | collective-permute-start | bytes 202760 | tf_op jit(solution)/shard_map/ppermute | solution.py:143

commit v6 on v5

--- a/solution.py
+++ b/solution.py
@@ -142,17 +142,18 @@
     def shift(array, by):
         return lax.ppermute(array, "local", [(i, (i + by) % n_local) for i in range(n_local)])
 
-    def hop(array, step, sign):
-        if step == 0:
-            return array
-        if step != near // 2:
-            return shift(array, sign * step)
+    def split(array, step):
         pairs = [
-            (g * n_local + i, g * n_local + (i + sign * (step if g % 2 == 0 else -step)) % n_local)
+            (g * n_local + i, g * n_local + (i + (step if g % 2 == 0 else -step)) % n_local)
             for g in range(n_group)
             for i in range(n_local)
         ]
         return lax.ppermute(array, ("group", "local"), pairs)
+
+    def hop(array, step, sign):
+        if step == 0:
+            return array
+        return split(array, sign * step) if step == near // 2 else shift(array, sign * step)
 
     def swap(array):
         return lax.ppermute(array, "group", [(i, i ^ 1) for i in range(n_group)])
@@ -170,13 +171,19 @@
         own, "local", axis=0, tiled=True, axis_index_groups=[[b + near * f for f in range(far)] for b in range(near)]
     )
 
-    codes = rows[:, 2 * width + 3 * topk : 2 * width + 3 * topk + groups].T
-    codes = codes.astype(F32)[:, None, None, :] == jnp.arange(per_group, dtype=F32)[None, None, :, None]
+    def codes_of(info):
+        codes = info[:, 3 * topk : 3 * topk + groups].T.astype(F32)
+        return codes[:, None, None, :] == jnp.arange(per_group, dtype=F32)[None, None, :, None]
+
+    info = rows[:, 2 * width :]
+    partner = swap(info)
     row_plane = jnp.arange(far * tok, dtype=jnp.int32) // tok
     away = sorted(range(far), key=lambda f: -min(f, far - f))
     planes = (z // near + jnp.array(away, jnp.int32)) % far
-    chooser = (codes & (row_plane[None, :] == planes[:, None])[None, :, None, :]).astype(BF)
-    chooser = chooser.reshape(groups * far * per_group, far * tok)
+    def chooser_of(info):
+        return (codes_of(info) & (row_plane[None, :] == planes[:, None])[None, :, None, :]).astype(BF)
+
+    chooser = chooser_of(info).reshape(groups * far * per_group, far * tok)
     parts = []
     for c in range(2):
         piece = jnp.concatenate(
@@ -190,8 +197,8 @@
     got = got.reshape(n_rows, width + META)
 
     steps = [near // 2] + [s for d in range(near // 2 - 1, 0, -1) for s in (d, -d)] + [0]
-    info = got[:, width:].T
-    row_group, row_pos, row_gate = info[:topk], info[topk : 2 * topk], info[2 * topk : 3 * topk]
+    facts = got[:, width:].T
+    row_group, row_pos, row_gate = facts[:topk], facts[topk : 2 * topk], facts[2 * topk : 3 * topk]
     turned = jnp.where(core == 0, near // 2, n_local - near // 2)
     target = jnp.array([s % n_local for s in steps], jnp.int32).at[0].set(turned)
     target = ((z + target) % n_local).astype(BF)
@@ -254,36 +261,75 @@
     term_k = jnp.sum(jnp.where(picked, term_at[None], 0.0), axis=1) / row_gate.astype(F32)
     term_k = jnp.pad(term_k, ((0, META - topk), (0, 0))).T
     send = jnp.concatenate([row_out.astype(BF), row_back.astype(BF), term_k.astype(BF)], axis=1)
-    send = send.reshape(n_group, far * per_group, width + META)
-
-    lone = jnp.sum(chooser.reshape(groups, far, per_group, far, tok), axis=3)
-
-    def to_tokens(low, high):
-        got = lax.all_to_all(
-            send[:, low * per_group : high * per_group], "group", split_axis=0, concat_axis=0, tiled=True
-        )
-        count = high - low
-        picks = lone[:, low:high, :, None, :] * jnp.eye(count, dtype=BF)[None, :, None, :, None]
-        picks = picks.reshape(groups * count * per_group, count * tok)
-        got = got.reshape(groups, 2, count * per_group, width + META)
-        sums = [dot(picks, got[:, c].reshape(groups * count * per_group, width + META), ((0,), (0,))) for c in range(2)]
-        return jnp.concatenate(
-            [
-                sums[0][:, :half],
-                sums[1][:, :half],
-                sums[0][:, half:width],
-                sums[1][:, half:width],
-                sums[0][:, width:] + sums[1][:, width:],
-            ],
-            axis=1,
-        )
-
-    first = shift(to_tokens(0, 1).astype(BF), near * away[0])
-    full = to_tokens(1, far).reshape(far - 1, tok, 2 * width + META)
-    total = full[far - 2]
-    for q in range(1, far - 1):
-        total = total + shift(full[q - 1].astype(BF), near * away[q]).astype(F32)
-    total = total + first.astype(F32)
+
+    source = jnp.arange(n_rows, dtype=jnp.int32).reshape(groups, 2, far, per_group)
+
+    def moved(order):
+        order = order.reshape(-1)
+        return dot((order[:, None] == jnp.arange(n_rows, dtype=jnp.int32)[None, :]).astype(BF), send, ((1,), (0,))).astype(BF)
+
+    def lone_of(info):
+        return jnp.sum(chooser_of(info).reshape(groups, far, per_group, far, tok), axis=3)
+
+    def diagonal(picks):
+        picks = picks[:, :, :, None, :] * jnp.eye(2, dtype=BF)[None, :, None, :, None]
+        return picks.reshape(groups, 2 * per_group, 2 * tok)
+
+    def gathered(array, picks):
+        count, lanes = picks.shape[1], array.shape[-1]
+        array = array.reshape(n_group, count, lanes)
+        array = lax.all_to_all(array, "group", split_axis=0, concat_axis=0, tiled=True)
+        array = array.reshape(groups, 2, count, lanes)
+        picks = picks.reshape(groups * count, -1)
+        return [dot(picks, array[:, c].reshape(groups * count, lanes), ((0,), (0,))) for c in range(2)]
+
+    mine_lone, partner_lone = lone_of(info), lone_of(partner)
+    both = jnp.stack(
+        [jnp.where(core == 0, mine_lone, partner_lone), jnp.where(core == 0, partner_lone, mine_lone)], axis=1
+    )
+    order = jnp.stack([source[:, :, 0], source[:, :, 0]], axis=1).reshape(-1)
+    outs = moved(order)
+    upward = (jnp.arange(order.shape[0], dtype=jnp.int32) // (2 * per_group) % 2 == 0)[:, None]
+    outs = jnp.concatenate([jnp.where(upward, outs[:, :half], outs[:, half:width]), outs[:, width:]], axis=1)
+    sums = gathered(outs, diagonal(both[:, :, 0]))
+    relay = jnp.concatenate([sums[0][:, :half], sums[1][:, :half], sums[0][:, half:] + sums[1][:, half:]], axis=1)
+    relay = split(relay.astype(BF), near).astype(F32)
+
+    sides = jnp.stack([source[:, :, 1], source[:, :, 2]], axis=1).reshape(groups, 2, 2 * per_group)
+    blank = jnp.full((groups, 2, per_group), n_rows, jnp.int32)
+    sides = jnp.concatenate([source[:, :, far - 1], sides, blank], axis=2)
+    beside = diagonal(jnp.where(core == 0, both[:, :, 1], both[:, :, 2]))
+    picks = jnp.concatenate(
+        [
+            jnp.pad(mine_lone[:, far - 1], ((0, 0), (0, 0), (0, 2 * tok))),
+            jnp.pad(beside, ((0, 0), (0, per_group), (tok, 0))),
+        ],
+        axis=1,
+    )
+    sums = gathered(moved(sides), picks)
+    full = jnp.concatenate(
+        [
+            sums[0][:, :half],
+            sums[1][:, :half],
+            sums[0][:, half:width],
+            sums[1][:, half:width],
+            sums[0][:, width:] + sums[1][:, width:],
+        ],
+        axis=1,
+    )
+    even = core == 0
+    pair = full[tok:] + jnp.concatenate(
+        [
+            jnp.where(even, relay[:, :width], 0.0),
+            jnp.where(even, 0.0, relay[:, :width]),
+            jnp.where(even, 0.0, relay[:, width:]),
+        ],
+        axis=1,
+    )
+    pair = split(pair.astype(BF), near)
+    theirs = swap(jnp.where(even, pair[tok:], pair[:tok]))
+    ours = jnp.where(even, pair[:tok], pair[tok:])
+    total = full[:tok] + ours.astype(F32) + theirs.astype(F32)
     return (
         total[:, :width].astype(BF),
         total[:, width : 2 * width].astype(BF),

time: 233 us -> 244 us (1.047)
  local copies, waits for them, and re-layouts: 4.74 us -> 11.7 us
  starting transfers between devices: 107 us -> 101 us
  other arithmetic: 2.49 us -> 6.69 us
  Pallas kernels: 4.69 us -> 8.22 us
  matrix products: 2.88 us -> 5.47 us
    ppermute x15 -> x12, starting transfers between devices: 69.7 us -> 45 us  [shift(): lax.ppermute(array, 'local', [(i, (i + by) % n_local) for i in range(n_lo...]
    ppermute x2 -> x4, waiting for transfers between devices: 0.01 us -> 19.9 us  [split(): return lax.ppermute(array, ('group', 'local'), pairs)]
    ppermute x2 -> x4, starting transfers between devices: 6.71 us -> 22.3 us  [split(): return lax.ppermute(array, ('group', 'local'), pairs)]
    ppermute x15 -> x12, waiting for transfers between devices: 24 us -> 9.48 us  [shift(): lax.ppermute(array, 'local', [(i, (i + by) % n_local) for i in range(n_lo...]
    ppermute x2 -> x4, starting transfers between devices: 7.53 us -> 12.9 us  [swap(): return lax.ppermute(array, 'group', [(i, i ^ 1) for i in range(n_group)])]
    unnamed x34 -> x73, local copies, waits for them, and re-layouts: 0.42 us -> 3.98 us
    pallas_call x3, Pallas kernels: 2.94 us -> 6.46 us  [whole(): pl.pallas_call(kernel, out_shape=outs, in_specs=[smem] * scalars + [vmem]...]
    ppermute x2 -> x4, waiting for transfers between devices: 3.92 us -> 1.23 us  [swap(): return lax.ppermute(array, 'group', [(i, i ^ 1) for i in range(n_group)])]
  transfers between devices with their start and end apart: 22 -> 23, of which waited for: 12 -> 13; matrix products, arithmetic and copies ran while one was open for 1% -> 5% of each run, Pallas kernels for 0% -> 2%
where the time goes in v6:
time: 244 us; the launch traced here: 243 us
  starting transfers between devices  101 us (41%)
  waiting for transfers between devices  56.1 us (23%)
  blocking collectives  51 us (21%)
  local copies, waits for them, and re-layouts  11.7 us (5%)
  Pallas kernels  8.22 us (3%)
  other arithmetic  6.69 us (3%)
  matrix products  5.47 us (2%)
    all_gather x1, blocking collectives, body(): lax.all_gather(own, 'local', axis=0, tiled=True, axis_index_groups=[[b +...  51 us
    ppermute x12, starting transfers between devices, shift(): lax.ppermute(array, 'local', [(i, (i + by) % n_local) for i in range(n_lo...  45 us
    ppermute x4, starting transfers between devices, split(): return lax.ppermute(array, ('group', 'local'), pairs)  22.3 us
    ppermute x4, waiting for transfers between devices, split(): return lax.ppermute(array, ('group', 'local'), pairs)  19.9 us
    all_to_all x1, waiting for transfers between devices, body(): got = lax.all_to_all(send, 'group', split_axis=0, concat_axis=0, tiled=True)  15.3 us
    ppermute x4, starting transfers between devices, swap(): return lax.ppermute(array, 'group', [(i, i ^ 1) for i in range(n_group)])  12.9 us
    all_to_all x1, starting transfers between devices, body(): got = lax.all_to_all(send, 'group', split_axis=0, concat_axis=0, tiled=True)  10.7 us
    all_to_all x2, starting transfers between devices, gathered(): lax.all_to_all(array, 'group', split_axis=0, concat_axis=0, tiled=True)  10.4 us
  transfers between devices with their start and end apart: 23, of which 13 were waited for; matrix products, arithmetic and copies ran while one was open for 5% of the time, Pallas kernels for 2%

profile of v6, /device:TPU:1, one launch (start us, length us, event | category | flops | bytes accessed | tf_op | source)
XLA Modules:
  0.0 242.6 jit_solution(15339947213560597611)
XLA Ops:
  0.7 1.8 shard_map.121
  2.4 51.0 %all_gather.3 = bf16[32,4224]{1,0:T(8,128)(2,1)S(1)} all-gather(bf16[8,4224]{1,0:T(8,128)(2,1)} %shard_map.121), channel_id=1, replica_groups={{0,8,16,24},{1,9,17,25},{2,10,18,26},{3,11,19,27},{4,12,20,28},{5,13,21..., dimensions={0}, use_global_device_ids=true | all-gather | bytes 337920 | tf_op jit(solution)/shard_map/all_gather | solution.py:170
  54.7 1.0 fusion.1
  55.7 1.1 pad_maximum_fusion
  56.9 10.7 %all-to-all-start = ((bf16[32,8,2176]{2,1,0:T(8,128)(2,1)}), bf16[32,8,2176]{2,1,0:T(8,128)(2,1)S(1)}, u32[]{:S(2)}, u32[]{:S(2)}) async-start(bf16[32,8,2176]{2,1,0:T(8,128)(2,1)} %bitcast.18), calls=%async_computation | async-start | bytes 2228224 | tf_op jit(solution)/shard_map/all_to_all | solution.py:195
  67.6 2.1 collective-permute-start
  69.9 15.3 %all-to-all-done = bf16[32,8,2176]{2,1,0:T(8,128)(2,1)S(1)} async-done(((bf16[32,8,2176]{2,1,0:T(8,128)(2,1)}), bf16[32,8,2176]{2,1,0:T(8,128)(2,1)S(1)}, u32[]{:S(2)}, u32[]{:S(2)}) %all-to-all-start) | async-done | bytes 1114144 | tf_op jit(solution)/shard_map/all_to_all | solution.py:195
  87.1 1.9 collective-permute-start.1
  89.0 3.4 %collective-permute-start.2 = (bf16[32,2048]{1,0:T(8,128)(2,1)S(1)}, bf16[32,2048]{1,0:T(8,128)(2,1)S(1)}, u32[]{:S(2)}, u32[]{:S(2)}) collective-permute-start(bf16[32,2048]{1,0:T(8,128)(2,1)S(1)} %get-tuple-element.45), channel_id=1, source_target_pairs={{0,3},{1,4},{2,5},{3,6},{4,7},{5,8},{6,9},{7,10},{8,11},{9,12},{10... | collective-permute-start | bytes 393224 | tf_op jit(solution)/shard_map/ppermute | solution.py:143
  92.5 4.8 %collective-permute-start.3 = (bf16[32,2048]{1,0:T(8,128)(2,1)S(1)}, bf16[32,2048]{1,0:T(8,128)(2,1)S(1)}, u32[]{:S(2)}, u32[]{:S(2)}) collective-permute-start(bf16[32,2048]{1,0:T(8,128)(2,1)S(1)} %get-tuple-element.46), channel_id=1, source_target_pairs={{0,29},{1,30},{2,31},{3,0},{4,1},{5,2},{6,3},{7,4},{8,5},{9,6},{10... | collective-permute-start | bytes 393224 | tf_op jit(solution)/shard_map/ppermute | solution.py:143
  97.3 4.0 %collective-permute-start.4 = (bf16[32,2048]{1,0:T(8,128)(2,1)S(1)}, bf16[32,2048]{1,0:T(8,128)(2,1)S(1)}, u32[]{:S(2)}, u32[]{:S(2)}) collective-permute-start(bf16[32,2048]{1,0:T(8,128)(2,1)S(1)} %get-tuple-element.47), channel_id=1, source_target_pairs={{0,2},{1,3},{2,4},{3,5},{4,6},{5,7},{6,8},{7,9},{8,10},{9,11},{10,... | collective-permute-start | bytes 393224 | tf_op jit(solution)/shard_map/ppermute | solution.py:143
  101.4 3.4 %collective-permute-start.5 = (bf16[32,2048]{1,0:T(8,128)(2,1)S(1)}, bf16[32,2048]{1,0:T(8,128)(2,1)S(1)}, u32[]{:S(2)}, u32[]{:S(2)}) collective-permute-start(bf16[32,2048]{1,0:T(8,128)(2,1)S(1)} %get-tuple-element.48), channel_id=1, source_target_pairs={{0,30},{1,31},{2,0},{3,1},{4,2},{5,3},{6,4},{7,5},{8,6},{9,7},{10,... | collective-permute-start | bytes 393224 | tf_op jit(solution)/shard_map/ppermute | solution.py:143
  104.8 1.6 collective-permute-done.2
  106.4 1.9 collective-permute-start.6
  108.4 4.6 %collective-permute-start.7 = (bf16[32,2048]{1,0:T(8,128)(2,1)S(1)}, bf16[32,2048]{1,0:T(8,128)(2,1)S(1)}, u32[]{:S(2)}, u32[]{:S(2)}) collective-permute-start(bf16[32,2048]{1,0:T(8,128)(2,1)S(1)} %get-tuple-element.43), channel_id=1, source_target_pairs={{0,31},{1,0},{2,1},{3,2},{4,3},{5,4},{6,5},{7,6},{8,7},{9,8},{10,9... | collective-permute-start | bytes 393224 | tf_op jit(solution)/shard_map/ppermute | solution.py:143
  113.0 1.2 collective-permute-done.5
  114.2 1.7 collective-permute-done.7
  116.0 7.0 %collective-permute-start.8 = (bf16[256,2048]{1,0:T(8,128)(2,1)S(1)}, bf16[256,2048]{1,0:T(8,128)(2,1)}, u32[]{:S(2)}, u32[]{:S(2)}) collective-permute-start(bf16[256,2048]{1,0:T(8,128)(2,1)S(1)} %fusion.30.mine), channel_id=1, source_target_pairs={{0,32},{32,0},{64,96},{96,64},{128,160},{160,128},{192,224},{224,1... | collective-permute-start | bytes 3145736 | tf_op jit(solution)/shard_map/ppermute | solution.py:159
  126.1 1.2 copy-done.2
  127.3 4.2 %shard_map.122 = (bf16[256,256]{1,0:T(8,128)(2,1)S(1)}, bf16[256,256]{1,0:T(8,128)(2,1)S(1)}, bf16[256,256]{1,0:T(8,128)(2,1)S(1)}, bf16[256,2048]{1,0:T(8,128)(2,1)}) custom-call(s32[1]{0:T(128)} %bitcast.24.core_ref, bf16[256,2048]{1,0:T(8,128)(2,1)S(1)} %fusion.30.mine, bf16[256,2048]{1,0:T(8,128)(2,1)} %collective-permute-done.8.other, ...), custom_call_target="tpu_custom_call" | custom-call | flops 1207959552 | bytes 5242884 | tf_op jit(solution)/shard_map/pallas_call | solution.py:23
  131.6 1.9 collective-permute-start.9
  133.5 0.8 convert_bitcast_fusion.2
  135.6 1.4 copy.72
  137.0 1.4 broadcast_multiply_fusion
  138.4 1.2 copy-done.3
  140.2 1.7 shard_map.124
  141.9 3.5 %collective-permute-start.10 = (bf16[32,2048]{1,0:T(8,128)(2,1)S(1)}, bf16[32,2048]{1,0:T(8,128)(2,1)S(1)}, u32[]{:S(2)}, u32[]{:S(2)}) collective-permute-start(bf16[32,2048]{1,0:T(8,128)(2,1)S(1)} %get-tuple-element.31), channel_id=1, source_target_pairs={{0,28},{1,29},{2,30},{3,31},{4,0},{5,1},{6,2},{7,3},{8,4},{9,5},{1... | collective-permute-start | bytes 393224 | tf_op jit(solution)/shard_map/ppermute | solution.py:151
  145.5 3.2 %collective-permute-start.11 = (bf16[32,2048]{1,0:T(8,128)(2,1)S(1)}, bf16[32,2048]{1,0:T(8,128)(2,1)S(1)}, u32[]{:S(2)}, u32[]{:S(2)}) collective-permute-start(bf16[32,2048]{1,0:T(8,128)(2,1)S(1)} %get-tuple-element.32), channel_id=1, source_target_pairs={{0,29},{1,30},{2,31},{3,0},{4,1},{5,2},{6,3},{7,4},{8,5},{9,6},{10... | collective-permute-start | bytes 393224 | tf_op jit(solution)/shard_map/ppermute | solution.py:143
  148.7 3.9 %collective-permute-start.12 = (bf16[32,2048]{1,0:T(8,128)(2,1)S(1)}, bf16[32,2048]{1,0:T(8,128)(2,1)S(1)}, u32[]{:S(2)}, u32[]{:S(2)}) collective-permute-start(bf16[32,2048]{1,0:T(8,128)(2,1)S(1)} %get-tuple-element.33), channel_id=1, source_target_pairs={{0,3},{1,4},{2,5},{3,6},{4,7},{5,8},{6,9},{7,10},{8,11},{9,12},{10... | collective-permute-start | bytes 393224 | tf_op jit(solution)/shard_map/ppermute | solution.py:143
  152.6 6.0 %collective-permute-start.13 = (bf16[32,2048]{1,0:T(8,128)(2,1)S(1)}, bf16[32,2048]{1,0:T(8,128)(2,1)S(1)}, u32[]{:S(2)}, u32[]{:S(2)}) collective-permute-start(bf16[32,2048]{1,0:T(8,128)(2,1)S(1)} %get-tuple-element.34), channel_id=1, source_target_pairs={{0,30},{1,31},{2,0},{3,1},{4,2},{5,3},{6,4},{7,5},{8,6},{9,7},{10,... | collective-permute-start | bytes 393224 | tf_op jit(solution)/shard_map/ppermute | solution.py:143
  158.6 1.9 collective-permute-start.14
  160.5 6.0 %collective-permute-start.15 = (bf16[32,2048]{1,0:T(8,128)(2,1)S(1)}, bf16[32,2048]{1,0:T(8,128)(2,1)S(1)}, u32[]{:S(2)}, u32[]{:S(2)}) collective-permute-start(bf16[32,2048]{1,0:T(8,128)(2,1)S(1)} %get-tuple-element.36), channel_id=1, source_target_pairs={{0,31},{1,0},{2,1},{3,2},{4,3},{5,4},{6,5},{7,6},{8,7},{9,8},{10,9... | collective-permute-start | bytes 393224 | tf_op jit(solution)/shard_map/ppermute | solution.py:143
  166.6 1.9 collective-permute-start.16
  169.1 1.9 collective-permute-done.14
  171.1 1.1 collective-permute-done.15
  172.2 1.3 collective-permute-done.16
  176.2 0.8 reshape.494
  177.0 6.7 %all-to-all-start.2 = ((bf16[32,4,1152]{2,1,0:T(4,128)(2,1)}), bf16[32,4,1152]{2,1,0:T(4,128)(2,1)S(1)}, u32[]{:S(2)}, u32[]{:S(2)}) async-start(bf16[32,4,1152]{2,1,0:T(4,128)(2,1)} %reshape.494), calls=%async_computation.2 | async-start | bytes 589824 | tf_op jit(solution)/shard_map/all_to_all | solution.py:281
  184.5 1.5 fusion
  186.0 7.0 %all-to-all-done.2 = bf16[32,4,1152]{2,1,0:T(4,128)(2,1)S(1)} async-done(((bf16[32,4,1152]{2,1,0:T(4,128)(2,1)}), bf16[32,4,1152]{2,1,0:T(4,128)(2,1)S(1)}, u32[]{:S(2)}, u32[]{:S(2)}) %all-to-all-start.2) | async-done | bytes 294944 | tf_op jit(solution)/shard_map/all_to_all | solution.py:281
  193.0 3.7 %all-to-all-start.1 = ((bf16[32,8,2176]{2,1,0:T(8,128)(2,1)}), bf16[32,8,2176]{2,1,0:T(8,128)(2,1)S(1)}, u32[]{:S(2)}, u32[]{:S(2)}) async-start(bf16[32,8,2176]{2,1,0:T(8,128)(2,1)} %fusion), calls=%async_computation.1 | async-start | bytes 2228224 | tf_op jit(solution)/shard_map/all_to_all | solution.py:281
  197.4 8.5 %collective-permute-start.17 = (bf16[16,2176]{1,0:T(8,128)(2,1)S(1)}, bf16[16,2176]{1,0:T(8,128)(2,1)S(1)}, u32[]{:S(2)}, u32[]{:S(2)}) collective-permute-start(bf16[16,2176]{1,0:T(8,128)(2,1)S(1)} %pad_maximum_fusion.6), channel_id=1, source_target_pairs={{0,8},{1,9},{2,10},{3,11},{4,12},{5,13},{6,14},{7,15},{8,16},{9,17... | collective-permute-start | bytes 208904 | tf_op jit(solution)/shard_map/ppermute | solution.py:151
  205.9 5.3 %collective-permute-done.17 = bf16[16,2176]{1,0:T(8,128)(2,1)S(1)} collective-permute-done((bf16[16,2176]{1,0:T(8,128)(2,1)S(1)}, bf16[16,2176]{1,0:T(8,128)(2,1)S(1)}, u32[]{:S(2)}, u32[]{:S(2)}) %collective-permute-start.17) | collective-permute-done | bytes 69664 | tf_op jit(solution)/shard_map/ppermute | solution.py:151
  211.3 3.2 %all-to-all-done.1 = bf16[32,8,2176]{2,1,0:T(8,128)(2,1)S(1)} async-done(((bf16[32,8,2176]{2,1,0:T(8,128)(2,1)}), bf16[32,8,2176]{2,1,0:T(8,128)(2,1)S(1)}, u32[]{:S(2)}, u32[]{:S(2)}) %all-to-all-start.1) | async-done | bytes 1114144 | tf_op jit(solution)/shard_map/all_to_all | solution.py:281
  215.0 8.5 %collective-permute-start.18 = (bf16[16,4224]{1,0:T(8,128)(2,1)S(1)}, bf16[16,4224]{1,0:T(8,128)(2,1)S(1)}, u32[]{:S(2)}, u32[]{:S(2)}) collective-permute-start(bf16[16,4224]{1,0:T(8,128)(2,1)S(1)} %fusion.9), channel_id=1, source_target_pairs={{0,8},{1,9},{2,10},{3,11},{4,12},{5,13},{6,14},{7,15},{8,16},{9,17... | collective-permute-start | bytes 405512 | tf_op jit(solution)/shard_map/ppermute | solution.py:151
  223.5 14.7 %collective-permute-done.18 = bf16[16,4224]{1,0:T(8,128)(2,1)S(1)} collective-permute-done((bf16[16,4224]{1,0:T(8,128)(2,1)S(1)}, bf16[16,4224]{1,0:T(8,128)(2,1)S(1)}, u32[]{:S(2)}, u32[]{:S(2)}) %collective-permute-start.18) | collective-permute-done | bytes 135200 | tf_op jit(solution)/shard_map/ppermute | solution.py:151
  238.2 1.9 collective-permute-start.19
  240.1 1.2 collective-permute-done.19
  (173 shorter events, 14.6 us)
Async XLA Ops:
  0.6 53.6 %copy-start.25 = (s32[4]{0:T(128)S(1)}, s32[4]{0:T(128)}, u32[]{:S(2)}) copy-start(s32[4]{0:T(128)} %constant.192.clone) | copy-start | bytes 52
  56.9 12.9 %copy-start.26 = (s32[8]{0:T(128)S(1)}, s32[8]{0:T(128)}, u32[]{:S(2)}) copy-start(s32[8]{0:T(128)} %constant.193.clone) | copy-start | bytes 100
  56.9 28.4 %all-to-all-start = ((bf16[32,8,2176]{2,1,0:T(8,128)(2,1)}), bf16[32,8,2176]{2,1,0:T(8,128)(2,1)S(1)}, u32[]{:S(2)}, u32[]{:S(2)}) async-start(bf16[32,8,2176]{2,1,0:T(8,128)(2,1)} %bitcast.18), calls=%async_computation | async-start | bytes 2228224 | tf_op jit(solution)/shard_map/all_to_all | solution.py:195
  67.6 65.9 %collective-permute-start = (bf16[32,128]{1,0:T(8,128)(2,1)}, bf16[32,128]{1,0:T(8,128)(2,1)}, u32[]{:S(2)}, u32[]{:S(2)}) collective-permute-start(bf16[32,128]{1,0:T(8,128)(2,1)} %slice.267), channel_id=1, source_target_pairs={{0,32},{32,0},{64,96},{96,64},{128,160},{160,128},{192,224},{224,1... | collective-permute-start | bytes 24584 | tf_op jit(solution)/shard_map/ppermute | solution.py:159
  69.9 15.7 %copy-start.18 = (bf16[8]{0:T(256)(128)(2,1)}, bf16[8]{0:T(256)(128)(2,1)S(1)}, u32[]{:S(2)}) copy-start(bf16[8]{0:T(256)(128)(2,1)S(1)} %fusion.55) | copy-start | bytes 52
  69.9 17.1 %copy-start.16 = (pred[4,256]{1,0:T(4,128)(4,1)}, pred[4,256]{1,0:T(4,128)(4,1)S(1)}, u32[]{:S(2)}) copy-start(pred[4,256]{1,0:T(4,128)(4,1)S(1)} %iota_compare_fusion.11) | copy-start | bytes 3076
  85.4 1.6 copy-start.8
  85.4 1.6 copy-start.10
  85.4 1.6 copy-start.13
  85.9 0.7 copy-start.6
  86.0 0.7 copy-start.4
  87.1 14.3 %collective-permute-start.1 = (bf16[32,2048]{1,0:T(8,128)(2,1)S(1)}, bf16[32,2048]{1,0:T(8,128)(2,1)S(1)}, u32[]{:S(2)}, u32[]{:S(2)}) collective-permute-start(bf16[32,2048]{1,0:T(8,128)(2,1)S(1)} %get-tuple-element.44), channel_id=1, source_target_pairs={{0,4},{1,5},{2,6},{3,7},{4,8},{5,9},{6,10},{7,11},{8,12},{9,13},{1... | collective-permute-start | bytes 393224 | tf_op jit(solution)/shard_map/ppermute | solution.py:151
  89.0 17.4 %collective-permute-start.2 = (bf16[32,2048]{1,0:T(8,128)(2,1)S(1)}, bf16[32,2048]{1,0:T(8,128)(2,1)S(1)}, u32[]{:S(2)}, u32[]{:S(2)}) collective-permute-start(bf16[32,2048]{1,0:T(8,128)(2,1)S(1)} %get-tuple-element.45), channel_id=1, source_target_pairs={{0,3},{1,4},{2,5},{3,6},{4,7},{5,8},{6,9},{7,10},{8,11},{9,12},{10... | collective-permute-start | bytes 393224 | tf_op jit(solution)/shard_map/ppermute | solution.py:143
  92.5 15.9 %collective-permute-start.3 = (bf16[32,2048]{1,0:T(8,128)(2,1)S(1)}, bf16[32,2048]{1,0:T(8,128)(2,1)S(1)}, u32[]{:S(2)}, u32[]{:S(2)}) collective-permute-start(bf16[32,2048]{1,0:T(8,128)(2,1)S(1)} %get-tuple-element.46), channel_id=1, source_target_pairs={{0,29},{1,30},{2,31},{3,0},{4,1},{5,2},{6,3},{7,4},{8,5},{9,6},{10... | collective-permute-start | bytes 393224 | tf_op jit(solution)/shard_map/ppermute | solution.py:143
  97.3 15.6 %collective-permute-start.4 = (bf16[32,2048]{1,0:T(8,128)(2,1)S(1)}, bf16[32,2048]{1,0:T(8,128)(2,1)S(1)}, u32[]{:S(2)}, u32[]{:S(2)}) collective-permute-start(bf16[32,2048]{1,0:T(8,128)(2,1)S(1)} %get-tuple-element.47), channel_id=1, source_target_pairs={{0,2},{1,3},{2,4},{3,5},{4,6},{5,7},{6,8},{7,9},{8,10},{9,11},{10,... | collective-permute-start | bytes 393224 | tf_op jit(solution)/shard_map/ppermute | solution.py:143
  101.4 12.8 %collective-permute-start.5 = (bf16[32,2048]{1,0:T(8,128)(2,1)S(1)}, bf16[32,2048]{1,0:T(8,128)(2,1)S(1)}, u32[]{:S(2)}, u32[]{:S(2)}) collective-permute-start(bf16[32,2048]{1,0:T(8,128)(2,1)S(1)} %get-tuple-element.48), channel_id=1, source_target_pairs={{0,30},{1,31},{2,0},{3,1},{4,2},{5,3},{6,4},{7,5},{8,6},{9,7},{10,... | collective-permute-start | bytes 393224 | tf_op jit(solution)/shard_map/ppermute | solution.py:143
  106.4 7.8 %collective-permute-start.6 = (bf16[32,2048]{1,0:T(8,128)(2,1)S(1)}, bf16[32,2048]{1,0:T(8,128)(2,1)S(1)}, u32[]{:S(2)}, u32[]{:S(2)}) collective-permute-start(bf16[32,2048]{1,0:T(8,128)(2,1)S(1)} %get-tuple-element.49), channel_id=1, source_target_pairs={{0,1},{1,2},{2,3},{3,4},{4,5},{5,6},{6,7},{7,8},{8,9},{9,10},{10,1... | collective-permute-start | bytes 393224 | tf_op jit(solution)/shard_map/ppermute | solution.py:143
  108.4 7.6 %collective-permute-start.7 = (bf16[32,2048]{1,0:T(8,128)(2,1)S(1)}, bf16[32,2048]{1,0:T(8,128)(2,1)S(1)}, u32[]{:S(2)}, u32[]{:S(2)}) collective-permute-start(bf16[32,2048]{1,0:T(8,128)(2,1)S(1)} %get-tuple-element.43), channel_id=1, source_target_pairs={{0,31},{1,0},{2,1},{3,2},{4,3},{5,4},{6,5},{7,6},{8,7},{9,8},{10,9... | collective-permute-start | bytes 393224 | tf_op jit(solution)/shard_map/ppermute | solution.py:143
  113.0 13.1 %copy-start = (bf16[1,1,2048,256]{3,2,1,0:T(8,128)(2,1)S(1)}, bf16[1,1,2048,256]{3,2,1,0:T(8,128)(2,1)}, u32[]{:S(2)}) copy-start(bf16[1,1,2048,256]{3,2,1,0:T(8,128)(2,1)} %param.17) | copy-start | bytes 3145732
  113.0 13.1 %copy-start.1 = (bf16[1,1,2048,256]{3,2,1,0:T(8,128)(2,1)S(1)}, bf16[1,1,2048,256]{3,2,1,0:T(8,128)(2,1)}, u32[]{:S(2)}) copy-start(bf16[1,1,2048,256]{3,2,1,0:T(8,128)(2,1)} %param.18) | copy-start | bytes 3145732
  116.0 10.1 %collective-permute-start.8 = (bf16[256,2048]{1,0:T(8,128)(2,1)S(1)}, bf16[256,2048]{1,0:T(8,128)(2,1)}, u32[]{:S(2)}, u32[]{:S(2)}) collective-permute-start(bf16[256,2048]{1,0:T(8,128)(2,1)S(1)} %fusion.30.mine), channel_id=1, source_target_pairs={{0,32},{32,0},{64,96},{96,64},{128,160},{160,128},{192,224},{224,1... | collective-permute-start | bytes 3145736 | tf_op jit(solution)/shard_map/ppermute | solution.py:159
  124.7 1.4 copy-start.21
  126.1 1.2 copy-start.2
  131.6 8.7 %collective-permute-start.9 = (bf16[256,2048]{1,0:T(8,128)(2,1)}, bf16[256,2048]{1,0:T(8,128)(2,1)}, u32[]{:S(2)}, u32[]{:S(2)}) collective-permute-start(bf16[256,2048]{1,0:T(8,128)(2,1)} %get-tuple-element.30), channel_id=1, source_target_pairs={{0,32},{32,0},{64,96},{96,64},{128,160},{160,128},{192,224},{224,1... | collective-permute-start | bytes 3145736 | tf_op jit(solution)/shard_map/ppermute | solution.py:159
  138.4 1.2 copy-start.3
  140.2 5.2 %copy-start.15 = (bf16[16,2,2,8]{0,3,2,1:T(8,128)(2,1)S(1)}, bf16[16,2,2,8]{0,3,2,1:T(8,128)(2,1)}, u32[]{:S(2)}) copy-start(bf16[16,2,2,8]{0,3,2,1:T(8,128)(2,1)} %get-tuple-element.64) | copy-start | bytes 3076
  140.2 5.2 %copy-start.20 = (bf16[4,16]{1,0:T(4,128)(2,1)S(1)}, bf16[4,16]{1,0:T(4,128)(2,1)}, u32[]{:S(2)}) copy-start(bf16[4,16]{1,0:T(4,128)(2,1)} %mul.52) | copy-start | bytes 388
  141.9 31.6 %copy-start.5 = (bf16[256,256]{1,0:T(8,128)(2,1)S(1)}, bf16[256,256]{1,0:T(8,128)(2,1)}, u32[]{:S(2)}) copy-start(bf16[256,256]{1,0:T(8,128)(2,1)} %copy-done.4) | copy-start | bytes 393220
  141.9 18.6 %collective-permute-start.10 = (bf16[32,2048]{1,0:T(8,128)(2,1)S(1)}, bf16[32,2048]{1,0:T(8,128)(2,1)S(1)}, u32[]{:S(2)}, u32[]{:S(2)}) collective-permute-start(bf16[32,2048]{1,0:T(8,128)(2,1)S(1)} %get-tuple-element.31), channel_id=1, source_target_pairs={{0,28},{1,29},{2,30},{3,31},{4,0},{5,1},{6,2},{7,3},{8,4},{9,5},{1... | collective-permute-start | bytes 393224 | tf_op jit(solution)/shard_map/ppermute | solution.py:151
  145.5 21.0 %collective-permute-start.11 = (bf16[32,2048]{1,0:T(8,128)(2,1)S(1)}, bf16[32,2048]{1,0:T(8,128)(2,1)S(1)}, u32[]{:S(2)}, u32[]{:S(2)}) collective-permute-start(bf16[32,2048]{1,0:T(8,128)(2,1)S(1)} %get-tuple-element.32), channel_id=1, source_target_pairs={{0,29},{1,30},{2,31},{3,0},{4,1},{5,2},{6,3},{7,4},{8,5},{9,6},{10... | collective-permute-start | bytes 393224 | tf_op jit(solution)/shard_map/ppermute | solution.py:143
  148.7 19.8 %collective-permute-start.12 = (bf16[32,2048]{1,0:T(8,128)(2,1)S(1)}, bf16[32,2048]{1,0:T(8,128)(2,1)S(1)}, u32[]{:S(2)}, u32[]{:S(2)}) collective-permute-start(bf16[32,2048]{1,0:T(8,128)(2,1)S(1)} %get-tuple-element.33), channel_id=1, source_target_pairs={{0,3},{1,4},{2,5},{3,6},{4,7},{5,8},{6,9},{7,10},{8,11},{9,12},{10... | collective-permute-start | bytes 393224 | tf_op jit(solution)/shard_map/ppermute | solution.py:143
  152.6 16.5 %collective-permute-start.13 = (bf16[32,2048]{1,0:T(8,128)(2,1)S(1)}, bf16[32,2048]{1,0:T(8,128)(2,1)S(1)}, u32[]{:S(2)}, u32[]{:S(2)}) collective-permute-start(bf16[32,2048]{1,0:T(8,128)(2,1)S(1)} %get-tuple-element.34), channel_id=1, source_target_pairs={{0,30},{1,31},{2,0},{3,1},{4,2},{5,3},{6,4},{7,5},{8,6},{9,7},{10,... | collective-permute-start | bytes 393224 | tf_op jit(solution)/shard_map/ppermute | solution.py:143
  158.6 12.5 %collective-permute-start.14 = (bf16[32,2048]{1,0:T(8,128)(2,1)S(1)}, bf16[32,2048]{1,0:T(8,128)(2,1)S(1)}, u32[]{:S(2)}, u32[]{:S(2)}) collective-permute-start(bf16[32,2048]{1,0:T(8,128)(2,1)S(1)} %get-tuple-element.35), channel_id=1, source_target_pairs={{0,2},{1,3},{2,4},{3,5},{4,6},{5,7},{6,8},{7,9},{8,10},{9,11},{10,... | collective-permute-start | bytes 393224 | tf_op jit(solution)/shard_map/ppermute | solution.py:143
  160.5 11.6 %collective-permute-start.15 = (bf16[32,2048]{1,0:T(8,128)(2,1)S(1)}, bf16[32,2048]{1,0:T(8,128)(2,1)S(1)}, u32[]{:S(2)}, u32[]{:S(2)}) collective-permute-start(bf16[32,2048]{1,0:T(8,128)(2,1)S(1)} %get-tuple-element.36), channel_id=1, source_target_pairs={{0,31},{1,0},{2,1},{3,2},{4,3},{5,4},{6,5},{7,6},{8,7},{9,8},{10,9... | collective-permute-start | bytes 393224 | tf_op jit(solution)/shard_map/ppermute | solution.py:143
  166.6 6.9 %collective-permute-start.16 = (bf16[32,2048]{1,0:T(8,128)(2,1)S(1)}, bf16[32,2048]{1,0:T(8,128)(2,1)S(1)}, u32[]{:S(2)}, u32[]{:S(2)}) collective-permute-start(bf16[32,2048]{1,0:T(8,128)(2,1)S(1)} %get-tuple-element.37), channel_id=1, source_target_pairs={{0,1},{1,2},{2,3},{3,4},{4,5},{5,6},{6,7},{7,8},{8,9},{9,10},{10,1... | collective-permute-start | bytes 393224 | tf_op jit(solution)/shard_map/ppermute | solution.py:143
  169.1 4.8 %copy-start.7 = (pred[8,4,8,256]{3,2,1,0:T(8,128)(4,1)S(1)}, pred[8,4,8,256]{3,2,1,0:T(8,128)(4,1)}, u32[]{:S(2)}) copy-start(pred[8,4,8,256]{3,2,1,0:T(8,128)(4,1)} %copy-done.6) | copy-start | bytes 196612
  173.5 0.8 copy-start.17
  173.5 0.9 copy-start.11
  173.6 0.9 copy-start.14
  173.6 0.9 copy-start.19
  173.6 1.9 copy-start.23
  176.0 8.3 %copy-start.9 = (bf16[16,2,2,2,8]{4,3,2,1,0:T(2,128)(2,1)S(1)}, bf16[16,2,2,2,8]{4,3,2,1,0:T(2,128)(2,1)}, u32[]{:S(2)}) copy-start(bf16[16,2,2,2,8]{4,3,2,1,0:T(2,128)(2,1)} %broadcast_multiply_fusion) | copy-start | bytes 6148
  176.0 8.4 %copy-start.22 = (s32[256]{0:T(256)S(1)}, s32[256]{0:T(256)}, u32[]{:S(2)}) copy-start(s32[256]{0:T(256)} %eq.270) | copy-start | bytes 3076
  177.0 16.0 %all-to-all-start.2 = ((bf16[32,4,1152]{2,1,0:T(4,128)(2,1)}), bf16[32,4,1152]{2,1,0:T(4,128)(2,1)S(1)}, u32[]{:S(2)}, u32[]{:S(2)}) async-start(bf16[32,4,1152]{2,1,0:T(4,128)(2,1)} %reshape.494), calls=%async_computation.2 | async-start | bytes 589824 | tf_op jit(solution)/shard_map/all_to_all | solution.py:281
  193.0 21.4 %all-to-all-start.1 = ((bf16[32,8,2176]{2,1,0:T(8,128)(2,1)}), bf16[32,8,2176]{2,1,0:T(8,128)(2,1)S(1)}, u32[]{:S(2)}, u32[]{:S(2)}) async-start(bf16[32,8,2176]{2,1,0:T(8,128)(2,1)} %fusion), calls=%async_computation.1 | async-start | bytes 2228224 | tf_op jit(solution)/shard_map/all_to_all | solution.py:281
  197.4 13.9 %collective-permute-start.17 = (bf16[16,2176]{1,0:T(8,128)(2,1)S(1)}, bf16[16,2176]{1,0:T(8,128)(2,1)S(1)}, u32[]{:S(2)}, u32[]{:S(2)}) collective-permute-start(bf16[16,2176]{1,0:T(8,128)(2,1)S(1)} %pad_maximum_fusion.6), channel_id=1, source_target_pairs={{0,8},{1,9},{2,10},{3,11},{4,12},{5,13},{6,14},{7,15},{8,16},{9,17... | collective-permute-start | bytes 208904 | tf_op jit(solution)/shard_map/ppermute | solution.py:151
  215.0 23.1 %collective-permute-start.18 = (bf16[16,4224]{1,0:T(8,128)(2,1)S(1)}, bf16[16,4224]{1,0:T(8,128)(2,1)S(1)}, u32[]{:S(2)}, u32[]{:S(2)}) collective-permute-start(bf16[16,4224]{1,0:T(8,128)(2,1)S(1)} %fusion.9), channel_id=1, source_target_pairs={{0,8},{1,9},{2,10},{3,11},{4,12},{5,13},{6,14},{7,15},{8,16},{9,17... | collective-permute-start | bytes 405512 | tf_op jit(solution)/shard_map/ppermute | solution.py:151
  238.2 3.2 %collective-permute-start.19 = (bf16[8,4224]{1,0:T(8,128)(2,1)S(1)}, bf16[8,4224]{1,0:T(8,128)(2,1)S(1)}, u32[]{:S(2)}, u32[]{:S(2)}) collective-permute-start(bf16[8,4224]{1,0:T(8,128)(2,1)S(1)} %broadcast_select_fusion), channel_id=1, source_target_pairs={{0,32},{32,0},{64,96},{96,64},{128,160},{160,128},{192,224},{224,1... | collective-permute-start | bytes 202760 | tf_op jit(solution)/shard_map/ppermute | solution.py:159
  (2 other events, 1.2 us)
